TPU v7x, 128 devices: a whole 4x4x4 slice. The times are simulated.
128 devices in a mesh: view: 4 (over z_lo, core), brick: 32 (over z_hi, x, y).
Axes of the slice: x: 4, y: 4, z: 4 (z_hi: 2, z_lo: 2; z = z_hi * 2 + z_lo), core: 2. Of those that a mesh axis runs over, the one named last changes fastest.
Arguments:
- start_estimate: float32 [1024, 256, 128], P('brick'), may hold values from 0.5 to 2
- observed: bfloat16 [4, 1024, 256, 128], P('view', 'brick'), may hold values from 0.25 to 4
- psf_taps: float32 [4, 3, 3, 15], P('view'), may hold values from 0.01 to 0.15
- offsets: int32 [4], P('view'), may hold values from 0 to 31
- coverage: int32 [4, 32], P(None, 'brick'), may hold values from 0 to 1, as said below
Outputs:
- estimate: float32 [1024, 256, 128], P('brick')
Inputs may be any that keep to these rules, and one draw needn't show every extreme that they name: `coverage`: each brick is covered by at least one view.
All inputs are finite; a program needn't handle non-finite values.
Results may differ from a plain program's by a relative error of at most 0.0003.
Values may be sent and summed in bfloat16 or wider, within the bound.
No kernel may reach another device: no remote copies, remote signals or barrier semaphores. Data moves between devices by JAX's collectives and lax.ppermute only.
A program may use at most 128 MiB of HBM per device.

v0:
```python
import jax
import jax.numpy as jnp
from jax import lax
from jax.sharding import PartitionSpec as P

ITERS = 2


def from_behind(value, axis, by):
    devices = lax.axis_size(axis)
    return lax.ppermute(value, axis, [(i, (i + by) % devices) for i in range(devices)])


def extended_2(value, sides, width):
    for axis, dim in sides:
        devices, length = (lax.axis_size(axis), value.shape[dim])
        up = [(i, (i + 1) % devices) for i in range(devices - 1)]
        down = [(j, i) for i, j in up]
        last = lax.slice_in_dim(value, length - width, length, axis=dim)
        first = lax.slice_in_dim(value, 0, width, axis=dim)
        before = lax.ppermute(last, axis, up)
        after = lax.ppermute(first, axis, down)
        value = jnp.concatenate([before, value, after], axis=dim)
    return value


def tap_matrix(kernel, extent):
    tap_count = kernel.shape[0]
    shape_all = (tap_count, extent, extent)
    rows_at = lax.broadcasted_iota(jnp.int32, shape_all, 1)
    cols_at = lax.broadcasted_iota(jnp.int32, shape_all, 2)
    taps_at = lax.broadcasted_iota(jnp.int32, shape_all, 0)
    picked = rows_at - cols_at + tap_count // 2 == taps_at
    return jnp.sum(jnp.where(picked, kernel[:, None, None], 0.0), axis=0)


def band_matrix(kernel, row_count, ext_count, flipped):
    tap_count = kernel.shape[0]
    shape_all = (tap_count, row_count, ext_count)
    rows_at = lax.broadcasted_iota(jnp.int32, shape_all, 1)
    cols_at = lax.broadcasted_iota(jnp.int32, shape_all, 2)
    taps_at = lax.broadcasted_iota(jnp.int32, shape_all, 0)
    if flipped:
        picked = cols_at - rows_at == tap_count - 1 - taps_at
    else:
        picked = cols_at - rows_at == taps_at
    return jnp.sum(jnp.where(picked, kernel[:, None, None], 0.0), axis=0)


def project(extended, kernels, mats_y, mats_z, row_count, flipped):
    summed = jnp.zeros((row_count,) + extended.shape[1:], jnp.float32)
    for member in range(len(mats_y)):
        matrix_x = band_matrix(kernels[0, member], row_count, extended.shape[0], flipped)
        along_x = jnp.einsum("re,eyz->ryz", matrix_x, extended, precision=lax.Precision.HIGHEST)
        matrix_y = mats_y[member].T if flipped else mats_y[member]
        matrix_z = mats_z[member].T if flipped else mats_z[member]
        along_y = jnp.einsum("xyz,yw->xwz", along_x, matrix_y, precision=lax.Precision.HIGHEST)
        summed = summed + jnp.dot(along_y, matrix_z, precision=lax.Precision.HIGHEST)
    return summed


def shards(start_estimate, observed, psf_taps, offsets, coverage):
    kernels = psf_taps[0]
    half_width = kernels.shape[2] // 2
    brick_rows = start_estimate.shape[0]
    view_index = lax.axis_index("view")
    own_mask = lax.dynamic_slice_in_dim(coverage[:, 0], view_index, 1)[0].astype(jnp.float32)
    counts = jnp.sum(coverage[:, 0]).astype(jnp.float32)
    mats_y = [
        tap_matrix(kernels[1, member], start_estimate.shape[1])
        for member in range(kernels.shape[1])
    ]
    mats_z = [
        tap_matrix(kernels[2, member], start_estimate.shape[2])
        for member in range(kernels.shape[1])
    ]
    tile_here = observed[0]
    tile_next = from_behind(tile_here, "brick", -1)
    joined = jnp.concatenate([tile_here, tile_next], axis=0)
    merged_view = lax.dynamic_slice_in_dim(joined, offsets[0], brick_rows, 0)
    estimate = start_estimate
    for iteration in range(ITERS):
        extended = extended_2(estimate.astype(jnp.bfloat16), (("brick", 0),), half_width).astype(
            estimate.dtype
        )
        blurred = project(extended, kernels, mats_y, mats_z, brick_rows, False)
        quotient = merged_view.astype(jnp.float32) / blurred
        widened = extended_2(quotient.astype(jnp.bfloat16), (("brick", 0),), half_width).astype(
            quotient.dtype
        )
        adjoint_term = project(widened, kernels, mats_y, mats_z, brick_rows, True)
        weighted = own_mask * adjoint_term
        summed = lax.psum(weighted, "view")
        estimate = estimate * summed / counts
    return estimate


def solution(mesh):
    in_specs = (
        P("brick", None, None),
        P("view", "brick", None, None),
        P("view", None, None, None),
        P("view"),
        P(None, "brick"),
    )
    out_specs = P("brick", None, None)
    return jax.shard_map(shards, mesh=mesh, in_specs=in_specs, out_specs=out_specs, check_vma=False)
```

profile of v0, /device:TPU:1, one launch (start us, length us, event | category | flops | bytes accessed | tf_op | source)
XLA Modules:
  0.0 480.2 jit_solution(13921264739930480523)
XLA Ops:
  10.1 4.0 collective-permute-start.1
  15.4 9.8 %collective-permute-start = (bf16[32,256,128]{2,1,0:T(8,128)(2,1)}, bf16[32,256,128]{2,1,0:T(8,128)(2,1)}, u32[]{:S(2)}, u32[]{:S(2)}) collective-permute-start(bf16[32,256,128]{2,1,0:T(8,128)(2,1)} %bitcast.5), channel_id=1, source_target_pairs={{0,31},{1,0},{2,1},{3,2},{4,3},{5,4},{6,5},{7,6},{8,7},{9,8},{10,9... | collective-permute-start | bytes 6291464 | tf_op jit(solution)/shard_map/ppermute | solution.py:11
  33.8 3.0 fusion.68
  36.9 6.6 %fusion.46 = f32[256,32,128]{2,0,1:T(8,128)S(1)} fusion(f32[32,256,128]{2,0,1:T(8,128)S(1)} %fusion.70, f32[256,256]{1,0:T(8,128)S(1)} %get-tuple-element.29), kind=kOutput, calls=%fused_computation.50 | convolution fusion | flops 3221225472 | bytes 8650752 | tf_op jit(solution)/shard_map/xyz,yw->xwz/dot_general | solution.py:57
  43.5 3.0 fusion.72
  46.5 3.6 fusion.22
  50.1 6.4 %fusion.44 = f32[256,32,128]{2,0,1:T(8,128)S(1)} fusion(f32[32,256,128]{2,0,1:T(8,128)S(1)} %fusion.68, f32[256,256]{1,0:T(8,128)S(1)} %get-tuple-element.28), kind=kOutput, calls=%fused_computation.48 | convolution fusion | flops 3221225472 | bytes 8650752 | tf_op jit(solution)/shard_map/xyz,yw->xwz/dot_general | solution.py:57
  56.5 3.6 fusion.20
  60.1 6.6 %fusion.48 = f32[256,32,128]{2,0,1:T(8,128)S(1)} fusion(f32[32,256,128]{2,0,1:T(8,128)S(1)} %fusion.72, f32[256,256]{1,0:T(8,128)S(1)} %select_reduce_fusion.2), kind=kOutput, calls=%fused_computation.52 | convolution fusion | flops 3221225472 | bytes 8650752 | tf_op jit(solution)/shard_map/xyz,yw->xwz/dot_general | solution.py:57
  66.7 5.6 %collective-permute-done = bf16[32,256,128]{2,1,0:T(8,128)(2,1)} collective-permute-done((bf16[32,256,128]{2,1,0:T(8,128)(2,1)}, bf16[32,256,128]{2,1,0:T(8,128)(2,1)}, u32[]{:S(2)}, u32[]{:S(2)}) %collective-permute-start) | collective-permute-done | bytes 2097184 | tf_op jit(solution)/shard_map/ppermute | solution.py:11
  72.3 6.0 %fusion = bf16[32,256,128]{2,1,0:T(8,128)(2,1)S(1)} fusion(f32[32,256,128]{2,1,0:T(8,128)S(1)} %fusion.20, f32[32,256,128]{2,1,0:T(8,128)S(1)} %fusion.22, f32[256,32,128]{2,0,1:T(8,128)S(1)} %fusion.48, f32[128,128]{1,0:T(8,128)S(1)} %select_reduce_fusion.5, s32[]{:T(128)S(6)} %select_n.54, bf16[32,256,128]{2,1,0:T(8,128)(2,1)} %collective-permute-done, ...), kind=kOutput, calls=%fused_computation.2 | convolution fusion | flops 1616904192 | bytes 18939908 | tf_op jit(solution)/shard_map/dot_general | solution.py:58
  79.4 3.2 collective-permute-start.3
  85.1 5.6 %collective-permute-done.3 = bf16[7,256,128]{2,1,0:T(8,128)(2,1)S(1)} collective-permute-done((bf16[7,256,128]{2,1,0:T(8,128)(2,1)}, bf16[7,256,128]{2,1,0:T(8,128)(2,1)S(1)}, u32[]{:S(2)}, u32[]{:S(2)}) %collective-permute-start.3) | collective-permute-done | bytes 458784 | tf_op jit(solution)/shard_map/ppermute | solution.py:21
  90.7 3.9 collective-permute-done.4
  96.0 3.0 fusion.64
  99.0 6.2 %fusion.40 = f32[256,32,128]{2,0,1:T(8,128)S(1)} fusion(f32[32,256,128]{2,0,1:T(8,128)S(1)} %fusion.64, f32[256,256]{1,0:T(8,128)S(1)} %get-tuple-element.29), kind=kOutput, calls=%fused_computation.44 | convolution fusion | flops 3221225472 | bytes 8650752 | tf_op jit(solution)/shard_map/xyz,yw->xwz/dot_general | solution.py:57
  105.3 3.6 fusion.16
  108.9 3.0 fusion.62
  112.0 6.2 %fusion.38 = f32[256,32,128]{2,0,1:T(8,128)S(1)} fusion(f32[32,256,128]{2,0,1:T(8,128)S(1)} %fusion.62, f32[256,256]{1,0:T(8,128)S(1)} %get-tuple-element.28), kind=kOutput, calls=%fused_computation.42 | convolution fusion | flops 3221225472 | bytes 8650752 | tf_op jit(solution)/shard_map/xyz,yw->xwz/dot_general | solution.py:57
  118.2 4.0 fusion.14
  122.2 3.0 fusion.66
  125.3 5.9 %fusion.42 = f32[256,32,128]{2,0,1:T(8,128)S(1)} fusion(f32[32,256,128]{2,0,1:T(8,128)S(1)} %fusion.66, f32[256,256]{1,0:T(8,128)S(1)} %select_reduce_fusion.2), kind=kOutput, calls=%fused_computation.46 | convolution fusion | flops 3221225472 | bytes 8650752 | tf_op jit(solution)/shard_map/xyz,yw->xwz/dot_general | solution.py:57
  131.2 5.7 %add_multiply_fusion.1 = f32[32,256,128]{2,1,0:T(8,128)} fusion(f32[32,256,128]{2,1,0:T(8,128)S(1)} %fusion.14, f32[32,256,128]{2,1,0:T(8,128)S(1)} %fusion.16, f32[256,32,128]{2,0,1:T(8,128)S(1)} %fusion.42, f32[]{:T(128)} %bitcast, f32[128,128]{1,0:T(8,128)S(1)} %select_reduce_fusion.5), kind=kOutput, calls=%fused_computation.57 | convolution fusion | flops 1613758464 | bytes 16842756 | tf_op jit(solution)/shard_map/dot_general | solution.py:58
  138.9 103.5 %all-reduce.3.cloned.1.call-done = f32[32,256,128]{2,1,0:T(8,128)} async-done(((f32[32,256,128]{2,1,0:T(8,128)}), f32[32,256,128]{2,1,0:T(8,128)}) %all-reduce.3.cloned.1.call-update) | async-done | bytes 4194320 | tf_op jit(solution)/shard_map/psum | solution.py:93
  242.4 4.2 fusion.120
  246.7 3.1 collective-permute-start.5
  251.3 8.1 %collective-permute-done.5 = bf16[7,256,128]{2,1,0:T(8,128)(2,1)S(1)} collective-permute-done((bf16[7,256,128]{2,1,0:T(8,128)(2,1)S(1)}, bf16[7,256,128]{2,1,0:T(8,128)(2,1)S(1)}, u32[]{:S(2)}, u32[]{:S(2)}) %collective-permute-start.5) | collective-permute-done | bytes 458784 | tf_op jit(solution)/shard_map/ppermute | solution.py:21
  259.5 3.8 collective-permute-done.6
  269.8 3.0 fusion.60
  272.8 6.6 %fusion.34 = f32[256,32,128]{2,0,1:T(8,128)S(1)} fusion(f32[32,256,128]{2,0,1:T(8,128)S(1)} %fusion.58, f32[256,256]{1,0:T(8,128)S(1)} %get-tuple-element.29), kind=kOutput, calls=%fused_computation.38 | convolution fusion | flops 3221225472 | bytes 8650752 | tf_op jit(solution)/shard_map/xyz,yw->xwz/dot_general | solution.py:57
  279.5 3.6 fusion.10
  283.1 6.4 %fusion.32 = f32[256,32,128]{2,0,1:T(8,128)S(1)} fusion(f32[32,256,128]{2,0,1:T(8,128)S(1)} %fusion.56, f32[256,256]{1,0:T(8,128)S(1)} %get-tuple-element.28), kind=kOutput, calls=%fused_computation.36 | convolution fusion | flops 3221225472 | bytes 8650752 | tf_op jit(solution)/shard_map/xyz,yw->xwz/dot_general | solution.py:57
  289.5 3.6 fusion.8
  293.1 6.2 %fusion.36 = f32[256,32,128]{2,0,1:T(8,128)S(1)} fusion(f32[32,256,128]{2,0,1:T(8,128)S(1)} %fusion.60, f32[256,256]{1,0:T(8,128)S(1)} %select_reduce_fusion.2), kind=kOutput, calls=%fused_computation.40 | convolution fusion | flops 3221225472 | bytes 8650752 | tf_op jit(solution)/shard_map/xyz,yw->xwz/dot_general | solution.py:57
  299.3 6.1 %fusion.1 = bf16[32,256,128]{2,1,0:T(8,128)(2,1)S(1)} fusion(f32[32,256,128]{2,1,0:T(8,128)S(1)} %fusion.8, f32[32,256,128]{2,1,0:T(8,128)S(1)} %fusion.10, f32[256,32,128]{2,0,1:T(8,128)S(1)} %fusion.36, f32[128,128]{1,0:T(8,128)S(1)} %select_reduce_fusion.5, s32[]{:T(128)S(6)} %select_n.54, bf16[32,256,128]{2,1,0:T(8,128)(2,1)} %collective-permute-done, ...), kind=kOutput, calls=%fused_computation.3 | convolution fusion | flops 1616904192 | bytes 18939908 | tf_op jit(solution)/shard_map/dot_general | solution.py:58
  305.5 3.1 collective-permute-start.7
  310.3 6.6 %collective-permute-done.7 = bf16[7,256,128]{2,1,0:T(8,128)(2,1)S(1)} collective-permute-done((bf16[7,256,128]{2,1,0:T(8,128)(2,1)S(1)}, bf16[7,256,128]{2,1,0:T(8,128)(2,1)S(1)}, u32[]{:S(2)}, u32[]{:S(2)}) %collective-permute-start.7) | collective-permute-done | bytes 458784 | tf_op jit(solution)/shard_map/ppermute | solution.py:21
  316.9 3.9 collective-permute-done.8
  321.1 3.0 fusion.52
  327.1 3.0 fusion.54
  330.2 6.1 %fusion.28 = f32[256,32,128]{2,0,1:T(8,128)S(1)} fusion(f32[32,256,128]{2,0,1:T(8,128)S(1)} %fusion.52, f32[256,256]{1,0:T(8,128)S(1)} %get-tuple-element.29), kind=kOutput, calls=%fused_computation.32 | convolution fusion | flops 3221225472 | bytes 8650752 | tf_op jit(solution)/shard_map/xyz,yw->xwz/dot_general | solution.py:57
  336.3 3.4 fusion.4
  339.7 6.1 %fusion.26 = f32[256,32,128]{2,0,1:T(8,128)S(1)} fusion(f32[32,256,128]{2,0,1:T(8,128)S(1)} %fusion.50, f32[256,256]{1,0:T(8,128)S(1)} %get-tuple-element.28), kind=kOutput, calls=%fused_computation.30 | convolution fusion | flops 3221225472 | bytes 8650752 | tf_op jit(solution)/shard_map/xyz,yw->xwz/dot_general | solution.py:57
  345.8 3.4 fusion.2
  349.2 5.9 %fusion.30 = f32[256,32,128]{2,0,1:T(8,128)S(1)} fusion(f32[32,256,128]{2,0,1:T(8,128)S(1)} %fusion.54, f32[256,256]{1,0:T(8,128)S(1)} %select_reduce_fusion.2), kind=kOutput, calls=%fused_computation.34 | convolution fusion | flops 3221225472 | bytes 8650752 | tf_op jit(solution)/shard_map/xyz,yw->xwz/dot_general | solution.py:57
  355.1 5.8 %add_multiply_fusion = f32[32,256,128]{2,1,0:T(8,128)} fusion(f32[32,256,128]{2,1,0:T(8,128)S(1)} %fusion.2, f32[32,256,128]{2,1,0:T(8,128)S(1)} %fusion.4, f32[256,32,128]{2,0,1:T(8,128)S(1)} %fusion.30, f32[]{:T(128)} %bitcast, f32[128,128]{1,0:T(8,128)S(1)} %select_reduce_fusion.5), kind=kOutput, calls=%fused_computation.55 | convolution fusion | flops 1613758464 | bytes 16842756 | tf_op jit(solution)/shard_map/dot_general | solution.py:58
  360.9 103.8 %all-reduce.5.cloned.1.call-done = f32[32,256,128]{2,1,0:T(8,128)} async-done(((f32[32,256,128]{2,1,0:T(8,128)}), f32[32,256,128]{2,1,0:T(8,128)}) %all-reduce.5.cloned.1.call-update) | async-done | bytes 4194320 | tf_op jit(solution)/shard_map/psum | solution.py:93
  464.7 8.2 %multiply_divide_fusion = f32[32,256,128]{2,1,0:T(8,128)} fusion(f32[32,256,128]{2,1,0:T(8,128)} %all-reduce.5.cloned.1.call-done, f32[]{:T(128)S(6)} %convert_element_type.34, f32[32,256,128]{2,1,0:T(8,128)} %param.5, f32[32,256,128]{2,1,0:T(8,128)} %all-reduce.3.cloned.1.call-done), kind=kLoop, calls=%fused_computation.54 | loop fusion | flops 4194304 | bytes 16777220 | tf_op jit(solution)/shard_map/div | solution.py:94
  (55 shorter events, 32.1 us)
Async XLA Ops:
  6.5 19.3 %copy-start.9 = (f32[1,3,3,15]{3,0,2,1:T(1,128)S(1)}, f32[1,3,3,15]{3,0,2,1:T(1,128)}, u32[]{:S(2)}) copy-start(f32[1,3,3,15]{3,0,2,1:T(1,128)} %param.7) | copy-start | bytes 1624
  6.5 235.9 %all-reduce.3.cloned.1.call-start = ((), (), s32[]{:S(2)}) async-start(), calls=%async_computation | async-start | bytes 8388608 | tf_op jit(solution)/shard_map/psum | solution.py:93
  10.1 19.3 %collective-permute-start.1 = (bf16[7,256,128]{2,1,0:T(8,128)(2,1)}, bf16[7,256,128]{2,1,0:T(8,128)(2,1)S(1)}, u32[]{:S(2)}, u32[]{:S(2)}) collective-permute-start(bf16[7,256,128]{2,1,0:T(8,128)(2,1)} %get-tuple-element.17), channel_id=1, source_target_pairs={{0,1},{1,2},{2,3},{3,4},{4,5},{5,6},{6,7},{7,8},{8,9},{9,10},{10,1... | collective-permute-start | bytes 1376264 | tf_op jit(solution)/shard_map/ppermute | solution.py:21
  14.1 15.3 %collective-permute-start.2 = (bf16[7,256,128]{2,1,0:T(8,128)(2,1)}, bf16[7,256,128]{2,1,0:T(8,128)(2,1)}, u32[]{:S(2)}, u32[]{:S(2)}) collective-permute-start(bf16[7,256,128]{2,1,0:T(8,128)(2,1)} %get-tuple-element.18), channel_id=1, source_target_pairs={{1,0},{2,1},{3,2},{4,3},{5,4},{6,5},{7,6},{8,7},{9,8},{10,9},{11,1... | collective-permute-start | bytes 1376264 | tf_op jit(solution)/shard_map/ppermute | solution.py:22
  15.4 56.9 %collective-permute-start = (bf16[32,256,128]{2,1,0:T(8,128)(2,1)}, bf16[32,256,128]{2,1,0:T(8,128)(2,1)}, u32[]{:S(2)}, u32[]{:S(2)}) collective-permute-start(bf16[32,256,128]{2,1,0:T(8,128)(2,1)} %bitcast.5), channel_id=1, source_target_pairs={{0,31},{1,0},{2,1},{3,2},{4,3},{5,4},{6,5},{7,6},{8,7},{9,8},{10,9... | collective-permute-start | bytes 6291464 | tf_op jit(solution)/shard_map/ppermute | solution.py:11
  28.2 5.6 %copy-start.7 = (f32[32,46]{1,0:T(8,128)}, f32[32,46]{1,0:T(8,128)S(1)}, u32[]{:S(2)}) copy-start(f32[32,46]{1,0:T(8,128)S(1)} %get-tuple-element.9) | copy-start | bytes 17668
  28.2 5.7 %copy-start.5 = (f32[32,46]{1,0:T(8,128)}, f32[32,46]{1,0:T(8,128)S(1)}, u32[]{:S(2)}) copy-start(f32[32,46]{1,0:T(8,128)S(1)} %get-tuple-element.7) | copy-start | bytes 17668
  28.2 15.3 %copy-start.3 = (f32[32,46]{1,0:T(8,128)}, f32[32,46]{1,0:T(8,128)S(1)}, u32[]{:S(2)}) copy-start(f32[32,46]{1,0:T(8,128)S(1)} %get-tuple-element.10) | copy-start | bytes 17668
  79.4 11.3 %collective-permute-start.3 = (bf16[7,256,128]{2,1,0:T(8,128)(2,1)}, bf16[7,256,128]{2,1,0:T(8,128)(2,1)S(1)}, u32[]{:S(2)}, u32[]{:S(2)}) collective-permute-start(bf16[7,256,128]{2,1,0:T(8,128)(2,1)} %get-tuple-element.15), channel_id=1, source_target_pairs={{0,1},{1,2},{2,3},{3,4},{4,5},{5,6},{6,7},{7,8},{8,9},{9,10},{10,1... | collective-permute-start | bytes 1376264 | tf_op jit(solution)/shard_map/ppermute | solution.py:21
  82.6 12.0 %collective-permute-start.4 = (bf16[7,256,128]{2,1,0:T(8,128)(2,1)}, bf16[7,256,128]{2,1,0:T(8,128)(2,1)}, u32[]{:S(2)}, u32[]{:S(2)}) collective-permute-start(bf16[7,256,128]{2,1,0:T(8,128)(2,1)} %get-tuple-element.16), channel_id=1, source_target_pairs={{1,0},{2,1},{3,2},{4,3},{5,4},{6,5},{7,6},{8,7},{9,8},{10,9},{11,1... | collective-permute-start | bytes 1376264 | tf_op jit(solution)/shard_map/ppermute | solution.py:22
  83.9 12.1 %copy-start.1 = (f32[32,46]{1,0:T(8,128)S(1)}, f32[32,46]{1,0:T(8,128)}, u32[]{:S(2)}) copy-start(f32[32,46]{1,0:T(8,128)} %get-tuple-element.8) | copy-start | bytes 17668
  105.3 3.6 copy-start
  136.9 0.7 copy-start.10
  136.9 327.8 %all-reduce.5.cloned.1.call-start = ((), (), s32[]{:S(2)}) async-start(), calls=%async_computation.1 | async-start | bytes 8388608 | tf_op jit(solution)/shard_map/psum | solution.py:93
  246.6 17.0 %copy-start.8 = (f32[32,46]{1,0:T(8,128)S(1)}, f32[32,46]{1,0:T(8,128)}, u32[]{:S(2)}) copy-start(f32[32,46]{1,0:T(8,128)} %copy-done.7) | copy-start | bytes 17668
  246.7 12.8 %collective-permute-start.5 = (bf16[7,256,128]{2,1,0:T(8,128)(2,1)S(1)}, bf16[7,256,128]{2,1,0:T(8,128)(2,1)S(1)}, u32[]{:S(2)}, u32[]{:S(2)}) collective-permute-start(bf16[7,256,128]{2,1,0:T(8,128)(2,1)S(1)} %get-tuple-element.13), channel_id=1, source_target_pairs={{0,1},{1,2},{2,3},{3,4},{4,5},{5,6},{6,7},{7,8},{8,9},{9,10},{10,1... | collective-permute-start | bytes 1376264 | tf_op jit(solution)/shard_map/ppermute | solution.py:21
  249.8 13.4 %collective-permute-start.6 = (bf16[7,256,128]{2,1,0:T(8,128)(2,1)S(1)}, bf16[7,256,128]{2,1,0:T(8,128)(2,1)S(1)}, u32[]{:S(2)}, u32[]{:S(2)}) collective-permute-start(bf16[7,256,128]{2,1,0:T(8,128)(2,1)S(1)} %get-tuple-element.14), channel_id=1, source_target_pairs={{1,0},{2,1},{3,2},{4,3},{5,4},{6,5},{7,6},{8,7},{9,8},{10,9},{11,1... | collective-permute-start | bytes 1376264 | tf_op jit(solution)/shard_map/ppermute | solution.py:22
  263.6 3.1 copy-start.6
  266.7 3.1 copy-start.4
  305.4 15.7 %copy-start.2 = (f32[32,46]{1,0:T(8,128)S(1)}, f32[32,46]{1,0:T(8,128)}, u32[]{:S(2)}) copy-start(f32[32,46]{1,0:T(8,128)} %get-tuple-element.8) | copy-start | bytes 17668
  305.5 11.4 %collective-permute-start.7 = (bf16[7,256,128]{2,1,0:T(8,128)(2,1)S(1)}, bf16[7,256,128]{2,1,0:T(8,128)(2,1)S(1)}, u32[]{:S(2)}, u32[]{:S(2)}) collective-permute-start(bf16[7,256,128]{2,1,0:T(8,128)(2,1)S(1)} %get-tuple-element.11), channel_id=1, source_target_pairs={{0,1},{1,2},{2,3},{3,4},{4,5},{5,6},{6,7},{7,8},{8,9},{9,10},{10,1... | collective-permute-start | bytes 1376264 | tf_op jit(solution)/shard_map/ppermute | solution.py:21
  308.6 12.1 %collective-permute-start.8 = (bf16[7,256,128]{2,1,0:T(8,128)(2,1)S(1)}, bf16[7,256,128]{2,1,0:T(8,128)(2,1)S(1)}, u32[]{:S(2)}, u32[]{:S(2)}) collective-permute-start(bf16[7,256,128]{2,1,0:T(8,128)(2,1)S(1)} %get-tuple-element.12), channel_id=1, source_target_pairs={{1,0},{2,1},{3,2},{4,3},{5,4},{6,5},{7,6},{8,7},{9,8},{10,9},{11,1... | collective-permute-start | bytes 1376264 | tf_op jit(solution)/shard_map/ppermute | solution.py:22
Sparse Core Ops, SparseCore 0:
  137.0 105.3 all-reduce.2
  361.1 103.6 all-reduce.4
where the time goes:
time: 490 us; the launch traced here: 480 us
  waiting for transfers between devices  245 us (50%)
  matrix products  164 us (33%)
  starting transfers between devices  29.1 us (6%)
  other arithmetic  23.2 us (5%)
  between operations  15.8 us (3%)
    psum x2, waiting for transfers between devices, shards(): summed = lax.psum(weighted, 'view')  207 us
    dot_general x12, matrix products, project(): jnp.einsum('xyz,yw->xwz', along_x, matrix_y, precision=lax.Precision.HIGH...  75.2 us
    dot_general x12, matrix products, project(): jnp.dot(along_y, matrix_z, precision=lax.Precision.HIGHEST)  52.4 us
    dot_general x12, matrix products, project(): jnp.einsum('re,eyz->ryz', matrix_x, extended, precision=lax.Precision.HIG...  36.5 us
    ppermute x4, waiting for transfers between devices, extended_2(): before = lax.ppermute(last, axis, up)  20.3 us
    ppermute x4, starting transfers between devices, extended_2(): before = lax.ppermute(last, axis, up)  13.5 us
    ppermute x4, waiting for transfers between devices, extended_2(): after = lax.ppermute(first, axis, down)  11.5 us
  transfers between devices with their start and end apart: 11, of which 9 were waited for; matrix products, arithmetic and copies ran while one was open for 9% of the time, Pallas kernels for 0%

commit v1 on v0

v1 whole, which is shorter than its diff:
```python
import jax
import jax.numpy as jnp
from jax import lax
from jax.experimental import pallas as pl
from jax.experimental.pallas import tpu as pltpu
from jax.sharding import PartitionSpec as P

BX, NY, NZ = 32, 256, 128
VIEWS, RANK, TAPS = 4, 3, 15
QY = NY // VIEWS
HX = TAPS // 2
HY = 8
EX, EY = BX + 2 * HX, QY + 2 * HY
PAIRS = VIEWS * RANK
YB = 16
YW = 32
FX = 2
FW = FX + TAPS - 1
AX = 4
AW = AX + TAPS - 1
KINDS = (0, 1, 2, 6, 7)
VMEM_LIMIT = 56 * 1024 * 1024


def split(value):
    high = value.astype(jnp.bfloat16)
    return high, (value - high.astype(jnp.float32)).astype(jnp.bfloat16)


def bands(kernels, rows, cols, shift):
    taps_at = lax.broadcasted_iota(jnp.int32, (rows, cols, TAPS), 2)
    rows_at = lax.broadcasted_iota(jnp.int32, (rows, cols, TAPS), 0)
    cols_at = lax.broadcasted_iota(jnp.int32, (rows, cols, TAPS), 1)
    picked = cols_at - rows_at - shift == taps_at
    return jnp.sum(jnp.where(picked, kernels[..., None, None, :], 0.0), axis=-1)


def plane_matrices(taps):
    along_x = taps[:, 0].reshape(PAIRS, TAPS)
    along_y = taps[:, 1].reshape(PAIRS, TAPS)
    y_band = bands(along_y, YB, YW, 1)
    x_forward = bands(along_x, FX, FW, 0)
    forward = x_forward[:, :, None, :, None] * y_band[:, None, :, None, :]
    forward = forward.astype(jnp.bfloat16).reshape(PAIRS * FX * YB, FW * YW)
    x_adjoint = jnp.transpose(bands(along_x, AX, AW, 0), (2, 0, 1))
    y_adjoint = jnp.transpose(y_band, (2, 0, 1))
    adjoint = x_adjoint[:, None, :, :, None] * y_adjoint[None, :, :, None, :]
    adjoint = adjoint.astype(jnp.bfloat16).reshape(AW * YW, PAIRS * AX * YB)
    return forward, adjoint


def weighted_planes(adjoint, weights):
    tops = jnp.arange(BX // AX)[jnp.array(KINDS)][:, None] * AX + jnp.arange(AW)[None, :]
    side = jnp.where(tops < HX, 0, jnp.where(tops < HX + BX, 1, 2))
    scale = jnp.where(side[..., None] == 1, weights[1], jnp.where(side[..., None] == 0, weights[0], weights[2]))
    scale = scale.astype(jnp.bfloat16)[:, :, None, :, None]
    scaled = scale * adjoint.reshape(1, AW, YW, VIEWS, RANK * AX * YB)
    return scaled.reshape(len(KINDS), AW * YW, PAIRS * AX * YB)


def line_matrices(taps):
    along_z = taps[:, 2]
    transposed = bands(along_z, NZ, NZ, -(TAPS // 2))
    high, low = split(jnp.swapaxes(transposed, 2, 3))
    forward = jnp.concatenate([high, low], axis=3).reshape(VIEWS, RANK * NZ, 2 * NZ)
    high, low = split(transposed)
    stacked = jnp.concatenate([high, low], axis=2)
    adjoint = jnp.transpose(stacked, (0, 2, 1, 3)).reshape(VIEWS, 2 * NZ, RANK * NZ)
    return forward, adjoint


def forward_plane(ext_ref, plane_ref, mid_ref):
    @pl.loop(0, BX // (2 * FX))
    def _(step):
        x0 = step * (2 * FX)
        for y0 in range(0, QY, YB):
            parts = [
                ext_ref[pl.ds(x0 + part * FX, FW), y0 : y0 + YW, :].reshape(FW * YW, NZ)
                for part in range(2)
            ]
            made = jnp.dot(
                plane_ref[...],
                jnp.concatenate(parts, axis=1),
                preferred_element_type=jnp.float32,
            ).astype(jnp.bfloat16)
            for view in range(VIEWS):
                for term in range(RANK):
                    for part in range(2):
                        for dx in range(FX):
                            row = ((view * RANK + term) * FX + dx) * YB
                            mid_ref[
                                view, x0 + part * FX + dx, y0 : y0 + YB, term * NZ : (term + 1) * NZ
                            ] = made[row : row + YB, part * NZ : (part + 1) * NZ]


def forward_line(mid_ref, line_ref, view, x0, rows):
    a = mid_ref[view, pl.ds(x0, rows)].reshape(rows * QY, RANK * NZ)
    made = jnp.dot(a, line_ref[view], preferred_element_type=jnp.float32)
    return made[:, :NZ] + made[:, NZ:]


def merged_row(offset, here_ref, next_ref, view, x):
    at = offset + x
    here = here_ref[view, jnp.minimum(at, BX - 1)].astype(jnp.float32)
    after = next_ref[view, jnp.maximum(at - BX, 0)].astype(jnp.float32)
    return jnp.where(at < BX, here, after)


def adjoint_line(quotient, line_ref, back_ref, view, x0, rows):
    doubled = jnp.concatenate([quotient, quotient], axis=1)
    made = jnp.dot(doubled, line_ref[view], preferred_element_type=jnp.float32).astype(jnp.bfloat16)
    for term in range(RANK):
        back_ref[view * RANK + term, pl.ds(x0, rows)] = made[:, term * NZ : (term + 1) * NZ].reshape(
            rows, QY, NZ
        )


def adjoint_plane(back_ref, plane_ref, out_ref):
    out_ref[...] = jnp.zeros_like(out_ref)

    @pl.loop(0, BX // AX)
    def _(step):
        x0 = step * AX
        kind = jnp.minimum(step, 2) + jnp.maximum(step - 5, 0)
        for y0 in range(0, QY // 2, YB):
            starts = (y0, y0 + QY // 2)
            parts = [
                back_ref[:, pl.ds(x0, AX), at : at + YB, :].reshape(PAIRS * AX * YB, NZ)
                for at in starts
            ]
            made = jnp.dot(
                plane_ref[kind],
                jnp.concatenate(parts, axis=1),
                preferred_element_type=jnp.float32,
            )
            for part, at in enumerate(starts):
                out_ref[pl.ds(x0, AW), at : at + YW, :] += made[
                    :, part * NZ : (part + 1) * NZ
                ].reshape(AW, YW, NZ)


ROWS = 4


def blur_kernel(ext_ref, plane_ref, line_ref, out_ref, mid_ref):
    forward_plane(ext_ref, plane_ref, mid_ref)
    for view in range(VIEWS):

        @pl.loop(0, BX // ROWS)
        def _(step):
            x0 = step * ROWS
            blurred = forward_line(mid_ref, line_ref, view, x0, ROWS)
            out_ref[view, pl.ds(x0, ROWS)] = blurred.reshape(ROWS, QY, NZ)


def quotient_rows(offset, here_ref, next_ref, blurred, view, x0):
    merged = [merged_row(offset, here_ref, next_ref, view, x0 + row) for row in range(ROWS)]
    return (jnp.concatenate(merged, axis=0) / blurred).astype(jnp.bfloat16)


def back_kernel(
    offsets_ref, blurred_ref, here_ref, next_ref, line_ref, plane_ref, out_ref, back_ref
):
    for view in range(VIEWS):
        offset = offsets_ref[view]

        @pl.loop(0, BX // ROWS)
        def _(step):
            x0 = step * ROWS
            blurred = blurred_ref[view, pl.ds(x0, ROWS)].reshape(ROWS * QY, NZ)
            quotient = quotient_rows(offset, here_ref, next_ref, blurred, view, x0)
            adjoint_line(quotient, line_ref, back_ref, view, x0, ROWS)

    adjoint_plane(back_ref, plane_ref, out_ref)


def both_kernel(
    offsets_ref,
    ext_ref,
    here_ref,
    next_ref,
    fplane_ref,
    fline_ref,
    aline_ref,
    aplane_ref,
    out_ref,
    mid_ref,
    back_ref,
):
    forward_plane(ext_ref, fplane_ref, mid_ref)
    for view in range(VIEWS):
        offset = offsets_ref[view]

        @pl.loop(0, BX // ROWS)
        def _(step):
            x0 = step * ROWS
            blurred = forward_line(mid_ref, fline_ref, view, x0, ROWS)
            quotient = quotient_rows(offset, here_ref, next_ref, blurred, view, x0)
            adjoint_line(quotient, aline_ref, back_ref, view, x0, ROWS)

    adjoint_plane(back_ref, aplane_ref, out_ref)


VMEM = pl.BlockSpec(memory_space=pltpu.VMEM)
SMEM = pl.BlockSpec(memory_space=pltpu.SMEM)
MID = pltpu.VMEM((VIEWS, BX, QY, RANK * NZ), jnp.bfloat16)
BACK = pltpu.VMEM((PAIRS, BX, QY, NZ), jnp.bfloat16)
FLOPS = 2 * VIEWS * BX * QY * NZ * RANK * 3 * TAPS * 16


def call(kernel, out_shape, in_specs, scratch, flops, args):
    bytes_all = sum(a.size * a.dtype.itemsize for a in args)
    return pl.pallas_call(
        kernel,
        out_shape=jax.ShapeDtypeStruct(out_shape, jnp.float32),
        in_specs=in_specs,
        out_specs=VMEM,
        scratch_shapes=scratch,
        compiler_params=pltpu.CompilerParams(vmem_limit_bytes=VMEM_LIMIT),
        cost_estimate=pl.CostEstimate(flops=flops, bytes_accessed=bytes_all, transcendentals=0),
    )(*args)


def to_xor(value, by):
    return lax.ppermute(value, "view", [(i, i ^ by) for i in range(VIEWS)])


def to_next(value, axis):
    return lax.ppermute(value, axis, [(i, i + 1) for i in range(lax.axis_size(axis) - 1)])


def to_previous(value, axis):
    return lax.ppermute(value, axis, [(i + 1, i) for i in range(lax.axis_size(axis) - 1)])


def widen_x(rows):
    before = to_next(rows[BX - HX :], "brick")
    after = to_previous(rows[:HX], "brick")
    return jnp.concatenate([before, rows, after], axis=0)


def widen_y(rows):
    before = to_next(rows[:, QY - HY :], "view")
    after = to_previous(rows[:, :HY], "view")
    return jnp.concatenate([before, rows, after], axis=1)


def fold_x(wide):
    from_next = to_previous(wide[:HX], "brick")
    from_previous = to_next(wide[EX - HX :], "brick")
    own = wide[HX : HX + BX]
    return jnp.concatenate(
        [own[:HX] + from_previous, own[HX : BX - HX], own[BX - HX :] + from_next], axis=0
    )


def fold_y(wide):
    from_next = to_previous(wide[:, :HY], "view")
    from_previous = to_next(wide[:, EY - HY :], "view")
    own = wide[:, HY : HY + QY]
    return jnp.concatenate(
        [own[:, :HY] + from_previous, own[:, HY : QY - HY], own[:, QY - HY :] + from_next], axis=1
    )


def shards(start_estimate, observed, psf_taps, offsets, coverage):
    me = lax.axis_index("view")
    small = jnp.concatenate([psf_taps.reshape(-1), offsets.astype(jnp.float32)])[None]
    smalls = jnp.concatenate([small] + [to_xor(small, by) for by in range(1, VIEWS)], axis=0)

    tile = observed[0]
    here, after = [], []
    bricks = lax.axis_size("brick")
    for by in range(VIEWS):
        piece = lax.dynamic_slice_in_dim(tile, QY * (me ^ by), QY, 1)
        piece = to_xor(piece, by) if by else piece
        here.append(piece)
        after.append(lax.ppermute(piece, "brick", [((i + 1) % bricks, i) for i in range(bricks)]))

    padded = jnp.pad(start_estimate, ((0, 0), (HY, HY), (0, 0)))
    wide = lax.dynamic_slice_in_dim(padded, QY * me, EY, 1)
    estimate = wide[:, HY : HY + QY]
    ext = widen_x(wide.astype(jnp.bfloat16))

    taps = smalls[:, : 3 * RANK * TAPS].reshape(VIEWS, 3, RANK, TAPS)
    shifts = smalls[:, 3 * RANK * TAPS].astype(jnp.int32)
    covered = coverage[:, 0].astype(jnp.float32)
    count = jnp.sum(covered)
    covers = jnp.stack([to_next(covered, "brick"), covered, to_previous(covered, "brick")])
    weights = jnp.concatenate(
        [lax.dynamic_slice_in_dim(covers, me ^ by, 1, 1) for by in range(VIEWS)], axis=1
    )
    fplane, aplane = plane_matrices(taps)
    aplane = weighted_planes(aplane, weights)
    fline, aline = line_matrices(taps)

    blurred = call(
        blur_kernel, (VIEWS, BX, QY, NZ), [VMEM] * 3, [MID], FLOPS, (ext, fplane, fline)
    )
    here, after = jnp.stack(here), jnp.stack(after)
    terms = call(
        back_kernel,
        (EX, EY, NZ),
        [SMEM] + [VMEM] * 5,
        [BACK],
        FLOPS,
        (shifts, blurred, here, after, aline, aplane),
    )
    estimate = estimate * fold_y(fold_x(terms)) / count

    ext = widen_x(widen_y(estimate.astype(jnp.bfloat16)))
    terms = call(
        both_kernel,
        (EX, EY, NZ),
        [SMEM] + [VMEM] * 7,
        [MID, BACK],
        2 * FLOPS,
        (shifts, ext, here, after, fplane, fline, aline, aplane),
    )
    estimate = estimate * fold_y(fold_x(terms)) / count

    across = to_xor(estimate, 2)
    quarters = [estimate, to_xor(estimate, 1), across, to_xor(across, 1)]
    result = jnp.zeros(start_estimate.shape, jnp.float32)
    for by in range(VIEWS):
        result = lax.dynamic_update_slice_in_dim(result, quarters[by], QY * (me ^ by), 1)
    return result


def solution(mesh):
    in_specs = (
        P("brick", None, None),
        P("view", "brick", None, None),
        P("view", None, None, None),
        P("view"),
        P(None, "brick"),
    )
    out_specs = P("brick", None, None)
    return jax.shard_map(shards, mesh=mesh, in_specs=in_specs, out_specs=out_specs, check_vma=False)
```

time: 490 us -> 300 us (0.61)
  the two profiles are of different devices: /device:TPU:1 before, /device:TPU:31 now
where the time goes in v1:
time: 300 us; the launch traced here: 299 us
  waiting for transfers between devices  124 us (41%)
  Pallas kernels  64.6 us (22%)
  starting transfers between devices  53.8 us (18%)
  local copies, waits for them, and re-layouts  30.2 us (10%)
  other arithmetic  25.5 us (8%)
    pallas_call x3, Pallas kernels, call(): pl.pallas_call(kernel, out_shape=jax.ShapeDtypeStruct(out_shape, jnp.floa...  64.6 us
    ppermute x8, waiting for transfers between devices, to_previous(): lax.ppermute(value, axis, [(i + 1, i) for i in range(lax.axis_size(axis)...  47.8 us
    ppermute x4, waiting for transfers between devices, shards(): lax.ppermute(piece, 'brick', [((i + 1) % bricks, i) for i in range(bricks)])  31.8 us
    ppermute x8, starting transfers between devices, to_next(): lax.ppermute(value, axis, [(i, i + 1) for i in range(lax.axis_size(axis)...  31.3 us
    ppermute x9, waiting for transfers between devices, to_xor(): return lax.ppermute(value, 'view', [(i, i ^ by) for i in range(VIEWS)])  25.8 us
    ppermute x8, waiting for transfers between devices, to_next(): lax.ppermute(value, axis, [(i, i + 1) for i in range(lax.axis_size(axis)...  18.6 us
    ppermute x8, starting transfers between devices, to_previous(): lax.ppermute(value, axis, [(i + 1, i) for i in range(lax.axis_size(axis)...  16.2 us
    mul x2, local copies, waits for them, and re-layouts, weighted_planes(): scaled = scale * adjoint.reshape(1, AW, YW, VIEWS, RANK * AX * YB)  15 us
  transfers between devices with their start and end apart: 29, of which 16 were waited for; matrix products, arithmetic and copies ran while one was open for 15% of the time, Pallas kernels for 5%

profile of v1, /device:TPU:31, one launch (start us, length us, event | category | flops | bytes accessed | tf_op | source)
XLA Modules:
  0.0 299.4 jit_solution(3785640586225191551)
XLA Ops:
  0.7 5.1 %collective-permute-start.12 = (bf16[4]{0:T(256)(128)(2,1)S(1)}, bf16[4]{0:T(256)(128)(2,1)S(1)}, u32[]{:S(2)}, u32[]{:S(2)}) collective-permute-start(bf16[4]{0:T(256)(128)(2,1)S(1)} %get-tuple-element.44), channel_id=1, source_target_pairs={{0,1},{1,2},{2,3},{3,4},{4,5},{5,6},{6,7},{7,8},{8,9},{9,10},{10,1... | collective-permute-start | bytes 32 | tf_op jit(solution)/shard_map/ppermute | solution.py:229
  5.7 1.9 collective-permute-start.13
  12.9 1.6 fusion
  15.2 1.4 constant_dynamic-slice_fusion.4
  17.8 4.1 %mul.96 = bf16[5,18,32,4,192]{4,3,2,1,0:T(4,128)(2,1)} broadcast(bf16[5,18,4]{2,1,0:T(8,128)(2,1)S(1)} %select_convert_fusion), dimensions={0,1,3} | broadcast | bytes 4424400 | tf_op jit(solution)/shard_map/mul | solution.py:57
  21.9 10.8 %mul.97 = bf16[5,576,768]{2,1,0:T(8,128)(2,1)} reshape(bf16[5,18,32,4,192]{4,3,2,1,0:T(4,128)(2,1)} %mul.96) | data formatting | bytes 8847360 | tf_op jit(solution)/shard_map/mul | solution.py:57
  32.7 2.0 collective-permute-start.7
  34.8 8.6 %collective-permute-start.3 = (bf16[7,80,128]{2,1,0:T(8,128)(2,1)}, bf16[7,80,128]{2,1,0:T(8,128)(2,1)}, u32[]{:S(2)}, u32[]{:S(2)}) collective-permute-start(bf16[7,80,128]{2,1,0:T(8,128)(2,1)} %get-tuple-element.27), channel_id=1, source_target_pairs={{0,1},{1,2},{2,3},{3,4},{4,5},{5,6},{6,7},{7,8},{8,9},{9,10},{10,1... | collective-permute-start | bytes 430088 | tf_op jit(solution)/shard_map/ppermute | solution.py:229
  43.4 2.1 collective-permute-start.4
  48.8 1.7 select_reduce_fusion
  51.3 4.8 %broadcast_multiply_fusion.plane_ref.aplane_ref = bf16[5,576,768]{2,1,0:T(8,128)(2,1)} fusion(bf16[5,576,768]{2,1,0:T(8,128)(2,1)} %mul.97, bf16[576,768]{1,0:T(8,128)(2,1)S(1)} %convert_element_type.91), kind=kLoop, calls=%fused_computation.5 | loop fusion | flops 2211840 | bytes 9732096 | tf_op jit(solution)/shard_map/mul | solution.py:57
  57.3 1.2 copy.16
  58.6 2.3 convert_element_type.79.plane_ref.fplane_ref
  61.1 1.2 copy.20.line_ref.aline_ref
  63.1 2.0 pad_maximum_fusion.4.ext_ref
  65.6 15.4 %shard_map.64.blurred_ref = f32[4,32,64,128]{3,2,1,0:T(8,128)} custom-call(bf16[46,80,128]{2,1,0:T(8,128)(2,1)} %pad_maximum_fusion.4.ext_ref, bf16[384,512]{1,0:T(8,128)(2,1)} %convert_element_type.79.plane_ref.fplane_ref, bf16[4,384,256]{2,1,0:T(8,128)(2,1)} %bitcast.49), custom_call_target="tpu_custom_call" | custom-call | flops 4529848320 | bytes 2121728 | tf_op jit(solution)/shard_map/pallas_call | solution.py:213
  81.0 3.0 pad_maximum_fusion.here_ref
  84.0 9.4 %collective-permute-done.9 = bf16[32,64,128]{2,1,0:T(8,128)(2,1)S(1)} collective-permute-done((bf16[32,64,128]{2,1,0:T(8,128)(2,1)}, bf16[32,64,128]{2,1,0:T(8,128)(2,1)S(1)}, u32[]{:S(2)}, u32[]{:S(2)}) %collective-permute-start.9) | collective-permute-done | bytes 524320 | tf_op jit(solution)/shard_map/ppermute | solution.py:278
  93.3 11.2 %collective-permute-done.10 = bf16[32,64,128]{2,1,0:T(8,128)(2,1)S(1)} collective-permute-done((bf16[32,64,128]{2,1,0:T(8,128)(2,1)}, bf16[32,64,128]{2,1,0:T(8,128)(2,1)S(1)}, u32[]{:S(2)}, u32[]{:S(2)}) %collective-permute-start.10) | collective-permute-done | bytes 524320 | tf_op jit(solution)/shard_map/ppermute | solution.py:278
  104.6 11.2 %collective-permute-done.11 = bf16[32,64,128]{2,1,0:T(8,128)(2,1)S(1)} collective-permute-done((bf16[32,64,128]{2,1,0:T(8,128)(2,1)}, bf16[32,64,128]{2,1,0:T(8,128)(2,1)S(1)}, u32[]{:S(2)}, u32[]{:S(2)}) %collective-permute-start.11) | collective-permute-done | bytes 524320 | tf_op jit(solution)/shard_map/ppermute | solution.py:278
  115.8 1.6 pad_maximum_fusion.1.next_ref
  117.4 18.4 %shard_map.65 = f32[46,80,128]{2,1,0:T(8,128)} custom-call(s32[4]{0:T(128)} %fusion.9.offsets_ref, f32[4,32,64,128]{3,2,1,0:T(8,128)} %shard_map.64.blurred_ref, bf16[4,32,64,128]{3,2,1,0:T(8,128)(2,1)} %pad_maximum_fusion.here_ref, bf16[4,32,64,128]{3,2,1,0:T(8,128)(2,1)} %pad_maximum_fusion.1.next_ref, bf16[4,256,384]{2,1,0:T(8,128)(2,1)} %copy.20.line_ref.aline_ref, ...), custom_call_target="tpu_custom_call" | custom-call | flops 4529848320 | bytes 13598736 | tf_op jit(solution)/shard_map/pallas_call | solution.py:213
  136.9 3.0 %collective-permute-start.14 = (f32[7,80,128]{2,1,0:T(8,128)S(1)}, f32[7,80,128]{2,1,0:T(8,128)S(1)}, u32[]{:S(2)}, u32[]{:S(2)}) collective-permute-start(f32[7,80,128]{2,1,0:T(8,128)S(1)} %slice.164), channel_id=1, source_target_pairs={{0,1},{1,2},{2,3},{3,4},{4,5},{5,6},{6,7},{7,8},{8,9},{9,10},{10,1... | collective-permute-start | bytes 860168 | tf_op jit(solution)/shard_map/ppermute | solution.py:229
  140.0 6.1 %collective-permute-done.14 = f32[7,80,128]{2,1,0:T(8,128)S(1)} collective-permute-done((f32[7,80,128]{2,1,0:T(8,128)S(1)}, f32[7,80,128]{2,1,0:T(8,128)S(1)}, u32[]{:S(2)}, u32[]{:S(2)}) %collective-permute-start.14) | collective-permute-done | bytes 286752 | tf_op jit(solution)/shard_map/ppermute | solution.py:229
  147.2 1.9 collective-permute-start.15
  149.2 12.0 %collective-permute-done.15 = f32[7,80,128]{2,1,0:T(8,128)S(1)} collective-permute-done((f32[7,80,128]{2,1,0:T(8,128)S(1)}, f32[7,80,128]{2,1,0:T(8,128)S(1)}, u32[]{:S(2)}, u32[]{:S(2)}) %collective-permute-start.15) | collective-permute-done | bytes 286752 | tf_op jit(solution)/shard_map/ppermute | solution.py:233
  161.2 5.6 %collective-permute-start.16 = (f32[32,8,128]{2,1,0:T(8,128)S(1)}, f32[32,8,128]{2,1,0:T(8,128)S(1)}, u32[]{:S(2)}, u32[]{:S(2)}) collective-permute-start(f32[32,8,128]{2,1,0:T(8,128)S(1)} %pad_maximum_fusion.13), channel_id=1, source_target_pairs={{0,32},{32,64},{64,96},{1,33},{33,65},{65,97},{2,34},{34,66},{66,9... | collective-permute-start | bytes 393224 | tf_op jit(solution)/shard_map/ppermute | solution.py:229
  167.5 1.3 collective-permute-done.16
  168.8 1.9 collective-permute-start.17
  170.9 4.9 %collective-permute-done.17 = f32[32,8,128]{2,1,0:T(8,128)S(1)} collective-permute-done((f32[32,8,128]{2,1,0:T(8,128)S(1)}, f32[32,8,128]{2,1,0:T(8,128)S(1)}, u32[]{:S(2)}, u32[]{:S(2)}) %collective-permute-start.17) | collective-permute-done | bytes 131104 | tf_op jit(solution)/shard_map/ppermute | solution.py:233
  176.7 1.9 collective-permute-start.18
  178.7 2.4 collective-permute-start.19
  181.1 3.2 %collective-permute-done.19 = bf16[32,8,128]{2,1,0:T(8,128)(2,1)S(1)} collective-permute-done((bf16[32,8,128]{2,1,0:T(8,128)(2,1)S(1)}, bf16[32,8,128]{2,1,0:T(8,128)(2,1)S(1)}, u32[]{:S(2)}, u32[]{:S(2)}) %collective-permute-start.19) | collective-permute-done | bytes 65568 | tf_op jit(solution)/shard_map/ppermute | solution.py:233
  184.3 3.2 %collective-permute-start.20 = (bf16[7,80,128]{2,1,0:T(8,128)(2,1)S(1)}, bf16[7,80,128]{2,1,0:T(8,128)(2,1)S(1)}, u32[]{:S(2)}, u32[]{:S(2)}) collective-permute-start(bf16[7,80,128]{2,1,0:T(8,128)(2,1)S(1)} %get-tuple-element.25), channel_id=1, source_target_pairs={{0,1},{1,2},{2,3},{3,4},{4,5},{5,6},{6,7},{7,8},{8,9},{9,10},{10,1... | collective-permute-start | bytes 430088 | tf_op jit(solution)/shard_map/ppermute | solution.py:229
  187.5 2.1 collective-permute-start.21
  190.2 9.2 %collective-permute-done.21 = bf16[7,80,128]{2,1,0:T(8,128)(2,1)S(1)} collective-permute-done((bf16[7,80,128]{2,1,0:T(8,128)(2,1)S(1)}, bf16[7,80,128]{2,1,0:T(8,128)(2,1)S(1)}, u32[]{:S(2)}, u32[]{:S(2)}) %collective-permute-start.21) | collective-permute-done | bytes 143392 | tf_op jit(solution)/shard_map/ppermute | solution.py:233
  200.5 30.7 %shard_map.66 = f32[46,80,128]{2,1,0:T(8,128)} custom-call(s32[4]{0:T(128)} %fusion.9.offsets_ref, bf16[46,80,128]{2,1,0:T(8,128)(2,1)} %pad_maximum_fusion.5.ext_ref, bf16[4,32,64,128]{3,2,1,0:T(8,128)(2,1)} %pad_maximum_fusion.here_ref, bf16[4,32,64,128]{3,2,1,0:T(8,128)(2,1)} %pad_maximum_fusion.1.next_ref, ...), custom_call_target="tpu_custom_call" | custom-call | flops 9059696640 | bytes 11526160 | tf_op jit(solution)/shard_map/pallas_call | solution.py:213
  231.2 1.1 slice.172
  232.3 1.9 collective-permute-start.22
  234.2 8.7 %collective-permute-done.22 = f32[7,80,128]{2,1,0:T(8,128)S(1)} collective-permute-done((f32[7,80,128]{2,1,0:T(8,128)S(1)}, f32[7,80,128]{2,1,0:T(8,128)S(1)}, u32[]{:S(2)}, u32[]{:S(2)}) %collective-permute-start.22) | collective-permute-done | bytes 286752 | tf_op jit(solution)/shard_map/ppermute | solution.py:229
  244.0 1.9 collective-permute-start.23
  246.0 13.6 %collective-permute-done.23 = f32[7,80,128]{2,1,0:T(8,128)S(1)} collective-permute-done((f32[7,80,128]{2,1,0:T(8,128)S(1)}, f32[7,80,128]{2,1,0:T(8,128)S(1)}, u32[]{:S(2)}, u32[]{:S(2)}) %collective-permute-start.23) | collective-permute-done | bytes 286752 | tf_op jit(solution)/shard_map/ppermute | solution.py:233
  259.7 1.9 collective-permute-start.24
  261.6 1.9 collective-permute-done.24
  263.5 1.9 collective-permute-start.25
  265.6 4.9 %collective-permute-done.25 = f32[32,8,128]{2,1,0:T(8,128)S(1)} collective-permute-done((f32[32,8,128]{2,1,0:T(8,128)S(1)}, f32[32,8,128]{2,1,0:T(8,128)S(1)}, u32[]{:S(2)}, u32[]{:S(2)}) %collective-permute-start.25) | collective-permute-done | bytes 131104 | tf_op jit(solution)/shard_map/ppermute | solution.py:233
  272.3 23.3 %collective-permute-done.27 = f32[32,64,128]{2,1,0:T(8,128)S(1)} collective-permute-done((f32[32,64,128]{2,1,0:T(8,128)S(1)}, f32[32,64,128]{2,1,0:T(8,128)S(1)}, u32[]{:S(2)}, u32[]{:S(2)}) %collective-permute-start.27) | collective-permute-done | bytes 1048608 | tf_op jit(solution)/shard_map/ppermute | solution.py:225
  295.8 2.5 collective-permute-done.28
  (106 shorter events, 23.8 us)
Async XLA Ops:
  0.7 15.9 %collective-permute-start.12 = (bf16[4]{0:T(256)(128)(2,1)S(1)}, bf16[4]{0:T(256)(128)(2,1)S(1)}, u32[]{:S(2)}, u32[]{:S(2)}) collective-permute-start(bf16[4]{0:T(256)(128)(2,1)S(1)} %get-tuple-element.44), channel_id=1, source_target_pairs={{0,1},{1,2},{2,3},{3,4},{4,5},{5,6},{6,7},{7,8},{8,9},{9,10},{10,1... | collective-permute-start | bytes 32 | tf_op jit(solution)/shard_map/ppermute | solution.py:229
  5.7 11.0 %collective-permute-start.13 = (bf16[4]{0:T(256)(128)(2,1)S(1)}, bf16[4]{0:T(256)(128)(2,1)S(1)}, u32[]{:S(2)}, u32[]{:S(2)}) collective-permute-start(bf16[4]{0:T(256)(128)(2,1)S(1)} %get-tuple-element.44), channel_id=1, source_target_pairs={{1,0},{2,1},{3,2},{4,3},{5,4},{6,5},{7,6},{8,7},{9,8},{10,9},{11,1... | collective-permute-start | bytes 32 | tf_op jit(solution)/shard_map/ppermute | solution.py:233
  9.2 23.5 %collective-permute-start = (f32[1,136]{1,0:T(1,128)S(1)}, f32[1,136]{1,0:T(1,128)S(1)}, u32[]{:S(2)}, u32[]{:S(2)}) collective-permute-start(f32[1,136]{1,0:T(1,128)S(1)} %bitcast.57), channel_id=1, source_target_pairs={{0,32},{32,0},{64,96},{96,64},{1,33},{33,1},{65,97},{97,65},{2,34}... | collective-permute-start | bytes 1640 | tf_op jit(solution)/shard_map/ppermute | solution.py:225
  10.2 24.6 %collective-permute-start.1 = (f32[1,136]{1,0:T(1,128)S(1)}, f32[1,136]{1,0:T(1,128)S(1)}, u32[]{:S(2)}, u32[]{:S(2)}) collective-permute-start(f32[1,136]{1,0:T(1,128)S(1)} %bitcast.58), channel_id=1, source_target_pairs={{0,64},{32,96},{64,0},{96,32},{1,65},{33,97},{65,1},{97,33},{2,66}... | collective-permute-start | bytes 1640 | tf_op jit(solution)/shard_map/ppermute | solution.py:225
  10.9 32.4 %collective-permute-start.2 = (f32[1,136]{1,0:T(1,128)S(1)}, f32[1,136]{1,0:T(1,128)S(1)}, u32[]{:S(2)}, u32[]{:S(2)}) collective-permute-start(f32[1,136]{1,0:T(1,128)S(1)} %bitcast.59), channel_id=1, source_target_pairs={{0,96},{32,64},{64,32},{96,0},{1,97},{33,65},{65,33},{97,1},{2,98}... | collective-permute-start | bytes 1640 | tf_op jit(solution)/shard_map/ppermute | solution.py:225
  12.9 2.3 copy-start.3
  16.6 48.6 %collective-permute-start.5 = (bf16[32,64,128]{2,1,0:T(8,128)(2,1)}, bf16[32,64,128]{2,1,0:T(8,128)(2,1)}, u32[]{:S(2)}, u32[]{:S(2)}) collective-permute-start(bf16[32,64,128]{2,1,0:T(8,128)(2,1)} %get-tuple-element.14), channel_id=1, source_target_pairs={{0,32},{32,0},{64,96},{96,64},{1,33},{33,1},{65,97},{97,65},{2,34}... | collective-permute-start | bytes 1572872 | tf_op jit(solution)/shard_map/ppermute | solution.py:225
  16.7 48.5 %collective-permute-start.6 = (bf16[32,64,128]{2,1,0:T(8,128)(2,1)}, bf16[32,64,128]{2,1,0:T(8,128)(2,1)}, u32[]{:S(2)}, u32[]{:S(2)}) collective-permute-start(bf16[32,64,128]{2,1,0:T(8,128)(2,1)} %get-tuple-element.16), channel_id=1, source_target_pairs={{0,64},{32,96},{64,0},{96,32},{1,65},{33,97},{65,1},{97,33},{2,66}... | collective-permute-start | bytes 1572872 | tf_op jit(solution)/shard_map/ppermute | solution.py:225
  32.7 32.5 %collective-permute-start.7 = (bf16[32,64,128]{2,1,0:T(8,128)(2,1)}, bf16[32,64,128]{2,1,0:T(8,128)(2,1)}, u32[]{:S(2)}, u32[]{:S(2)}) collective-permute-start(bf16[32,64,128]{2,1,0:T(8,128)(2,1)} %get-tuple-element.15), channel_id=1, source_target_pairs={{0,96},{32,64},{64,32},{96,0},{1,97},{33,65},{65,33},{97,1},{2,98}... | collective-permute-start | bytes 1572872 | tf_op jit(solution)/shard_map/ppermute | solution.py:225
  34.8 28.3 %collective-permute-start.3 = (bf16[7,80,128]{2,1,0:T(8,128)(2,1)}, bf16[7,80,128]{2,1,0:T(8,128)(2,1)}, u32[]{:S(2)}, u32[]{:S(2)}) collective-permute-start(bf16[7,80,128]{2,1,0:T(8,128)(2,1)} %get-tuple-element.27), channel_id=1, source_target_pairs={{0,1},{1,2},{2,3},{3,4},{4,5},{5,6},{6,7},{7,8},{8,9},{9,10},{10,1... | collective-permute-start | bytes 430088 | tf_op jit(solution)/shard_map/ppermute | solution.py:229
  43.4 19.7 %collective-permute-start.4 = (bf16[7,80,128]{2,1,0:T(8,128)(2,1)}, bf16[7,80,128]{2,1,0:T(8,128)(2,1)}, u32[]{:S(2)}, u32[]{:S(2)}) collective-permute-start(bf16[7,80,128]{2,1,0:T(8,128)(2,1)} %get-tuple-element.28), channel_id=1, source_target_pairs={{1,0},{2,1},{3,2},{4,3},{5,4},{6,5},{7,6},{8,7},{9,8},{10,9},{11,1... | collective-permute-start | bytes 430088 | tf_op jit(solution)/shard_map/ppermute | solution.py:233
  58.6 2.3 copy-start.2
  58.6 4.5 %copy-start.4 = (bf16[1,32,64,128]{3,2,1,0:T(8,128)(2,1)S(1)}, bf16[1,32,64,128]{3,2,1,0:T(8,128)(2,1)}, u32[]{:S(2)}) copy-start(bf16[1,32,64,128]{3,2,1,0:T(8,128)(2,1)} %get-tuple-element.13) | copy-start | bytes 1572868
  63.1 20.9 %collective-permute-start.8 = (bf16[32,64,128]{2,1,0:T(8,128)(2,1)S(1)}, bf16[32,64,128]{2,1,0:T(8,128)(2,1)S(1)}, u32[]{:S(2)}, u32[]{:S(2)}) collective-permute-start(bf16[32,64,128]{2,1,0:T(8,128)(2,1)S(1)} %bitcast.46), channel_id=1, source_target_pairs={{1,0},{2,1},{3,2},{4,3},{5,4},{6,5},{7,6},{8,7},{9,8},{10,9},{11,1... | collective-permute-start | bytes 1572872 | tf_op jit(solution)/shard_map/ppermute | solution.py:278
  65.2 28.2 %collective-permute-start.9 = (bf16[32,64,128]{2,1,0:T(8,128)(2,1)}, bf16[32,64,128]{2,1,0:T(8,128)(2,1)S(1)}, u32[]{:S(2)}, u32[]{:S(2)}) collective-permute-start(bf16[32,64,128]{2,1,0:T(8,128)(2,1)} %collective-permute-done.5), channel_id=1, source_target_pairs={{1,0},{2,1},{3,2},{4,3},{5,4},{6,5},{7,6},{8,7},{9,8},{10,9},{11,1... | collective-permute-start | bytes 1572872 | tf_op jit(solution)/shard_map/ppermute | solution.py:278
  65.2 39.4 %collective-permute-start.10 = (bf16[32,64,128]{2,1,0:T(8,128)(2,1)}, bf16[32,64,128]{2,1,0:T(8,128)(2,1)S(1)}, u32[]{:S(2)}, u32[]{:S(2)}) collective-permute-start(bf16[32,64,128]{2,1,0:T(8,128)(2,1)} %collective-permute-done.6), channel_id=1, source_target_pairs={{1,0},{2,1},{3,2},{4,3},{5,4},{6,5},{7,6},{8,7},{9,8},{10,9},{11,1... | collective-permute-start | bytes 1572872 | tf_op jit(solution)/shard_map/ppermute | solution.py:278
  65.3 50.5 %collective-permute-start.11 = (bf16[32,64,128]{2,1,0:T(8,128)(2,1)}, bf16[32,64,128]{2,1,0:T(8,128)(2,1)S(1)}, u32[]{:S(2)}, u32[]{:S(2)}) collective-permute-start(bf16[32,64,128]{2,1,0:T(8,128)(2,1)} %collective-permute-done.7), channel_id=1, source_target_pairs={{1,0},{2,1},{3,2},{4,3},{5,4},{6,5},{7,6},{8,7},{9,8},{10,9},{11,1... | collective-permute-start | bytes 1572872 | tf_op jit(solution)/shard_map/ppermute | solution.py:278
  135.8 13.3 %copy-start.6 = (f32[46,80,128]{2,1,0:T(8,128)S(1)}, f32[46,80,128]{2,1,0:T(8,128)}, u32[]{:S(2)}) copy-start(f32[46,80,128]{2,1,0:T(8,128)} %shard_map.65) | copy-start | bytes 5652484
  136.9 9.2 %collective-permute-start.14 = (f32[7,80,128]{2,1,0:T(8,128)S(1)}, f32[7,80,128]{2,1,0:T(8,128)S(1)}, u32[]{:S(2)}, u32[]{:S(2)}) collective-permute-start(f32[7,80,128]{2,1,0:T(8,128)S(1)} %slice.164), channel_id=1, source_target_pairs={{0,1},{1,2},{2,3},{3,4},{4,5},{5,6},{6,7},{7,8},{8,9},{9,10},{10,1... | collective-permute-start | bytes 860168 | tf_op jit(solution)/shard_map/ppermute | solution.py:229
  147.2 19.6 %copy-start.7 = (s32[4,1]{0,1:T(1,128)S(1)}, s32[4,1]{0,1:T(1,128)}, u32[]{:S(2)}) copy-start(s32[4,1]{0,1:T(1,128)} %param.10) | copy-start | bytes 52
  147.2 14.0 %collective-permute-start.15 = (f32[7,80,128]{2,1,0:T(8,128)S(1)}, f32[7,80,128]{2,1,0:T(8,128)S(1)}, u32[]{:S(2)}, u32[]{:S(2)}) collective-permute-start(f32[7,80,128]{2,1,0:T(8,128)S(1)} %get-tuple-element.20), channel_id=1, source_target_pairs={{1,0},{2,1},{3,2},{4,3},{5,4},{6,5},{7,6},{8,7},{9,8},{10,9},{11,1... | collective-permute-start | bytes 860168 | tf_op jit(solution)/shard_map/ppermute | solution.py:233
  161.2 7.5 %collective-permute-start.16 = (f32[32,8,128]{2,1,0:T(8,128)S(1)}, f32[32,8,128]{2,1,0:T(8,128)S(1)}, u32[]{:S(2)}, u32[]{:S(2)}) collective-permute-start(f32[32,8,128]{2,1,0:T(8,128)S(1)} %pad_maximum_fusion.13), channel_id=1, source_target_pairs={{0,32},{32,64},{64,96},{1,33},{33,65},{65,97},{2,34},{34,66},{66,9... | collective-permute-start | bytes 393224 | tf_op jit(solution)/shard_map/ppermute | solution.py:229
  168.8 7.0 %collective-permute-start.17 = (f32[32,8,128]{2,1,0:T(8,128)S(1)}, f32[32,8,128]{2,1,0:T(8,128)S(1)}, u32[]{:S(2)}, u32[]{:S(2)}) collective-permute-start(f32[32,8,128]{2,1,0:T(8,128)S(1)} %get-tuple-element.24), channel_id=1, source_target_pairs={{32,0},{64,32},{96,64},{33,1},{65,33},{97,65},{34,2},{66,34},{98,6... | collective-permute-start | bytes 393224 | tf_op jit(solution)/shard_map/ppermute | solution.py:233
  170.7 5.1 %copy-start = (f32[32,256,128]{2,1,0:T(8,128)S(1)}, f32[32,256,128]{2,1,0:T(8,128)}, u32[]{:S(2)}) copy-start(f32[32,256,128]{2,1,0:T(8,128)} %param.6) | copy-start | bytes 12582916
  176.7 4.3 %collective-permute-start.18 = (bf16[32,8,128]{2,1,0:T(8,128)(2,1)S(1)}, bf16[32,8,128]{2,1,0:T(8,128)(2,1)S(1)}, u32[]{:S(2)}, u32[]{:S(2)}) collective-permute-start(bf16[32,8,128]{2,1,0:T(8,128)(2,1)S(1)} %get-tuple-element.29), channel_id=1, source_target_pairs={{0,32},{32,64},{64,96},{1,33},{33,65},{65,97},{2,34},{34,66},{66,9... | collective-permute-start | bytes 196616 | tf_op jit(solution)/shard_map/ppermute | solution.py:229
  178.7 5.6 %collective-permute-start.19 = (bf16[32,8,128]{2,1,0:T(8,128)(2,1)S(1)}, bf16[32,8,128]{2,1,0:T(8,128)(2,1)S(1)}, u32[]{:S(2)}, u32[]{:S(2)}) collective-permute-start(bf16[32,8,128]{2,1,0:T(8,128)(2,1)S(1)} %get-tuple-element.30), channel_id=1, source_target_pairs={{32,0},{64,32},{96,64},{33,1},{65,33},{97,65},{34,2},{66,34},{98,6... | collective-permute-start | bytes 196616 | tf_op jit(solution)/shard_map/ppermute | solution.py:233
  184.3 5.9 %collective-permute-start.20 = (bf16[7,80,128]{2,1,0:T(8,128)(2,1)S(1)}, bf16[7,80,128]{2,1,0:T(8,128)(2,1)S(1)}, u32[]{:S(2)}, u32[]{:S(2)}) collective-permute-start(bf16[7,80,128]{2,1,0:T(8,128)(2,1)S(1)} %get-tuple-element.25), channel_id=1, source_target_pairs={{0,1},{1,2},{2,3},{3,4},{4,5},{5,6},{6,7},{7,8},{8,9},{9,10},{10,1... | collective-permute-start | bytes 430088 | tf_op jit(solution)/shard_map/ppermute | solution.py:229
  187.5 11.9 %collective-permute-start.21 = (bf16[7,80,128]{2,1,0:T(8,128)(2,1)S(1)}, bf16[7,80,128]{2,1,0:T(8,128)(2,1)S(1)}, u32[]{:S(2)}, u32[]{:S(2)}) collective-permute-start(bf16[7,80,128]{2,1,0:T(8,128)(2,1)S(1)} %get-tuple-element.26), channel_id=1, source_target_pairs={{1,0},{2,1},{3,2},{4,3},{5,4},{6,5},{7,6},{8,7},{9,8},{10,9},{11,1... | collective-permute-start | bytes 430088 | tf_op jit(solution)/shard_map/ppermute | solution.py:233
  231.2 14.7 %copy-start.5 = (f32[46,80,128]{2,1,0:T(8,128)S(1)}, f32[46,80,128]{2,1,0:T(8,128)}, u32[]{:S(2)}) copy-start(f32[46,80,128]{2,1,0:T(8,128)} %shard_map.66) | copy-start | bytes 5652484
  232.3 10.6 %collective-permute-start.22 = (f32[7,80,128]{2,1,0:T(8,128)S(1)}, f32[7,80,128]{2,1,0:T(8,128)S(1)}, u32[]{:S(2)}, u32[]{:S(2)}) collective-permute-start(f32[7,80,128]{2,1,0:T(8,128)S(1)} %slice.172), channel_id=1, source_target_pairs={{0,1},{1,2},{2,3},{3,4},{4,5},{5,6},{6,7},{7,8},{8,9},{9,10},{10,1... | collective-permute-start | bytes 860168 | tf_op jit(solution)/shard_map/ppermute | solution.py:229
  244.0 15.6 %collective-permute-start.23 = (f32[7,80,128]{2,1,0:T(8,128)S(1)}, f32[7,80,128]{2,1,0:T(8,128)S(1)}, u32[]{:S(2)}, u32[]{:S(2)}) collective-permute-start(f32[7,80,128]{2,1,0:T(8,128)S(1)} %get-tuple-element.18), channel_id=1, source_target_pairs={{1,0},{2,1},{3,2},{4,3},{5,4},{6,5},{7,6},{8,7},{9,8},{10,9},{11,1... | collective-permute-start | bytes 860168 | tf_op jit(solution)/shard_map/ppermute | solution.py:233
  259.7 3.9 %collective-permute-start.24 = (f32[32,8,128]{2,1,0:T(8,128)S(1)}, f32[32,8,128]{2,1,0:T(8,128)S(1)}, u32[]{:S(2)}, u32[]{:S(2)}) collective-permute-start(f32[32,8,128]{2,1,0:T(8,128)S(1)} %pad_maximum_fusion.11), channel_id=1, source_target_pairs={{0,32},{32,64},{64,96},{1,33},{33,65},{65,97},{2,34},{34,66},{66,9... | collective-permute-start | bytes 393224 | tf_op jit(solution)/shard_map/ppermute | solution.py:229
  263.5 7.0 %collective-permute-start.25 = (f32[32,8,128]{2,1,0:T(8,128)S(1)}, f32[32,8,128]{2,1,0:T(8,128)S(1)}, u32[]{:S(2)}, u32[]{:S(2)}) collective-permute-start(f32[32,8,128]{2,1,0:T(8,128)S(1)} %get-tuple-element.22), channel_id=1, source_target_pairs={{32,0},{64,32},{96,64},{33,1},{65,33},{97,65},{34,2},{66,34},{98,6... | collective-permute-start | bytes 393224 | tf_op jit(solution)/shard_map/ppermute | solution.py:233
  271.9 23.7 %collective-permute-start.27 = (f32[32,64,128]{2,1,0:T(8,128)S(1)}, f32[32,64,128]{2,1,0:T(8,128)S(1)}, u32[]{:S(2)}, u32[]{:S(2)}) collective-permute-start(f32[32,64,128]{2,1,0:T(8,128)S(1)} %get-tuple-element.6), channel_id=1, source_target_pairs={{0,64},{32,96},{64,0},{96,32},{1,65},{33,97},{65,1},{97,33},{2,66}... | collective-permute-start | bytes 3145736 | tf_op jit(solution)/shard_map/ppermute | solution.py:225
  272.0 23.6 %collective-permute-start.26 = (f32[32,64,128]{2,1,0:T(8,128)S(1)}, f32[32,64,128]{2,1,0:T(8,128)S(1)}, u32[]{:S(2)}, u32[]{:S(2)}) collective-permute-start(f32[32,64,128]{2,1,0:T(8,128)S(1)} %get-tuple-element.6), channel_id=1, source_target_pairs={{0,32},{32,0},{64,96},{96,64},{1,33},{33,1},{65,97},{97,65},{2,34}... | collective-permute-start | bytes 3145736 | tf_op jit(solution)/shard_map/ppermute | solution.py:225
  295.6 2.7 collective-permute-start.28
  295.8 2.5 copy-start.1

commit v2 on v1

v2 whole, which is shorter than its diff:
```python
import functools

import jax
import jax.numpy as jnp
from jax import lax
from jax.experimental import pallas as pl
from jax.experimental.pallas import tpu as pltpu
from jax.sharding import PartitionSpec as P

BX, NY, NZ = 32, 256, 128
VIEWS, RANK, TAPS = 4, 3, 15
QY = NY // VIEWS
HX = TAPS // 2
HY = 8
EX, EY = BX + 2 * HX, QY + 2 * HY
PAIRS = VIEWS * RANK
YB = 16
YW = 32
FX = 2
FW = FX + TAPS - 1
AX = 4
AW = AX + TAPS - 1
KINDS = (0, 1, 2, 6, 7)
ROWS = 8
HALF = VIEWS // 2
VMEM_LIMIT = 56 * 1024 * 1024
KX, KY, KZ, OFFSET = (d * RANK * TAPS for d in range(4))


def iota(shape, dim):
    return lax.broadcasted_iota(jnp.int32, shape, dim)


def split(value):
    high = value.astype(jnp.bfloat16)
    return high, (value - high.astype(jnp.float32)).astype(jnp.bfloat16)


def prepare_kernel(small_ref, weights_ref, fplane_ref, aplane_ref, fline_ref, aline_ref):
    def tap(base, pair, t):
        return small_ref[pair // RANK, base + (pair % RANK) * TAPS + t]

    lane = iota((YB, 128), 1)
    t_y = (lane & (YW - 1)) - iota((YB, 128), 0) - 1
    group = lane >> 5
    for pair in range(PAIRS):
        y = jnp.zeros((YB, 128), jnp.float32)
        for t in range(TAPS):
            y = jnp.where(t_y == t, tap(KY, pair, t), y)
        for dx in range(FX):
            for column in range(FW * YW // 128):
                x = jnp.zeros((YB, 128), jnp.float32)
                for j in range(4):
                    t = 4 * column + j - dx
                    if 0 <= t < TAPS:
                        x = jnp.where(group == j, tap(KX, pair, t), x)
                row = (pair * FX + dx) * YB
                fplane_ref[row : row + YB, column * 128 : column * 128 + 128] = (x * y).astype(jnp.bfloat16)

    lane = iota((YW, 128), 1)
    t_y = iota((YW, 128), 0) - (lane & (YB - 1)) - 1
    group = lane >> 4
    for column in range(PAIRS // 2):
        pairs = (2 * column, 2 * column + 1)
        first = group < AX
        y = jnp.zeros((YW, 128), jnp.float32)
        for t in range(TAPS):
            y = jnp.where(t_y == t, jnp.where(first, tap(KY, pairs[0], t), tap(KY, pairs[1], t)), y)
        sided = [
            y * jnp.where(first, weights_ref[side, pairs[0] // RANK], weights_ref[side, pairs[1] // RANK])
            for side in range(3)
        ]
        for xw in range(AW):
            x = jnp.zeros((YW, 128), jnp.float32)
            for half in range(2):
                for dx in range(AX):
                    if 0 <= xw - dx < TAPS:
                        x = jnp.where(group == half * AX + dx, tap(KX, pairs[half], xw - dx), x)
            made = {}
            for kind, step in enumerate(KINDS):
                row = step * AX + xw
                side = 0 if row < HX else 1 if row < HX + BX else 2
                if side not in made:
                    made[side] = (x * sided[side]).astype(jnp.bfloat16)
                aplane_ref[kind, xw * YW : xw * YW + YW, column * 128 : column * 128 + 128] = made[side]

    t_z = iota((NZ, NZ), 0) - iota((NZ, NZ), 1) + TAPS // 2

    @pl.loop(0, VIEWS)
    def _(view):
        for term in range(RANK):
            forward = jnp.zeros((NZ, NZ), jnp.float32)
            adjoint = jnp.zeros((NZ, NZ), jnp.float32)
            for t in range(TAPS):
                k = small_ref[view, KZ + term * TAPS + t]
                forward = jnp.where(t_z == t, k, forward)
                adjoint = jnp.where(t_z == TAPS - 1 - t, k, adjoint)
            at = term * NZ
            high, low = split(forward)
            fline_ref[view, at : at + NZ, :NZ] = high
            fline_ref[view, at : at + NZ, NZ:] = low
            high, low = split(adjoint)
            aline_ref[view, :NZ, at : at + NZ] = high
            aline_ref[view, NZ:, at : at + NZ] = low


def forward_plane(ext_ref, plane_ref, mid_ref):
    @pl.loop(0, BX // (2 * FX))
    def _(step):
        x0 = step * (2 * FX)
        for y0 in range(0, QY, YB):
            parts = [
                ext_ref[pl.ds(x0 + part * FX, FW), y0 : y0 + YW, :].reshape(FW * YW, NZ)
                for part in range(2)
            ]
            made = jnp.dot(
                plane_ref[...],
                jnp.concatenate(parts, axis=1),
                preferred_element_type=jnp.float32,
            ).astype(jnp.bfloat16)
            for view in range(VIEWS):
                for term in range(RANK):
                    for part in range(2):
                        for dx in range(FX):
                            row = ((view * RANK + term) * FX + dx) * YB
                            mid_ref[
                                view, x0 + part * FX + dx, y0 : y0 + YB, term * NZ : (term + 1) * NZ
                            ] = made[row : row + YB, part * NZ : (part + 1) * NZ]


def forward_line(mid_ref, line_ref, view, x0):
    a = mid_ref[view, pl.ds(x0, ROWS)].reshape(ROWS * QY, RANK * NZ)
    made = jnp.dot(a, line_ref[view], preferred_element_type=jnp.float32)
    return made[:, :NZ] + made[:, NZ:]


def quotient_rows(tiles_ref, slot, start, blurred):
    merged = tiles_ref[slot, pl.ds(start, ROWS)].reshape(ROWS * QY, NZ)
    return (merged.astype(jnp.float32) / blurred).astype(jnp.bfloat16)


def adjoint_line(quotient, line_ref, back_ref, view, slot, x0):
    doubled = jnp.concatenate([quotient, quotient], axis=1)
    made = jnp.dot(doubled, line_ref[view], preferred_element_type=jnp.float32).astype(jnp.bfloat16)
    for term in range(RANK):
        back_ref[slot * RANK + term, pl.ds(x0, ROWS)] = made[:, term * NZ : (term + 1) * NZ].reshape(
            ROWS, QY, NZ
        )


def adjoint_plane(back_ref, plane_ref, out_ref, first_pair, pairs):
    columns = slice(first_pair * AX * YB, (first_pair + pairs) * AX * YB)

    @pl.loop(0, BX // AX)
    def _(step):
        x0 = step * AX
        kind = jnp.minimum(step, 2) + jnp.maximum(step - 5, 0)
        for y0 in range(0, QY // 2, YB):
            starts = (y0, y0 + QY // 2)
            parts = [
                back_ref[:pairs, pl.ds(x0, AX), at : at + YB, :].reshape(pairs * AX * YB, NZ)
                for at in starts
            ]
            made = jnp.dot(
                plane_ref[kind, :, columns],
                jnp.concatenate(parts, axis=1),
                preferred_element_type=jnp.float32,
            )
            for part, at in enumerate(starts):
                out_ref[pl.ds(x0, AW), at : at + YW, :] += made[
                    :, part * NZ : (part + 1) * NZ
                ].reshape(AW, YW, NZ)


def edges(out_ref, up_ref, down_ref):
    rows = up_ref.shape[0]
    up_ref[...] = out_ref[:rows]
    down_ref[...] = out_ref[EX - rows :]


def blur_kernel(ext_ref, plane_ref, line_hbm, first_ref, last_ref, mid_ref, line_ref, sem):
    copy = pltpu.make_async_copy(line_hbm, line_ref, sem.at[0])
    copy.start()
    forward_plane(ext_ref, plane_ref, mid_ref)
    copy.wait()
    for view in range(VIEWS):
        out_ref = (first_ref, last_ref)[view // HALF]

        @pl.loop(0, BX // ROWS)
        def _(step):
            x0 = step * ROWS
            blurred = forward_line(mid_ref, line_ref, view, x0)
            out_ref[view % HALF, pl.ds(x0, ROWS)] = blurred.reshape(ROWS, QY, NZ)


def back_kernel(first_view, begun, edge_rows, *refs):
    refs = list(refs)
    offsets_ref, blurred_hbm = refs[:2]
    tiles_hbm = refs[2 : 2 + 2 * HALF]
    line_ref, plane_hbm = refs[2 + 2 * HALF : 4 + 2 * HALF]
    rest = refs[4 + 2 * HALF :]
    before_ref = rest.pop(0) if begun else None
    out_refs = [rest.pop(0) for _ in range(3 if begun else 1)]
    blurred_ref, tiles_ref, plane_ref, back_ref, sems = rest
    out_ref = out_refs[0]
    copies = [
        [pltpu.make_async_copy(blurred_hbm.at[slot], blurred_ref.at[slot], sems.at[slot])]
        + [
            pltpu.make_async_copy(
                tiles_hbm[2 * slot + part],
                tiles_ref.at[slot, pl.ds(part * BX, BX)],
                sems.at[HALF + 2 * slot + part],
            )
            for part in range(2)
        ]
        for slot in range(HALF)
    ]
    plane_copy = pltpu.make_async_copy(plane_hbm, plane_ref, sems.at[3 * HALF])
    for copy in copies[0] + copies[1] + [plane_copy]:
        copy.start()
    out_ref[...] = before_ref[...] if begun else jnp.zeros_like(out_ref)
    for slot in range(HALF):
        view = first_view + slot
        offset = offsets_ref[view]
        for copy in copies[slot]:
            copy.wait()

        @pl.loop(0, BX // ROWS)
        def _(step):
            x0 = step * ROWS
            blurred = blurred_ref[slot, pl.ds(x0, ROWS)].reshape(ROWS * QY, NZ)
            quotient = quotient_rows(tiles_ref, slot, offset + x0, blurred)
            adjoint_line(quotient, line_ref, back_ref, view, slot, x0)

    plane_copy.wait()
    adjoint_plane(back_ref, plane_ref, out_ref, first_view * RANK, HALF * RANK)
    if begun:
        edges(*out_refs)


def both_kernel(offsets_ref, ext_ref, fplane_ref, fline_hbm, aline_hbm, aplane_hbm, *refs):
    tiles_hbm = refs[: 2 * VIEWS]
    out_ref, up_ref, down_ref, mid_ref, back_ref, fline_ref, aline_ref, aplane_ref, tiles_ref, sems = refs[
        2 * VIEWS :
    ]
    line_copies = [
        pltpu.make_async_copy(fline_hbm, fline_ref, sems.at[0]),
        pltpu.make_async_copy(aline_hbm, aline_ref, sems.at[1]),
    ]
    plane_copy = pltpu.make_async_copy(aplane_hbm, aplane_ref, sems.at[2])
    tile_copies = [
        pltpu.make_async_copy(
            tiles_hbm[2 * view + part], tiles_ref.at[view, pl.ds(part * BX, BX)], sems.at[3 + 2 * view + part]
        )
        for view in range(VIEWS)
        for part in range(2)
    ]
    for copy in line_copies + tile_copies + [plane_copy]:
        copy.start()
    out_ref[...] = jnp.zeros_like(out_ref)
    forward_plane(ext_ref, fplane_ref, mid_ref)
    for copy in line_copies + tile_copies:
        copy.wait()
    for view in range(VIEWS):
        offset = offsets_ref[view]

        @pl.loop(0, BX // ROWS)
        def _(step):
            x0 = step * ROWS
            blurred = forward_line(mid_ref, fline_ref, view, x0)
            quotient = quotient_rows(tiles_ref, view, offset + x0, blurred)
            adjoint_line(quotient, aline_ref, back_ref, view, view, x0)

    plane_copy.wait()
    adjoint_plane(back_ref, aplane_ref, out_ref, 0, PAIRS)
    edges(out_ref, up_ref, down_ref)


VMEM = pl.BlockSpec(memory_space=pltpu.VMEM)
SMEM = pl.BlockSpec(memory_space=pltpu.SMEM)
ANY = pl.BlockSpec(memory_space=pl.ANY)
F32, BF16 = jnp.float32, jnp.bfloat16
FPLANE = ((PAIRS * FX * YB, FW * YW), BF16)
APLANE = ((len(KINDS), AW * YW, PAIRS * AX * YB), BF16)
FLINE = ((VIEWS, RANK * NZ, 2 * NZ), BF16)
ALINE = ((VIEWS, 2 * NZ, RANK * NZ), BF16)
MID = ((VIEWS, BX, QY, RANK * NZ), BF16)
SUMS = ((EX, EY, NZ), F32)
FLOPS = 2 * VIEWS * BX * QY * NZ * RANK * 3 * TAPS * 16


def call(kernel, outs, in_specs, scratch, flops, args):
    bytes_all = sum(a.size * a.dtype.itemsize for a in args)
    return pl.pallas_call(
        kernel,
        out_shape=[jax.ShapeDtypeStruct(*out) for out in outs],
        in_specs=in_specs,
        out_specs=[VMEM] * len(outs),
        scratch_shapes=[
            pltpu.SemaphoreType.DMA((s,)) if isinstance(s, int) else pltpu.VMEM(*s) for s in scratch
        ],
        compiler_params=pltpu.CompilerParams(vmem_limit_bytes=VMEM_LIMIT),
        cost_estimate=pl.CostEstimate(flops=flops, bytes_accessed=bytes_all, transcendentals=0),
    )(*args)


def to_xor(value, by):
    return lax.ppermute(value, "view", [(i, i ^ by) for i in range(VIEWS)])


def exchange(axis, to_previous, to_next):
    up = [(i, i + 1) for i in range(lax.axis_size(axis) - 1)]
    from_previous = lax.ppermute(to_next, axis, up)
    from_next = lax.ppermute(to_previous, axis, [(j, i) for i, j in up])
    return lax.optimization_barrier((from_previous, from_next))


def fold(value, from_previous, from_next, dim, skip):
    width, size = from_next.shape[dim], value.shape[dim]
    pads = [[(0, 0)] * 3 for _ in range(2)]
    pads[0][dim] = (skip, size - width - skip)
    pads[1][dim] = (size - width - skip, skip)
    return value + jnp.pad(from_previous, pads[0]) + jnp.pad(from_next, pads[1])


def shards(start_estimate, observed, psf_taps, offsets, coverage):
    me = lax.axis_index("view")
    bricks = lax.axis_size("brick")

    pieces = [lax.dynamic_slice_in_dim(observed[0], QY * (me ^ by), QY, 1) for by in range(VIEWS)]
    pieces, start_estimate, psf_taps, coverage = lax.optimization_barrier(
        (pieces, start_estimate, psf_taps, coverage)
    )
    tiles = []
    for by, piece in enumerate(pieces):
        piece = to_xor(piece, by) if by else piece
        tiles.append((piece, lax.ppermute(piece, "brick", [((i + 1) % bricks, i) for i in range(bricks)])))

    small = jnp.concatenate([psf_taps.reshape(-1), offsets.astype(F32)])[None]
    smalls = jnp.concatenate([small] + [to_xor(small, by) for by in range(1, VIEWS)], axis=0)
    shifts = smalls[:, OFFSET].astype(jnp.int32)
    covered = coverage[:, 0].astype(F32)
    before, after = exchange("brick", covered, covered)
    covers = jnp.stack([before, covered, after])
    weights = jnp.concatenate(
        [lax.dynamic_slice_in_dim(covers, me ^ by, 1, 1) for by in range(VIEWS)], axis=1
    )
    counts = jnp.maximum(jnp.sum(covers, axis=1), 1.0)
    row_counts = jnp.concatenate(
        [jnp.full((HX,), counts[0]), jnp.full((BX,), counts[1]), jnp.full((HX,), counts[2])]
    )[:, None, None]
    fplane, aplane, fline, aline = call(
        prepare_kernel, [FPLANE, APLANE, FLINE, ALINE], [SMEM, SMEM], [], 10**9, (smalls, weights)
    )

    padded = jnp.pad(start_estimate, ((0, 0), (HY, HY), (0, 0)))
    estimate = lax.dynamic_slice_in_dim(padded, QY * me, EY, 1)
    edge = estimate.astype(BF16)
    before, after = exchange("brick", edge[:HX], edge[BX - HX :])
    estimate = jnp.concatenate([before.astype(F32), estimate, after.astype(F32)], axis=0)

    half = ((HALF, BX, QY, NZ), F32)
    blurred = call(
        blur_kernel,
        [half, half],
        [VMEM, VMEM, ANY],
        [MID, FLINE, 1],
        FLOPS,
        (estimate.astype(BF16), fplane, fline),
    )
    tile_scratch = lambda views: ((views, 2 * BX, QY, NZ), BF16)
    back_scratch = lambda views: ((views * RANK, BX, QY, NZ), BF16)
    terms = ()
    for part in range(2):
        first_view = part * HALF
        outs = [SUMS, ((2 * HX, EY, NZ), F32), ((2 * HX, EY, NZ), F32)] if part else [SUMS]
        own_tiles = [tile for pair in tiles[first_view : first_view + HALF] for tile in pair]
        terms = call(
            functools.partial(back_kernel, first_view, part == 1, 2 * HX),
            outs,
            [SMEM] + [ANY] * (1 + 2 * HALF) + [VMEM, ANY] + [VMEM] * part,
            [half, tile_scratch(HALF), APLANE, back_scratch(HALF), 3 * HALF + 1],
            FLOPS // 2,
            (shifts, blurred[part], *own_tiles, aline, aplane, *terms),
        )
    summed, to_previous, to_next = terms
    summed = fold(summed, *exchange("brick", to_previous, to_next), 0, 0)
    summed = fold(summed, *exchange("view", summed[:, : 2 * HY], summed[:, QY:]), 1, 0)
    estimate = estimate * summed / row_counts

    summed, to_previous, to_next = call(
        both_kernel,
        [SUMS, ((HX, EY, NZ), F32), ((HX, EY, NZ), F32)],
        [SMEM, VMEM, VMEM] + [ANY] * (3 + 2 * VIEWS),
        [MID, back_scratch(VIEWS), FLINE, ALINE, APLANE, tile_scratch(VIEWS), 3 + 2 * VIEWS],
        2 * FLOPS,
        (shifts, estimate.astype(BF16), fplane, fline, aline, aplane, *[tile for pair in tiles for tile in pair]),
    )
    summed = fold(summed[HX : HX + BX], *exchange("brick", to_previous, to_next), 0, 0)
    summed = fold(
        summed[:, HY : HY + QY], *exchange("view", summed[:, :HY], summed[:, EY - HY :]), 1, 0
    )
    estimate = estimate[HX : HX + BX, HY : HY + QY] * summed / counts[1]

    across = to_xor(estimate, 2)
    quarters = [estimate, to_xor(estimate, 1), across, to_xor(across, 1)]
    result = jnp.zeros(start_estimate.shape, F32)
    for by in range(VIEWS):
        result = lax.dynamic_update_slice_in_dim(result, quarters[by], QY * (me ^ by), 1)
    return result


def solution(mesh):
    in_specs = (
        P("brick", None, None),
        P("view", "brick", None, None),
        P("view", None, None, None),
        P("view"),
        P(None, "brick"),
    )
    out_specs = P("brick", None, None)
    return jax.shard_map(shards, mesh=mesh, in_specs=in_specs, out_specs=out_specs, check_vma=False)
```

time: 300 us -> 246 us (0.82)
  local copies, waits for them, and re-layouts: 30.2 us -> 9.32 us
  other arithmetic: 25.5 us -> 10.3 us
  waiting for transfers between devices: 124 us -> 112 us
  starting transfers between devices: 53.8 us -> 48.1 us
    ppermute x9, waiting for transfers between devices: 25.8 us -> 69 us  [to_xor(): return lax.ppermute(value, 'view', [(i, i ^ by) for i in range(VIEWS)])]
    ppermute x4, waiting for transfers between devices: 31.8 us -> 0.01 us  [shards(): lax.ppermute(piece, 'brick', [((i + 1) % bricks, i) for i in range(bricks)])]
    ppermute x16 -> x12, waiting for transfers between devices: 66.4 us -> 43 us  [the longest x6 30.3 us: exchange(): from_next = lax.ppermute(to_previous, axis, [(j, i) for i, j in up])]
    mul x6 -> x0, local copies, waits for them, and re-layouts: 15.7 us -> none  [the longest x2 15 us: weighted_planes(): scaled = scale * adjoint.reshape(1, AW, YW, VIEWS, RANK * AX * YB)]
    ppermute x16 -> x12, starting transfers between devices: 47.5 us -> 41.3 us  [the longest x6 28.2 us: exchange(): from_previous = lax.ppermute(to_next, axis, up)]
    convert_element_type x3 -> x0, local copies, waits for them, and re-layouts: 4.93 us -> none  [the longest x1 2.28 us: plane_matrices(): forward = forward.astype(jnp.bfloat16).reshape(PAIRS * FX * YB, FW * YW)]
    mul x1 -> x0, other arithmetic: 4.83 us -> none  [weighted_planes(): scaled = scale * adjoint.reshape(1, AW, YW, VIEWS, RANK * AX * YB)]
    another operation x3 -> x1, other arithmetic: 4.56 us -> 0.12 us  [shards(): covers = jnp.stack([before, covered, after])]
  transfers between devices with their start and end apart: 29 -> 25, of which waited for: 16 -> 11; matrix products, arithmetic and copies ran while one was open for 15% -> 3% of each run, Pallas kernels for 5% -> 12%
where the time goes in v2:
time: 246 us; the launch traced here: 245 us
  waiting for transfers between devices  112 us (46%)
  Pallas kernels  64.1 us (26%)
  starting transfers between devices  48.1 us (20%)
  other arithmetic  10.3 us (4%)
  local copies, waits for them, and re-layouts  9.32 us (4%)
    ppermute x9, waiting for transfers between devices, to_xor(): return lax.ppermute(value, 'view', [(i, i ^ by) for i in range(VIEWS)])  69 us
    pallas_call x5, Pallas kernels, call(): pl.pallas_call(kernel, out_shape=[jax.ShapeDtypeStruct(*out) for out in o...  64.1 us
    ppermute x6, waiting for transfers between devices, exchange(): from_next = lax.ppermute(to_previous, axis, [(j, i) for i, j in up])  30.3 us
    ppermute x6, starting transfers between devices, exchange(): from_previous = lax.ppermute(to_next, axis, up)  28.2 us
    ppermute x6, starting transfers between devices, exchange(): from_next = lax.ppermute(to_previous, axis, [(j, i) for i, j in up])  13.1 us
    ppermute x6, waiting for transfers between devices, exchange(): from_previous = lax.ppermute(to_next, axis, up)  12.7 us
    ppermute x9, starting transfers between devices, to_xor(): return lax.ppermute(value, 'view', [(i, i ^ by) for i in range(VIEWS)])  6.71 us
  transfers between devices with their start and end apart: 25, of which 11 were waited for; matrix products, arithmetic and copies ran while one was open for 3% of the time, Pallas kernels for 12%

profile of v2, /device:TPU:31, one launch (start us, length us, event | category | flops | bytes accessed | tf_op | source)
XLA Modules:
  0.0 244.9 jit_solution(16938139834391883483)
XLA Ops:
  0.0 2.8 %dynamic-slice_bitcast_fusion = (bf16[32,64,128]{2,1,0:T(8,128)(2,1)}, bf16[32,64,128]{2,1,0:T(8,128)(2,1)S(1)}, bf16[32,64,128]{2,1,0:T(8,128)(2,1)S(1)}, bf16[32,64,128]{2,1,0:T(8,128)(2,1)}) fusion(bf16[1,32,256,128]{3,2,1,0:T(8,128)(2,1)} %param.6, s32[]{:T(128)S(6)} %select_n.34, s32[]{:T(128)S(6)} %select_n.32, s32[]{:T(128)S(6)} %select_n.31, ...), kind=kLoop, calls=%fused_computation.10 | loop fusion | bytes 4194320 | tf_op jit(solution)/shard_map/dynamic_slice | solution.py:330
  2.8 5.1 %collective-permute-start.5 = (f32[4]{0:T(128)S(1)}, f32[4]{0:T(128)S(1)}, u32[]{:S(2)}, u32[]{:S(2)}) collective-permute-start(f32[4]{0:T(128)S(1)} %get-tuple-element.93), channel_id=1, source_target_pairs={{0,1},{1,2},{2,3},{3,4},{4,5},{5,6},{6,7},{7,8},{8,9},{9,10},{10,1... | collective-permute-start | bytes 56 | tf_op jit(solution)/shard_map/ppermute | solution.py:313
  7.9 1.9 collective-permute-start.6
  10.7 1.0 collective-permute-start.2
  11.7 0.8 collective-permute-start.3
  12.4 1.0 collective-permute-start.4
  13.4 1.5 fusion.8
  15.1 2.8 %collective-permute-done.6 = f32[4]{0:T(128)S(1)} collective-permute-done((f32[4]{0:T(128)S(1)}, f32[4]{0:T(128)S(1)}, u32[]{:S(2)}, u32[]{:S(2)}) %collective-permute-start.6) | collective-permute-done | bytes 48 | tf_op jit(solution)/shard_map/ppermute | solution.py:314
  17.9 2.7 %collective-permute-start.9 = (bf16[32,64,128]{2,1,0:T(8,128)(2,1)}, bf16[32,64,128]{2,1,0:T(8,128)(2,1)S(1)}, u32[]{:S(2)}, u32[]{:S(2)}) collective-permute-start(bf16[32,64,128]{2,1,0:T(8,128)(2,1)} %get-tuple-element.47), channel_id=1, source_target_pairs={{0,96},{32,64},{64,32},{96,0},{1,97},{33,65},{65,33},{97,1},{2,98}... | collective-permute-start | bytes 1572872 | tf_op jit(solution)/shard_map/ppermute | solution.py:308
  20.9 0.8 collective-permute-start.7
  21.6 0.7 pad_maximum_fusion.3.weights_ref
  22.3 4.9 %collective-permute-start = (bf16[7,80,128]{2,1,0:T(8,128)(2,1)S(1)}, bf16[7,80,128]{2,1,0:T(8,128)(2,1)S(1)}, u32[]{:S(2)}, u32[]{:S(2)}) collective-permute-start(bf16[7,80,128]{2,1,0:T(8,128)(2,1)S(1)} %get-tuple-element.82), channel_id=1, source_target_pairs={{0,1},{1,2},{2,3},{3,4},{4,5},{5,6},{6,7},{7,8},{8,9},{9,10},{10,1... | collective-permute-start | bytes 430088 | tf_op jit(solution)/shard_map/ppermute | solution.py:313
  27.2 1.9 collective-permute-start.1
  29.7 6.7 %shard_map.55 = (bf16[384,512]{1,0:T(8,128)(2,1)}, bf16[5,576,768]{2,1,0:T(8,128)(2,1)}, bf16[4,384,256]{2,1,0:T(8,128)(2,1)}, bf16[4,256,384]{2,1,0:T(8,128)(2,1)}) custom-call(f32[4,136]{1,0:T(4,128)} %pad_maximum_fusion.1.small_ref, f32[3,4]{1,0:T(4,128)} %pad_maximum_fusion.3.weights_ref), custom_call_target="tpu_custom_call" | custom-call | flops 1000000000 | bytes 2224 | tf_op jit(solution)/shard_map/pallas_call | solution.py:294
  36.4 0.7 fusion.4.refs_0_.offsets_ref
  37.1 2.3 collective-permute-done.1
  39.6 1.1 fusion.ext_ref
  40.7 43.2 %collective-permute-done.7.refs_2_.refs_4_ = bf16[32,64,128]{2,1,0:T(8,128)(2,1)S(1)} collective-permute-done((bf16[32,64,128]{2,1,0:T(8,128)(2,1)}, bf16[32,64,128]{2,1,0:T(8,128)(2,1)S(1)}, u32[]{:S(2)}, u32[]{:S(2)}) %collective-permute-start.7) | collective-permute-done | bytes 524320 | tf_op jit(solution)/shard_map/ppermute | solution.py:308
  83.9 12.5 %shard_map.56 = (f32[2,32,64,128]{3,2,1,0:T(8,128)}, f32[2,32,64,128]{3,2,1,0:T(8,128)}) custom-call(bf16[46,80,128]{2,1,0:T(8,128)(2,1)} %fusion.ext_ref, bf16[384,512]{1,0:T(8,128)(2,1)} %get-tuple-element.43.plane_ref.fplane_ref, bf16[4,384,256]{2,1,0:T(8,128)(2,1)} %get-tuple-element.44.line_hbm.fline_hbm), custom_call_target="tpu_custom_call" | custom-call | flops 4529848320 | bytes 2121728 | tf_op jit(solution)/shard_map/pallas_call | solution.py:294
  96.5 0.8 copy-done.5
  97.4 10.2 %shard_map.57.refs_8_ = f32[46,80,128]{2,1,0:T(8,128)} custom-call(s32[4]{0:T(128)} %fusion.4.refs_0_.offsets_ref, f32[2,32,64,128]{3,2,1,0:T(8,128)} %get-tuple-element.50.refs_1_, bf16[32,64,128]{2,1,0:T(8,128)(2,1)} %copy-done.1, bf16[32,64,128]{2,1,0:T(8,128)(2,1)} %copy-done.5, bf16[32,64,128]{2,1,0:T(8,128)(2,1)} %copy-done.2, ...), custom_call_target="tpu_custom_call" | custom-call | flops 2264924160 | bytes 9404432 | tf_op jit(solution)/shard_map/pallas_call | solution.py:294
  107.7 0.8 copy-done.7
  108.7 11.2 %shard_map.58 = (f32[46,80,128]{2,1,0:T(8,128)}, f32[14,80,128]{2,1,0:T(8,128)}, f32[14,80,128]{2,1,0:T(8,128)}) custom-call(s32[4]{0:T(128)} %fusion.4.refs_0_.offsets_ref, f32[2,32,64,128]{3,2,1,0:T(8,128)} %get-tuple-element.45.refs_1_, bf16[32,64,128]{2,1,0:T(8,128)(2,1)} %copy-done.4, bf16[32,64,128]{2,1,0:T(8,128)(2,1)} %copy-done.8, ...), custom_call_target="tpu_custom_call" | custom-call | flops 2264924160 | bytes 11288592 | tf_op jit(solution)/shard_map/pallas_call | solution.py:294
  119.8 8.9 %collective-permute-start.14 = (f32[14,80,128]{2,1,0:T(8,128)}, f32[14,80,128]{2,1,0:T(8,128)S(1)}, u32[]{:S(2)}, u32[]{:S(2)}) collective-permute-start(f32[14,80,128]{2,1,0:T(8,128)} %get-tuple-element.54), channel_id=1, source_target_pairs={{0,1},{1,2},{2,3},{3,4},{4,5},{5,6},{6,7},{7,8},{8,9},{9,10},{10,1... | collective-permute-start | bytes 1720328 | tf_op jit(solution)/shard_map/ppermute | solution.py:313
  128.8 1.9 collective-permute-start.15
  130.7 10.1 %collective-permute-done.14 = f32[14,80,128]{2,1,0:T(8,128)S(1)} collective-permute-done((f32[14,80,128]{2,1,0:T(8,128)}, f32[14,80,128]{2,1,0:T(8,128)S(1)}, u32[]{:S(2)}, u32[]{:S(2)}) %collective-permute-start.14) | collective-permute-done | bytes 573472 | tf_op jit(solution)/shard_map/ppermute | solution.py:313
  140.7 9.4 %collective-permute-done.15 = f32[14,80,128]{2,1,0:T(8,128)S(1)} collective-permute-done((f32[14,80,128]{2,1,0:T(8,128)}, f32[14,80,128]{2,1,0:T(8,128)S(1)}, u32[]{:S(2)}, u32[]{:S(2)}) %collective-permute-start.15) | collective-permute-done | bytes 573472 | tf_op jit(solution)/shard_map/ppermute | solution.py:314
  150.2 1.7 pad_add_fusion
  151.9 4.4 %collective-permute-start.16 = (f32[46,16,128]{2,1,0:T(8,128)S(1)}, f32[46,16,128]{2,1,0:T(8,128)S(1)}, u32[]{:S(2)}, u32[]{:S(2)}) collective-permute-start(f32[46,16,128]{2,1,0:T(8,128)S(1)} %get-tuple-element.78), channel_id=1, source_target_pairs={{0,32},{32,64},{64,96},{1,33},{33,65},{65,97},{2,34},{34,66},{66,9... | collective-permute-start | bytes 1130504 | tf_op jit(solution)/shard_map/ppermute | solution.py:313
  156.4 2.1 collective-permute-start.17
  158.5 0.7 fusion.12
  159.1 0.6 broadcast_in_dim.18
  159.8 0.7 broadcast_in_dim.19
  161.2 4.1 %collective-permute-done.17 = f32[46,16,128]{2,1,0:T(8,128)S(1)} collective-permute-done((f32[46,16,128]{2,1,0:T(8,128)S(1)}, f32[46,16,128]{2,1,0:T(8,128)S(1)}, u32[]{:S(2)}, u32[]{:S(2)}) %collective-permute-start.17) | collective-permute-done | bytes 376864 | tf_op jit(solution)/shard_map/ppermute | solution.py:314
  165.3 1.4 fusion.7
  166.6 23.5 %shard_map.59 = (f32[46,80,128]{2,1,0:T(8,128)}, f32[7,80,128]{2,1,0:T(8,128)}, f32[7,80,128]{2,1,0:T(8,128)}) custom-call(s32[4]{0:T(128)} %fusion.4.refs_0_.offsets_ref, bf16[46,80,128]{2,1,0:T(8,128)(2,1)} %get-tuple-element.69.ext_ref, bf16[384,512]{1,0:T(8,128)(2,1)} %get-tuple-element.43.plane_ref.fplane_ref, ...), custom_call_target="tpu_custom_call" | custom-call | flops 9059696640 | bytes 11526160 | tf_op jit(solution)/shard_map/pallas_call | solution.py:294
  190.1 1.9 collective-permute-start.18
  192.1 3.4 %collective-permute-start.19 = (f32[7,80,128]{2,1,0:T(8,128)}, f32[7,80,128]{2,1,0:T(8,128)S(1)}, u32[]{:S(2)}, u32[]{:S(2)}) collective-permute-start(f32[7,80,128]{2,1,0:T(8,128)} %get-tuple-element.62), channel_id=1, source_target_pairs={{1,0},{2,1},{3,2},{4,3},{5,4},{6,5},{7,6},{8,7},{9,8},{10,9},{11,1... | collective-permute-start | bytes 860168 | tf_op jit(solution)/shard_map/ppermute | solution.py:314
  195.4 2.6 %collective-permute-done.18 = f32[7,80,128]{2,1,0:T(8,128)S(1)} collective-permute-done((f32[7,80,128]{2,1,0:T(8,128)}, f32[7,80,128]{2,1,0:T(8,128)S(1)}, u32[]{:S(2)}, u32[]{:S(2)}) %collective-permute-start.18) | collective-permute-done | bytes 286752 | tf_op jit(solution)/shard_map/ppermute | solution.py:313
  198.0 7.4 %collective-permute-done.19 = f32[7,80,128]{2,1,0:T(8,128)S(1)} collective-permute-done((f32[7,80,128]{2,1,0:T(8,128)}, f32[7,80,128]{2,1,0:T(8,128)S(1)}, u32[]{:S(2)}, u32[]{:S(2)}) %collective-permute-start.19) | collective-permute-done | bytes 286752 | tf_op jit(solution)/shard_map/ppermute | solution.py:314
  205.4 1.4 pad_add_fusion.1
  206.8 2.9 %collective-permute-start.20 = (f32[32,8,128]{2,1,0:T(8,128)S(1)}, f32[32,8,128]{2,1,0:T(8,128)S(1)}, u32[]{:S(2)}, u32[]{:S(2)}) collective-permute-start(f32[32,8,128]{2,1,0:T(8,128)S(1)} %get-tuple-element.80), channel_id=1, source_target_pairs={{0,32},{32,64},{64,96},{1,33},{33,65},{65,97},{2,34},{34,66},{66,9... | collective-permute-start | bytes 393224 | tf_op jit(solution)/shard_map/ppermute | solution.py:313
  209.8 1.9 collective-permute-start.21
  211.7 4.3 %collective-permute-done.21 = f32[32,8,128]{2,1,0:T(8,128)S(1)} collective-permute-done((f32[32,8,128]{2,1,0:T(8,128)S(1)}, f32[32,8,128]{2,1,0:T(8,128)S(1)}, u32[]{:S(2)}, u32[]{:S(2)}) %collective-permute-start.21) | collective-permute-done | bytes 131104 | tf_op jit(solution)/shard_map/ppermute | solution.py:314
  216.6 1.0 constant_dynamic-update-slice_fusion.3
  217.9 23.3 %collective-permute-done.23 = f32[32,64,128]{2,1,0:T(8,128)S(1)} collective-permute-done((f32[32,64,128]{2,1,0:T(8,128)S(1)}, f32[32,64,128]{2,1,0:T(8,128)S(1)}, u32[]{:S(2)}, u32[]{:S(2)}) %collective-permute-start.23) | collective-permute-done | bytes 1048608 | tf_op jit(solution)/shard_map/ppermute | solution.py:308
  241.4 2.5 %collective-permute-done.24 = f32[32,64,128]{2,1,0:T(8,128)S(1)} collective-permute-done((f32[32,64,128]{2,1,0:T(8,128)S(1)}, f32[32,64,128]{2,1,0:T(8,128)S(1)}, u32[]{:S(2)}, u32[]{:S(2)}) %collective-permute-start.24) | collective-permute-done | bytes 1048608 | tf_op jit(solution)/shard_map/ppermute | solution.py:308
  243.9 1.1 constant_dynamic-update-slice_fusion
  (62 shorter events, 3.5 us)
Async XLA Ops:
  0.0 2.8 %copy-start.11 = (s32[4,1]{0,1:T(1,128)S(1)}, s32[4,1]{0,1:T(1,128)}, u32[]{:S(2)}) copy-start(s32[4,1]{0,1:T(1,128)} %param.9) | copy-start | bytes 52
  0.0 9.8 %copy-start.10 = (f32[1,3,3,15]{3,0,2,1:T(1,128)S(1)}, f32[1,3,3,15]{3,0,2,1:T(1,128)}, u32[]{:S(2)}) copy-start(f32[1,3,3,15]{3,0,2,1:T(1,128)} %param.7) | copy-start | bytes 1624
  2.8 34.3 %copy-start.1 = (bf16[32,64,128]{2,1,0:T(8,128)(2,1)}, bf16[32,64,128]{2,1,0:T(8,128)(2,1)S(1)}, u32[]{:S(2)}) copy-start(bf16[32,64,128]{2,1,0:T(8,128)(2,1)S(1)} %get-tuple-element.51.refs_2_.refs_0_) | copy-start | bytes 1572868
  2.8 12.1 %collective-permute-start.5 = (f32[4]{0:T(128)S(1)}, f32[4]{0:T(128)S(1)}, u32[]{:S(2)}, u32[]{:S(2)}) collective-permute-start(f32[4]{0:T(128)S(1)} %get-tuple-element.93), channel_id=1, source_target_pairs={{0,1},{1,2},{2,3},{3,4},{4,5},{5,6},{6,7},{7,8},{8,9},{9,10},{10,1... | collective-permute-start | bytes 56 | tf_op jit(solution)/shard_map/ppermute | solution.py:313
  7.9 10.0 %collective-permute-start.6 = (f32[4]{0:T(128)S(1)}, f32[4]{0:T(128)S(1)}, u32[]{:S(2)}, u32[]{:S(2)}) collective-permute-start(f32[4]{0:T(128)S(1)} %get-tuple-element.93), channel_id=1, source_target_pairs={{1,0},{2,1},{3,2},{4,3},{5,4},{6,5},{7,6},{8,7},{9,8},{10,9},{11,1... | collective-permute-start | bytes 56 | tf_op jit(solution)/shard_map/ppermute | solution.py:314
  10.7 10.2 %collective-permute-start.2 = (f32[1,136]{1,0:T(1,128)S(1)}, f32[1,136]{1,0:T(1,128)S(1)}, u32[]{:S(2)}, u32[]{:S(2)}) collective-permute-start(f32[1,136]{1,0:T(1,128)S(1)} %bitcast.18), channel_id=1, source_target_pairs={{0,32},{32,0},{64,96},{96,64},{1,33},{33,1},{65,97},{97,65},{2,34}... | collective-permute-start | bytes 1640 | tf_op jit(solution)/shard_map/ppermute | solution.py:308
  11.7 10.6 %collective-permute-start.3 = (f32[1,136]{1,0:T(1,128)S(1)}, f32[1,136]{1,0:T(1,128)S(1)}, u32[]{:S(2)}, u32[]{:S(2)}) collective-permute-start(f32[1,136]{1,0:T(1,128)S(1)} %bitcast.19), channel_id=1, source_target_pairs={{0,64},{32,96},{64,0},{96,32},{1,65},{33,97},{65,1},{97,33},{2,66}... | collective-permute-start | bytes 1640 | tf_op jit(solution)/shard_map/ppermute | solution.py:308
  12.4 14.7 %collective-permute-start.4 = (f32[1,136]{1,0:T(1,128)S(1)}, f32[1,136]{1,0:T(1,128)S(1)}, u32[]{:S(2)}, u32[]{:S(2)}) collective-permute-start(f32[1,136]{1,0:T(1,128)S(1)} %bitcast.20), channel_id=1, source_target_pairs={{0,96},{32,64},{64,32},{96,0},{1,97},{33,65},{65,33},{97,1},{2,98}... | collective-permute-start | bytes 1640 | tf_op jit(solution)/shard_map/ppermute | solution.py:308
  15.0 24.6 %collective-permute-start.12 = (bf16[32,64,128]{2,1,0:T(8,128)(2,1)S(1)}, bf16[32,64,128]{2,1,0:T(8,128)(2,1)S(1)}, u32[]{:S(2)}, u32[]{:S(2)}) collective-permute-start(bf16[32,64,128]{2,1,0:T(8,128)(2,1)S(1)} %get-tuple-element.52), channel_id=1, source_target_pairs={{0,32},{32,0},{64,96},{96,64},{1,33},{33,1},{65,97},{97,65},{2,34}... | collective-permute-start | bytes 1572872 | tf_op jit(solution)/shard_map/ppermute | solution.py:308
  17.9 22.8 %collective-permute-start.9 = (bf16[32,64,128]{2,1,0:T(8,128)(2,1)}, bf16[32,64,128]{2,1,0:T(8,128)(2,1)S(1)}, u32[]{:S(2)}, u32[]{:S(2)}) collective-permute-start(bf16[32,64,128]{2,1,0:T(8,128)(2,1)} %get-tuple-element.47), channel_id=1, source_target_pairs={{0,96},{32,64},{64,32},{96,0},{1,97},{33,65},{65,33},{97,1},{2,98}... | collective-permute-start | bytes 1572872 | tf_op jit(solution)/shard_map/ppermute | solution.py:308
  20.9 63.0 %collective-permute-start.7 = (bf16[32,64,128]{2,1,0:T(8,128)(2,1)}, bf16[32,64,128]{2,1,0:T(8,128)(2,1)S(1)}, u32[]{:S(2)}, u32[]{:S(2)}) collective-permute-start(bf16[32,64,128]{2,1,0:T(8,128)(2,1)} %get-tuple-element.46), channel_id=1, source_target_pairs={{0,64},{32,96},{64,0},{96,32},{1,65},{33,97},{65,1},{97,33},{2,66}... | collective-permute-start | bytes 1572872 | tf_op jit(solution)/shard_map/ppermute | solution.py:308
  22.3 14.9 %collective-permute-start = (bf16[7,80,128]{2,1,0:T(8,128)(2,1)S(1)}, bf16[7,80,128]{2,1,0:T(8,128)(2,1)S(1)}, u32[]{:S(2)}, u32[]{:S(2)}) collective-permute-start(bf16[7,80,128]{2,1,0:T(8,128)(2,1)S(1)} %get-tuple-element.82), channel_id=1, source_target_pairs={{0,1},{1,2},{2,3},{3,4},{4,5},{5,6},{6,7},{7,8},{8,9},{9,10},{10,1... | collective-permute-start | bytes 430088 | tf_op jit(solution)/shard_map/ppermute | solution.py:313
  27.2 12.3 %collective-permute-start.1 = (bf16[7,80,128]{2,1,0:T(8,128)(2,1)S(1)}, bf16[7,80,128]{2,1,0:T(8,128)(2,1)S(1)}, u32[]{:S(2)}, u32[]{:S(2)}) collective-permute-start(bf16[7,80,128]{2,1,0:T(8,128)(2,1)S(1)} %get-tuple-element.81), channel_id=1, source_target_pairs={{1,0},{2,1},{3,2},{4,3},{5,4},{6,5},{7,6},{8,7},{9,8},{10,9},{11,1... | collective-permute-start | bytes 430088 | tf_op jit(solution)/shard_map/ppermute | solution.py:314
  29.7 6.7 %copy-start.9 = (f32[4,136]{1,0:T(4,128)S(1)}, f32[4,136]{1,0:T(4,128)}, u32[]{:S(2)}) copy-start(f32[4,136]{1,0:T(4,128)} %pad_maximum_fusion.1.small_ref) | copy-start | bytes 6532
  37.1 59.3 %collective-permute-start.11 = (bf16[32,64,128]{2,1,0:T(8,128)(2,1)S(1)}, bf16[32,64,128]{2,1,0:T(8,128)(2,1)S(1)}, u32[]{:S(2)}, u32[]{:S(2)}) collective-permute-start(bf16[32,64,128]{2,1,0:T(8,128)(2,1)S(1)} %get-tuple-element.51.refs_2_.refs_0_), channel_id=1, source_target_pairs={{1,0},{2,1},{3,2},{4,3},{5,4},{6,5},{7,6},{8,7},{9,8},{10,9},{11,1... | collective-permute-start | bytes 1572872 | tf_op jit(solution)/shard_map/ppermute | solution.py:337
  39.5 56.9 %copy-start.2 = (bf16[32,64,128]{2,1,0:T(8,128)(2,1)}, bf16[32,64,128]{2,1,0:T(8,128)(2,1)S(1)}, u32[]{:S(2)}) copy-start(bf16[32,64,128]{2,1,0:T(8,128)(2,1)S(1)} %collective-permute-done.12.refs_4_.refs_2_) | copy-start | bytes 1572868
  39.5 57.0 %collective-permute-start.13 = (bf16[32,64,128]{2,1,0:T(8,128)(2,1)S(1)}, bf16[32,64,128]{2,1,0:T(8,128)(2,1)S(1)}, u32[]{:S(2)}, u32[]{:S(2)}) collective-permute-start(bf16[32,64,128]{2,1,0:T(8,128)(2,1)S(1)} %collective-permute-done.12.refs_4_.refs_2_), channel_id=1, source_target_pairs={{1,0},{2,1},{3,2},{4,3},{5,4},{6,5},{7,6},{8,7},{9,8},{10,9},{11,1... | collective-permute-start | bytes 1572872 | tf_op jit(solution)/shard_map/ppermute | solution.py:337
  40.7 55.7 %copy-start.3 = (bf16[32,64,128]{2,1,0:T(8,128)(2,1)}, bf16[32,64,128]{2,1,0:T(8,128)(2,1)S(1)}, u32[]{:S(2)}) copy-start(bf16[32,64,128]{2,1,0:T(8,128)(2,1)S(1)} %collective-permute-done.9.refs_4_.refs_6_) | copy-start | bytes 1572868
  40.7 67.0 %collective-permute-start.10 = (bf16[32,64,128]{2,1,0:T(8,128)(2,1)S(1)}, bf16[32,64,128]{2,1,0:T(8,128)(2,1)S(1)}, u32[]{:S(2)}, u32[]{:S(2)}) collective-permute-start(bf16[32,64,128]{2,1,0:T(8,128)(2,1)S(1)} %collective-permute-done.9.refs_4_.refs_6_), channel_id=1, source_target_pairs={{1,0},{2,1},{3,2},{4,3},{5,4},{6,5},{7,6},{8,7},{9,8},{10,9},{11,1... | collective-permute-start | bytes 1572872 | tf_op jit(solution)/shard_map/ppermute | solution.py:337
  83.9 12.6 %copy-start.4 = (bf16[32,64,128]{2,1,0:T(8,128)(2,1)}, bf16[32,64,128]{2,1,0:T(8,128)(2,1)S(1)}, u32[]{:S(2)}) copy-start(bf16[32,64,128]{2,1,0:T(8,128)(2,1)S(1)} %collective-permute-done.7.refs_2_.refs_4_) | copy-start | bytes 1572868
  83.9 23.8 %collective-permute-start.8 = (bf16[32,64,128]{2,1,0:T(8,128)(2,1)S(1)}, bf16[32,64,128]{2,1,0:T(8,128)(2,1)S(1)}, u32[]{:S(2)}, u32[]{:S(2)}) collective-permute-start(bf16[32,64,128]{2,1,0:T(8,128)(2,1)S(1)} %collective-permute-done.7.refs_2_.refs_4_), channel_id=1, source_target_pairs={{1,0},{2,1},{3,2},{4,3},{5,4},{6,5},{7,6},{8,7},{9,8},{10,9},{11,1... | collective-permute-start | bytes 1572872 | tf_op jit(solution)/shard_map/ppermute | solution.py:337
  96.5 0.8 copy-start.5
  96.5 0.9 copy-start.6
  107.7 0.8 copy-start.7
  107.7 1.0 copy-start.8
  119.8 20.9 %collective-permute-start.14 = (f32[14,80,128]{2,1,0:T(8,128)}, f32[14,80,128]{2,1,0:T(8,128)S(1)}, u32[]{:S(2)}, u32[]{:S(2)}) collective-permute-start(f32[14,80,128]{2,1,0:T(8,128)} %get-tuple-element.54), channel_id=1, source_target_pairs={{0,1},{1,2},{2,3},{3,4},{4,5},{5,6},{6,7},{7,8},{8,9},{9,10},{10,1... | collective-permute-start | bytes 1720328 | tf_op jit(solution)/shard_map/ppermute | solution.py:313
  128.8 21.4 %collective-permute-start.15 = (f32[14,80,128]{2,1,0:T(8,128)}, f32[14,80,128]{2,1,0:T(8,128)S(1)}, u32[]{:S(2)}, u32[]{:S(2)}) collective-permute-start(f32[14,80,128]{2,1,0:T(8,128)} %get-tuple-element.55), channel_id=1, source_target_pairs={{1,0},{2,1},{3,2},{4,3},{5,4},{6,5},{7,6},{8,7},{9,8},{10,9},{11,1... | collective-permute-start | bytes 1720328 | tf_op jit(solution)/shard_map/ppermute | solution.py:314
  151.9 9.3 %collective-permute-start.16 = (f32[46,16,128]{2,1,0:T(8,128)S(1)}, f32[46,16,128]{2,1,0:T(8,128)S(1)}, u32[]{:S(2)}, u32[]{:S(2)}) collective-permute-start(f32[46,16,128]{2,1,0:T(8,128)S(1)} %get-tuple-element.78), channel_id=1, source_target_pairs={{0,32},{32,64},{64,96},{1,33},{33,65},{65,97},{2,34},{34,66},{66,9... | collective-permute-start | bytes 1130504 | tf_op jit(solution)/shard_map/ppermute | solution.py:313
  156.4 8.9 %collective-permute-start.17 = (f32[46,16,128]{2,1,0:T(8,128)S(1)}, f32[46,16,128]{2,1,0:T(8,128)S(1)}, u32[]{:S(2)}, u32[]{:S(2)}) collective-permute-start(f32[46,16,128]{2,1,0:T(8,128)S(1)} %get-tuple-element.77), channel_id=1, source_target_pairs={{32,0},{64,32},{96,64},{33,1},{65,33},{97,65},{34,2},{66,34},{98,6... | collective-permute-start | bytes 1130504 | tf_op jit(solution)/shard_map/ppermute | solution.py:314
  190.1 7.9 %collective-permute-start.18 = (f32[7,80,128]{2,1,0:T(8,128)}, f32[7,80,128]{2,1,0:T(8,128)S(1)}, u32[]{:S(2)}, u32[]{:S(2)}) collective-permute-start(f32[7,80,128]{2,1,0:T(8,128)} %get-tuple-element.61), channel_id=1, source_target_pairs={{0,1},{1,2},{2,3},{3,4},{4,5},{5,6},{6,7},{7,8},{8,9},{9,10},{10,1... | collective-permute-start | bytes 860168 | tf_op jit(solution)/shard_map/ppermute | solution.py:313
  192.1 13.3 %collective-permute-start.19 = (f32[7,80,128]{2,1,0:T(8,128)}, f32[7,80,128]{2,1,0:T(8,128)S(1)}, u32[]{:S(2)}, u32[]{:S(2)}) collective-permute-start(f32[7,80,128]{2,1,0:T(8,128)} %get-tuple-element.62), channel_id=1, source_target_pairs={{1,0},{2,1},{3,2},{4,3},{5,4},{6,5},{7,6},{8,7},{9,8},{10,9},{11,1... | collective-permute-start | bytes 860168 | tf_op jit(solution)/shard_map/ppermute | solution.py:314
  206.8 4.9 %collective-permute-start.20 = (f32[32,8,128]{2,1,0:T(8,128)S(1)}, f32[32,8,128]{2,1,0:T(8,128)S(1)}, u32[]{:S(2)}, u32[]{:S(2)}) collective-permute-start(f32[32,8,128]{2,1,0:T(8,128)S(1)} %get-tuple-element.80), channel_id=1, source_target_pairs={{0,32},{32,64},{64,96},{1,33},{33,65},{65,97},{2,34},{34,66},{66,9... | collective-permute-start | bytes 393224 | tf_op jit(solution)/shard_map/ppermute | solution.py:313
  209.8 6.3 %collective-permute-start.21 = (f32[32,8,128]{2,1,0:T(8,128)S(1)}, f32[32,8,128]{2,1,0:T(8,128)S(1)}, u32[]{:S(2)}, u32[]{:S(2)}) collective-permute-start(f32[32,8,128]{2,1,0:T(8,128)S(1)} %get-tuple-element.79), channel_id=1, source_target_pairs={{32,0},{64,32},{96,64},{33,1},{65,33},{97,65},{34,2},{66,34},{98,6... | collective-permute-start | bytes 393224 | tf_op jit(solution)/shard_map/ppermute | solution.py:314
  217.5 23.7 %collective-permute-start.23 = (f32[32,64,128]{2,1,0:T(8,128)S(1)}, f32[32,64,128]{2,1,0:T(8,128)S(1)}, u32[]{:S(2)}, u32[]{:S(2)}) collective-permute-start(f32[32,64,128]{2,1,0:T(8,128)S(1)} %get-tuple-element.68), channel_id=1, source_target_pairs={{0,64},{32,96},{64,0},{96,32},{1,65},{33,97},{65,1},{97,33},{2,66}... | collective-permute-start | bytes 3145736 | tf_op jit(solution)/shard_map/ppermute | solution.py:308
  217.6 23.6 %collective-permute-start.22 = (f32[32,64,128]{2,1,0:T(8,128)S(1)}, f32[32,64,128]{2,1,0:T(8,128)S(1)}, u32[]{:S(2)}, u32[]{:S(2)}) collective-permute-start(f32[32,64,128]{2,1,0:T(8,128)S(1)} %get-tuple-element.68), channel_id=1, source_target_pairs={{0,32},{32,0},{64,96},{96,64},{1,33},{33,1},{65,97},{97,65},{2,34}... | collective-permute-start | bytes 3145736 | tf_op jit(solution)/shard_map/ppermute | solution.py:308
  241.2 2.7 %collective-permute-start.24 = (f32[32,64,128]{2,1,0:T(8,128)S(1)}, f32[32,64,128]{2,1,0:T(8,128)S(1)}, u32[]{:S(2)}, u32[]{:S(2)}) collective-permute-start(f32[32,64,128]{2,1,0:T(8,128)S(1)} %collective-permute-done.23), channel_id=1, source_target_pairs={{0,32},{32,0},{64,96},{96,64},{1,33},{33,1},{65,97},{97,65},{2,34}... | collective-permute-start | bytes 3145736 | tf_op jit(solution)/shard_map/ppermute | solution.py:308
  241.4 2.5 %copy-start = (f32[32,256,128]{2,1,0:T(8,128)}, f32[32,256,128]{2,1,0:T(8,128)S(1)}, u32[]{:S(2)}) copy-start(f32[32,256,128]{2,1,0:T(8,128)S(1)} %constant_dynamic-update-slice_fusion.1) | copy-start | bytes 12582916

commit v3 on v2

--- a/solution.py
+++ b/solution.py
@@ -36,9 +36,14 @@
     return high, (value - high.astype(jnp.float32)).astype(jnp.bfloat16)
 
 
-def prepare_kernel(small_ref, weights_ref, fplane_ref, aplane_ref, fline_ref, aline_ref):
+def prepare_kernel(first_ref, small_ref, covers_ref, fplane_ref, aplane_ref, fline_ref, aline_ref):
+    me = first_ref[0]
+
     def tap(base, pair, t):
         return small_ref[pair // RANK, base + (pair % RANK) * TAPS + t]
+
+    def weight(side, pair):
+        return covers_ref[side, me ^ (pair // RANK)]
 
     lane = iota((YB, 128), 1)
     t_y = (lane & (YW - 1)) - iota((YB, 128), 0) - 1
@@ -67,8 +72,7 @@
         for t in range(TAPS):
             y = jnp.where(t_y == t, jnp.where(first, tap(KY, pairs[0], t), tap(KY, pairs[1], t)), y)
         sided = [
-            y * jnp.where(first, weights_ref[side, pairs[0] // RANK], weights_ref[side, pairs[1] // RANK])
-            for side in range(3)
+            y * jnp.where(first, weight(side, pairs[0]), weight(side, pairs[1])) for side in range(3)
         ]
         for xw in range(AW):
             x = jnp.zeros((YW, 128), jnp.float32)
@@ -178,6 +182,10 @@
     down_ref[...] = out_ref[EX - rows :]
 
 
+def tile_copy(tile_hbm, rows_ref, part, sem):
+    return pltpu.make_async_copy(tile_hbm.at[pl.ds(0, BX)], rows_ref.at[pl.ds(part * BX, BX)], sem)
+
+
 def blur_kernel(ext_ref, plane_ref, line_hbm, first_ref, last_ref, mid_ref, line_ref, sem):
     copy = pltpu.make_async_copy(line_hbm, line_ref, sem.at[0])
     copy.start()
@@ -206,11 +214,7 @@
     copies = [
         [pltpu.make_async_copy(blurred_hbm.at[slot], blurred_ref.at[slot], sems.at[slot])]
         + [
-            pltpu.make_async_copy(
-                tiles_hbm[2 * slot + part],
-                tiles_ref.at[slot, pl.ds(part * BX, BX)],
-                sems.at[HALF + 2 * slot + part],
-            )
+            tile_copy(tiles_hbm[2 * slot + part], tiles_ref.at[slot], part, sems.at[HALF + 2 * slot + part])
             for part in range(2)
         ]
         for slot in range(HALF)
@@ -249,9 +253,7 @@
     ]
     plane_copy = pltpu.make_async_copy(aplane_hbm, aplane_ref, sems.at[2])
     tile_copies = [
-        pltpu.make_async_copy(
-            tiles_hbm[2 * view + part], tiles_ref.at[view, pl.ds(part * BX, BX)], sems.at[3 + 2 * view + part]
-        )
+        tile_copy(tiles_hbm[2 * view + part], tiles_ref.at[view], part, sems.at[3 + 2 * view + part])
         for view in range(VIEWS)
         for part in range(2)
     ]
@@ -304,14 +306,33 @@
     )(*args)
 
 
+def place(quarter, brick, bricks):
+    return (quarter ^ (2 if brick >= bricks // 2 else 0)) * bricks + brick
+
+
+def send(value, pairs):
+    bricks = lax.axis_size("brick")
+    perm = [(place(*a, bricks), place(*b, bricks)) for a, b in pairs]
+    return lax.ppermute(value, ("view", "brick"), perm)
+
+
 def to_xor(value, by):
     return lax.ppermute(value, "view", [(i, i ^ by) for i in range(VIEWS)])
 
 
+def from_next_brick(value):
+    bricks = lax.axis_size("brick")
+    return send(value, [((q, (b + 1) % bricks), (q, b)) for b in range(bricks) for q in range(VIEWS)])
+
+
 def exchange(axis, to_previous, to_next):
-    up = [(i, i + 1) for i in range(lax.axis_size(axis) - 1)]
-    from_previous = lax.ppermute(to_next, axis, up)
-    from_next = lax.ppermute(to_previous, axis, [(j, i) for i, j in up])
+    bricks = lax.axis_size("brick")
+    if axis == "brick":
+        up = [((q, b), (q, b + 1)) for b in range(bricks - 1) for q in range(VIEWS)]
+    else:
+        up = [((q, b), (q + 1, b)) for b in range(bricks) for q in range(VIEWS - 1)]
+    from_previous = send(to_next, up)
+    from_next = send(to_previous, [(j, i) for i, j in up])
     return lax.optimization_barrier((from_previous, from_next))
 
 
@@ -323,41 +344,54 @@
     return value + jnp.pad(from_previous, pads[0]) + jnp.pad(from_next, pads[1])
 
 
+def in_bf16(values):
+    rows = []
+    for _ in range(3):
+        rows.append(lax.reduce_precision(values, 8, 7))
+        values = values - rows[-1]
+    return jnp.stack(rows).astype(BF16)
+
+
 def shards(start_estimate, observed, psf_taps, offsets, coverage):
     me = lax.axis_index("view")
     bricks = lax.axis_size("brick")
-
-    pieces = [lax.dynamic_slice_in_dim(observed[0], QY * (me ^ by), QY, 1) for by in range(VIEWS)]
-    pieces, start_estimate, psf_taps, coverage = lax.optimization_barrier(
-        (pieces, start_estimate, psf_taps, coverage)
-    )
-    tiles = []
-    for by, piece in enumerate(pieces):
-        piece = to_xor(piece, by) if by else piece
-        tiles.append((piece, lax.ppermute(piece, "brick", [((i + 1) % bricks, i) for i in range(bricks)])))
-
-    small = jnp.concatenate([psf_taps.reshape(-1), offsets.astype(F32)])[None]
-    smalls = jnp.concatenate([small] + [to_xor(small, by) for by in range(1, VIEWS)], axis=0)
+    quarter = me ^ (2 * (lax.axis_index("brick") // (bricks // 2)))
+
+    small = jnp.concatenate([psf_taps.reshape(-1), offsets.astype(F32)])
+    wide = -(-small.shape[0] // NZ)
+    row = in_bf16(jnp.pad(small, (0, wide * NZ - small.shape[0]))).reshape(1, 3 * wide, NZ)
+    row = jnp.pad(row, ((0, 0), (0, QY - 3 * wide), (0, 0)))
+    pieces = [lax.dynamic_slice_in_dim(observed[0], QY * (quarter ^ by), QY, 1) for by in range(VIEWS)]
+    pieces = [jnp.concatenate([piece, row], axis=0) for piece in pieces]
+    start_estimate, pieces = lax.optimization_barrier((start_estimate, pieces))
+    here = [to_xor(piece, by) if by else piece for by, piece in enumerate(pieces)]
+    beyond = [from_next_brick(tile) for tile in here]
+    across = lax.rem(lax.axis_index("brick") + 1, bricks // 2) == 0
+    here = [jnp.where(across, here[by ^ 2], here[by]) for by in range(VIEWS)]
+    first = jnp.where(across, me ^ 2, me)
+    tiles = list(zip(here, beyond))
+    smalls = jnp.concatenate([tile[BX:] for tile in here], axis=0)[:, : 3 * wide].astype(F32).reshape(VIEWS, 3, wide * NZ)
+    smalls = (smalls[:, 2] + smalls[:, 1]) + smalls[:, 0]
     shifts = smalls[:, OFFSET].astype(jnp.int32)
-    covered = coverage[:, 0].astype(F32)
-    before, after = exchange("brick", covered, covered)
-    covers = jnp.stack([before, covered, after])
-    weights = jnp.concatenate(
-        [lax.dynamic_slice_in_dim(covers, me ^ by, 1, 1) for by in range(VIEWS)], axis=1
-    )
+
+    padded = jnp.pad(start_estimate, ((0, 0), (HY, HY), (0, 0)))
+    estimate = lax.dynamic_slice_in_dim(padded, QY * quarter, EY, 1)
+    edge = estimate.astype(BF16)
+    covered = jnp.broadcast_to(coverage.reshape(1, VIEWS, 1).astype(BF16), (1, VIEWS, NZ))
+    covered = jnp.pad(covered, ((0, 0), (0, EY - VIEWS), (0, 0)))
+    before, after = exchange(
+        "brick",
+        jnp.concatenate([edge[:HX], covered], axis=0),
+        jnp.concatenate([edge[BX - HX :], covered], axis=0),
+    )
+    covers = jnp.stack([rows[HX, :VIEWS, 0] for rows in (before, jnp.pad(covered, ((HX, 0), (0, 0), (0, 0))), after)])
+    covers = covers.astype(F32)
     counts = jnp.maximum(jnp.sum(covers, axis=1), 1.0)
-    row_counts = jnp.concatenate(
-        [jnp.full((HX,), counts[0]), jnp.full((BX,), counts[1]), jnp.full((HX,), counts[2])]
-    )[:, None, None]
+    row_counts = jnp.repeat(counts, jnp.array([HX, BX, HX]), total_repeat_length=EX)[:, None, None]
+    estimate = jnp.concatenate([before[:HX].astype(F32), estimate, after[:HX].astype(F32)], axis=0)
     fplane, aplane, fline, aline = call(
-        prepare_kernel, [FPLANE, APLANE, FLINE, ALINE], [SMEM, SMEM], [], 10**9, (smalls, weights)
-    )
-
-    padded = jnp.pad(start_estimate, ((0, 0), (HY, HY), (0, 0)))
-    estimate = lax.dynamic_slice_in_dim(padded, QY * me, EY, 1)
-    edge = estimate.astype(BF16)
-    before, after = exchange("brick", edge[:HX], edge[BX - HX :])
-    estimate = jnp.concatenate([before.astype(F32), estimate, after.astype(F32)], axis=0)
+        prepare_kernel, [FPLANE, APLANE, FLINE, ALINE], [SMEM] * 3, [], 10**9, (first[None], smalls, covers)
+    )
 
     half = ((HALF, BX, QY, NZ), F32)
     blurred = call(
@@ -406,7 +440,7 @@
     quarters = [estimate, to_xor(estimate, 1), across, to_xor(across, 1)]
     result = jnp.zeros(start_estimate.shape, F32)
     for by in range(VIEWS):
-        result = lax.dynamic_update_slice_in_dim(result, quarters[by], QY * (me ^ by), 1)
+        result = lax.dynamic_update_slice_in_dim(result, quarters[by], QY * (quarter ^ by), 1)
     return result
 
 

time: 246 us -> 218 us (0.89)
  waiting for transfers between devices: 112 us -> 84.8 us
  other arithmetic: 10.3 us -> 17.7 us
  starting transfers between devices: 48.1 us -> 42.6 us
    ppermute x9 -> x6, waiting for transfers between devices: 69 us -> 36.5 us  [to_xor(): return lax.ppermute(value, 'view', [(i, i ^ by) for i in range(VIEWS)])]
    ppermute x16 -> x14, waiting for transfers between devices: 43 us -> 48.2 us  [send(): return lax.ppermute(value, ('view', 'brick'), perm)]
    ppermute x9 -> x6, starting transfers between devices: 6.71 us -> 2.96 us  [to_xor(): return lax.ppermute(value, 'view', [(i, i ^ by) for i in range(VIEWS)])]
    select_n x0 -> x2, other arithmetic: none -> 2.6 us  [shards(): here = [jnp.where(across, here[by ^ 2], here[by]) for by in range(VIEWS)]]
    ppermute x16 -> x14, starting transfers between devices: 41.4 us -> 39.6 us  [send(): return lax.ppermute(value, ('view', 'brick'), perm)]
  transfers between devices with their start and end apart: 25 -> 20, of which waited for: 11 -> 11; matrix products, arithmetic and copies ran while one was open for 3% -> 5% of each run, Pallas kernels for 12% -> 13%
where the time goes in v3:
time: 218 us
  waiting for transfers between devices  84.8 us (39%)
  Pallas kernels  64 us (29%)
  starting transfers between devices  42.6 us (20%)
  other arithmetic  17.7 us (8%)
  local copies, waits for them, and re-layouts  7.61 us (3%)
    pallas_call x5, Pallas kernels, call(): pl.pallas_call(kernel, out_shape=[jax.ShapeDtypeStruct(*out) for out in o...  64 us
    ppermute x14, waiting for transfers between devices, send(): return lax.ppermute(value, ('view', 'brick'), perm)  48.2 us
    ppermute x14, starting transfers between devices, send(): return lax.ppermute(value, ('view', 'brick'), perm)  39.6 us
    ppermute x6, waiting for transfers between devices, to_xor(): return lax.ppermute(value, 'view', [(i, i ^ by) for i in range(VIEWS)])  36.5 us
  transfers between devices with their start and end apart: 20, of which 11 were waited for; matrix products, arithmetic and copies ran while one was open for 5% of the time, Pallas kernels for 13%

profile of v3, /device:TPU:31, one launch (start us, length us, event | category | flops | bytes accessed | tf_op | source)
XLA Modules:
  0.0 217.7 jit_solution(3726374152763388652)
XLA Ops:
  0.0 0.7 reduce.2
  1.6 1.7 dynamic-slice_bitcast_fusion
  3.3 1.3 fusion.8
  4.6 1.5 fusion.17
  6.3 5.2 %collective-permute-start = (bf16[8,80,128]{2,1,0:T(8,128)(2,1)S(1)}, bf16[8,80,128]{2,1,0:T(8,128)(2,1)S(1)}, u32[]{:S(2)}, u32[]{:S(2)}) collective-permute-start(bf16[8,80,128]{2,1,0:T(8,128)(2,1)S(1)} %get-tuple-element.94), channel_id=1, source_target_pairs={{0,1},{32,33},{64,65},{96,97},{1,2},{33,34},{65,66},{97,98},{2,3},... | collective-permute-start | bytes 491528 | tf_op jit(solution)/shard_map/ppermute | solution.py:316
  11.6 1.9 collective-permute-start.1
  13.6 2.5 %collective-permute-start.3 = (bf16[33,64,128]{2,1,0:T(8,128)(2,1)}, bf16[33,64,128]{2,1,0:T(8,128)(2,1)}, u32[]{:S(2)}, u32[]{:S(2)}) collective-permute-start(bf16[33,64,128]{2,1,0:T(8,128)(2,1)} %get-tuple-element.49), channel_id=1, source_target_pairs={{0,96},{32,64},{64,32},{96,0},{1,97},{33,65},{65,33},{97,1},{2,98}... | collective-permute-start | bytes 1622024 | tf_op jit(solution)/shard_map/ppermute | solution.py:320
  16.1 7.7 %collective-permute-done.1 = bf16[8,80,128]{2,1,0:T(8,128)(2,1)} collective-permute-done((bf16[8,80,128]{2,1,0:T(8,128)(2,1)S(1)}, bf16[8,80,128]{2,1,0:T(8,128)(2,1)}, u32[]{:S(2)}, u32[]{:S(2)}) %collective-permute-start.1) | collective-permute-done | bytes 163872 | tf_op jit(solution)/shard_map/ppermute | solution.py:316
  23.8 0.9 slice_convert_fusion
  24.7 0.7 slice_reduce_fusion
  26.1 1.1 fusion.ext_ref
  27.1 1.3 broadcast_select_fusion.3
  28.5 10.7 %collective-permute-done.3 = bf16[33,64,128]{2,1,0:T(8,128)(2,1)} collective-permute-done((bf16[33,64,128]{2,1,0:T(8,128)(2,1)}, bf16[33,64,128]{2,1,0:T(8,128)(2,1)}, u32[]{:S(2)}, u32[]{:S(2)}) %collective-permute-start.3) | collective-permute-done | bytes 540704 | tf_op jit(solution)/shard_map/ppermute | solution.py:320
  39.3 1.3 broadcast_select_fusion.2
  40.6 0.8 copy-done.4
  42.0 6.7 %shard_map.64 = (bf16[384,512]{1,0:T(8,128)(2,1)}, bf16[5,576,768]{2,1,0:T(8,128)(2,1)}, bf16[4,384,256]{2,1,0:T(8,128)(2,1)}, bf16[4,256,384]{2,1,0:T(8,128)(2,1)}) custom-call(s32[1]{0:T(128)} %bitcast.6.first_ref, f32[4,256]{1,0:T(4,128)} %fusion.10.small_ref, f32[3,4]{1,0:T(4,128)} %maximum_convert_fusion.covers_ref), custom_call_target="tpu_custom_call" | custom-call | flops 1000000000 | bytes 4148 | tf_op jit(solution)/shard_map/pallas_call | solution.py:296
  48.9 1.0 collective-permute-start.6
  49.9 0.7 fusion.11.refs_0_.offsets_ref
  50.6 12.3 %shard_map.65 = (f32[2,32,64,128]{3,2,1,0:T(8,128)}, f32[2,32,64,128]{3,2,1,0:T(8,128)}) custom-call(bf16[46,80,128]{2,1,0:T(8,128)(2,1)} %fusion.ext_ref, bf16[384,512]{1,0:T(8,128)(2,1)} %get-tuple-element.51.plane_ref.fplane_ref, bf16[4,384,256]{2,1,0:T(8,128)(2,1)} %get-tuple-element.52.line_hbm.fline_hbm), custom_call_target="tpu_custom_call" | custom-call | flops 4529848320 | bytes 2121728 | tf_op jit(solution)/shard_map/pallas_call | solution.py:296
  63.0 0.8 copy-done.5
  63.8 10.2 %shard_map.66.refs_8_ = f32[46,80,128]{2,1,0:T(8,128)} custom-call(s32[4]{0:T(128)} %fusion.11.refs_0_.offsets_ref, f32[2,32,64,128]{3,2,1,0:T(8,128)} %get-tuple-element.56.refs_1_, bf16[33,64,128]{2,1,0:T(8,128)(2,1)} %copy-done.1, bf16[33,64,128]{2,1,0:T(8,128)(2,1)} %collective-permute-done.7.refs_3_.refs_1_, bf16[33,64,128]{2,1,0:T(8,128)(2,1)} %copy-done.3, ...), custom_call_target="tpu_custom_call" | custom-call | flops 2264924160 | bytes 9469968 | tf_op jit(solution)/shard_map/pallas_call | solution.py:296
  74.1 10.5 %collective-permute-done.6.refs_5_.refs_7_ = bf16[33,64,128]{2,1,0:T(8,128)(2,1)S(1)} collective-permute-done((bf16[33,64,128]{2,1,0:T(8,128)(2,1)}, bf16[33,64,128]{2,1,0:T(8,128)(2,1)S(1)}, u32[]{:S(2)}, u32[]{:S(2)}) %collective-permute-start.6) | collective-permute-done | bytes 540704 | tf_op jit(solution)/shard_map/ppermute | solution.py:316
  84.6 0.8 copy-done.7
  85.4 11.1 %shard_map.67 = (f32[46,80,128]{2,1,0:T(8,128)}, f32[14,80,128]{2,1,0:T(8,128)}, f32[14,80,128]{2,1,0:T(8,128)}) custom-call(s32[4]{0:T(128)} %fusion.11.refs_0_.offsets_ref, f32[2,32,64,128]{3,2,1,0:T(8,128)} %get-tuple-element.53.refs_1_, bf16[33,64,128]{2,1,0:T(8,128)(2,1)} %copy-done.2, bf16[33,64,128]{2,1,0:T(8,128)(2,1)} %copy-done.6, ...), custom_call_target="tpu_custom_call" | custom-call | flops 2264924160 | bytes 11354128 | tf_op jit(solution)/shard_map/pallas_call | solution.py:296
  96.6 1.9 collective-permute-start.10
  98.5 8.8 %collective-permute-start.9 = (f32[14,80,128]{2,1,0:T(8,128)}, f32[14,80,128]{2,1,0:T(8,128)S(1)}, u32[]{:S(2)}, u32[]{:S(2)}) collective-permute-start(f32[14,80,128]{2,1,0:T(8,128)} %get-tuple-element.58), channel_id=1, source_target_pairs={{0,1},{32,33},{64,65},{96,97},{1,2},{33,34},{65,66},{97,98},{2,3},... | collective-permute-start | bytes 1720328 | tf_op jit(solution)/shard_map/ppermute | solution.py:316
  107.4 10.8 %collective-permute-done.10 = f32[14,80,128]{2,1,0:T(8,128)S(1)} collective-permute-done((f32[14,80,128]{2,1,0:T(8,128)}, f32[14,80,128]{2,1,0:T(8,128)S(1)}, u32[]{:S(2)}, u32[]{:S(2)}) %collective-permute-start.10) | collective-permute-done | bytes 573472 | tf_op jit(solution)/shard_map/ppermute | solution.py:316
  118.2 1.0 collective-permute-done.9
  119.2 1.7 pad_add_fusion
  121.0 1.9 collective-permute-start.11
  123.0 3.0 %collective-permute-start.12 = (f32[46,16,128]{2,1,0:T(8,128)S(1)}, f32[46,16,128]{2,1,0:T(8,128)S(1)}, u32[]{:S(2)}, u32[]{:S(2)}) collective-permute-start(f32[46,16,128]{2,1,0:T(8,128)S(1)} %get-tuple-element.83), channel_id=1, source_target_pairs={{32,0},{64,32},{96,64},{33,1},{65,33},{97,65},{34,2},{66,34},{98,6... | collective-permute-start | bytes 1130504 | tf_op jit(solution)/shard_map/ppermute | solution.py:316
  126.0 0.6 fusion.22
  126.7 1.9 select_select_fusion
  128.6 3.3 %collective-permute-done.12 = f32[46,16,128]{2,1,0:T(8,128)S(1)} collective-permute-done((f32[46,16,128]{2,1,0:T(8,128)S(1)}, f32[46,16,128]{2,1,0:T(8,128)S(1)}, u32[]{:S(2)}, u32[]{:S(2)}) %collective-permute-start.12) | collective-permute-done | bytes 376864 | tf_op jit(solution)/shard_map/ppermute | solution.py:316
  131.9 1.4 fusion.16
  133.2 23.5 %shard_map.68 = (f32[46,80,128]{2,1,0:T(8,128)}, f32[7,80,128]{2,1,0:T(8,128)}, f32[7,80,128]{2,1,0:T(8,128)}) custom-call(s32[4]{0:T(128)} %fusion.11.refs_0_.offsets_ref, bf16[46,80,128]{2,1,0:T(8,128)(2,1)} %get-tuple-element.73.ext_ref, bf16[384,512]{1,0:T(8,128)(2,1)} %get-tuple-element.51.plane_ref.fplane_ref, ...), custom_call_target="tpu_custom_call" | custom-call | flops 9059696640 | bytes 11657232 | tf_op jit(solution)/shard_map/pallas_call | solution.py:296
  156.7 9.4 %collective-permute-start.13 = (f32[7,80,128]{2,1,0:T(8,128)}, f32[7,80,128]{2,1,0:T(8,128)S(1)}, u32[]{:S(2)}, u32[]{:S(2)}) collective-permute-start(f32[7,80,128]{2,1,0:T(8,128)} %get-tuple-element.65), channel_id=1, source_target_pairs={{0,1},{32,33},{64,65},{96,97},{1,2},{33,34},{65,66},{97,98},{2,3},... | collective-permute-start | bytes 860168 | tf_op jit(solution)/shard_map/ppermute | solution.py:316
  166.2 1.9 collective-permute-start.14
  168.1 1.9 collective-permute-done.13
  170.0 9.1 %collective-permute-done.14 = f32[7,80,128]{2,1,0:T(8,128)S(1)} collective-permute-done((f32[7,80,128]{2,1,0:T(8,128)}, f32[7,80,128]{2,1,0:T(8,128)S(1)}, u32[]{:S(2)}, u32[]{:S(2)}) %collective-permute-start.14) | collective-permute-done | bytes 286752 | tf_op jit(solution)/shard_map/ppermute | solution.py:316
  179.2 1.4 pad_add_fusion.1
  180.7 1.9 collective-permute-start.15
  182.6 2.4 %collective-permute-start.16 = (f32[32,8,128]{2,1,0:T(8,128)S(1)}, f32[32,8,128]{2,1,0:T(8,128)S(1)}, u32[]{:S(2)}, u32[]{:S(2)}) collective-permute-start(f32[32,8,128]{2,1,0:T(8,128)S(1)} %get-tuple-element.85), channel_id=1, source_target_pairs={{32,0},{64,32},{96,64},{33,1},{65,33},{97,65},{34,2},{66,34},{98,6... | collective-permute-start | bytes 393224 | tf_op jit(solution)/shard_map/ppermute | solution.py:316
  185.0 3.9 %collective-permute-done.16 = f32[32,8,128]{2,1,0:T(8,128)S(1)} collective-permute-done((f32[32,8,128]{2,1,0:T(8,128)S(1)}, f32[32,8,128]{2,1,0:T(8,128)S(1)}, u32[]{:S(2)}, u32[]{:S(2)}) %collective-permute-start.16) | collective-permute-done | bytes 131104 | tf_op jit(solution)/shard_map/ppermute | solution.py:316
  189.3 0.9 constant_dynamic-update-slice_fusion.3
  190.7 23.3 %collective-permute-done.18 = f32[32,64,128]{2,1,0:T(8,128)S(1)} collective-permute-done((f32[32,64,128]{2,1,0:T(8,128)S(1)}, f32[32,64,128]{2,1,0:T(8,128)S(1)}, u32[]{:S(2)}, u32[]{:S(2)}) %collective-permute-start.18) | collective-permute-done | bytes 1048608 | tf_op jit(solution)/shard_map/ppermute | solution.py:320
  214.2 2.5 %collective-permute-done.19 = f32[32,64,128]{2,1,0:T(8,128)S(1)} collective-permute-done((f32[32,64,128]{2,1,0:T(8,128)S(1)}, f32[32,64,128]{2,1,0:T(8,128)S(1)}, u32[]{:S(2)}, u32[]{:S(2)}) %collective-permute-start.19) | collective-permute-done | bytes 1048608 | tf_op jit(solution)/shard_map/ppermute | solution.py:320
  216.6 1.1 constant_dynamic-update-slice_fusion.2
  (71 shorter events, 3.0 us)
Async XLA Ops:
  4.6 1.5 copy-start.13
  6.3 9.8 %collective-permute-start = (bf16[8,80,128]{2,1,0:T(8,128)(2,1)S(1)}, bf16[8,80,128]{2,1,0:T(8,128)(2,1)S(1)}, u32[]{:S(2)}, u32[]{:S(2)}) collective-permute-start(bf16[8,80,128]{2,1,0:T(8,128)(2,1)S(1)} %get-tuple-element.94), channel_id=1, source_target_pairs={{0,1},{32,33},{64,65},{96,97},{1,2},{33,34},{65,66},{97,98},{2,3},... | collective-permute-start | bytes 491528 | tf_op jit(solution)/shard_map/ppermute | solution.py:316
  11.6 12.2 %collective-permute-start.1 = (bf16[8,80,128]{2,1,0:T(8,128)(2,1)S(1)}, bf16[8,80,128]{2,1,0:T(8,128)(2,1)}, u32[]{:S(2)}, u32[]{:S(2)}) collective-permute-start(bf16[8,80,128]{2,1,0:T(8,128)(2,1)S(1)} %get-tuple-element.93), channel_id=1, source_target_pairs={{1,0},{33,32},{65,64},{97,96},{2,1},{34,33},{66,65},{98,97},{3,2},... | collective-permute-start | bytes 491528 | tf_op jit(solution)/shard_map/ppermute | solution.py:316
  13.5 13.7 %collective-permute-start.2 = (bf16[33,64,128]{2,1,0:T(8,128)(2,1)S(1)}, bf16[33,64,128]{2,1,0:T(8,128)(2,1)S(1)}, u32[]{:S(2)}, u32[]{:S(2)}) collective-permute-start(bf16[33,64,128]{2,1,0:T(8,128)(2,1)S(1)} %get-tuple-element.47), channel_id=1, source_target_pairs={{0,64},{32,96},{64,0},{96,32},{1,65},{33,97},{65,1},{97,33},{2,66}... | collective-permute-start | bytes 1622024 | tf_op jit(solution)/shard_map/ppermute | solution.py:320
  13.6 25.7 %collective-permute-start.3 = (bf16[33,64,128]{2,1,0:T(8,128)(2,1)}, bf16[33,64,128]{2,1,0:T(8,128)(2,1)}, u32[]{:S(2)}, u32[]{:S(2)}) collective-permute-start(bf16[33,64,128]{2,1,0:T(8,128)(2,1)} %get-tuple-element.49), channel_id=1, source_target_pairs={{0,96},{32,64},{64,32},{96,0},{1,97},{33,65},{65,33},{97,1},{2,98}... | collective-permute-start | bytes 1622024 | tf_op jit(solution)/shard_map/ppermute | solution.py:320
  16.1 23.2 %collective-permute-start.4 = (bf16[33,64,128]{2,1,0:T(8,128)(2,1)}, bf16[33,64,128]{2,1,0:T(8,128)(2,1)}, u32[]{:S(2)}, u32[]{:S(2)}) collective-permute-start(bf16[33,64,128]{2,1,0:T(8,128)(2,1)} %get-tuple-element.50), channel_id=1, source_target_pairs={{0,32},{32,0},{64,96},{96,64},{1,33},{33,1},{65,97},{97,65},{2,34}... | collective-permute-start | bytes 1622024 | tf_op jit(solution)/shard_map/ppermute | solution.py:320
  16.1 46.8 %collective-permute-start.7 = (bf16[33,64,128]{2,1,0:T(8,128)(2,1)}, bf16[33,64,128]{2,1,0:T(8,128)(2,1)}, u32[]{:S(2)}, u32[]{:S(2)}) collective-permute-start(bf16[33,64,128]{2,1,0:T(8,128)(2,1)} %get-tuple-element.48), channel_id=1, source_target_pairs={{1,0},{33,32},{65,64},{97,96},{2,1},{34,33},{66,65},{98,97},{3,2},... | collective-permute-start | bytes 1622024 | tf_op jit(solution)/shard_map/ppermute | solution.py:316
  27.1 12.1 %copy-start.8 = (bf16[33,64,128]{2,1,0:T(8,128)(2,1)}, bf16[33,64,128]{2,1,0:T(8,128)(2,1)S(1)}, u32[]{:S(2)}) copy-start(bf16[33,64,128]{2,1,0:T(8,128)(2,1)S(1)} %collective-permute-done.2) | copy-start | bytes 1622020
  28.5 20.3 %copy-start.1 = (bf16[33,64,128]{2,1,0:T(8,128)(2,1)}, bf16[33,64,128]{2,1,0:T(8,128)(2,1)S(1)}, u32[]{:S(2)}) copy-start(bf16[33,64,128]{2,1,0:T(8,128)(2,1)S(1)} %get-tuple-element.87.refs_2_.refs_0_) | copy-start | bytes 1622020
  28.5 20.3 %copy-start.2 = (bf16[33,64,128]{2,1,0:T(8,128)(2,1)}, bf16[33,64,128]{2,1,0:T(8,128)(2,1)S(1)}, u32[]{:S(2)}) copy-start(bf16[33,64,128]{2,1,0:T(8,128)(2,1)S(1)} %get-tuple-element.88.refs_2_.refs_4_) | copy-start | bytes 1622020
  40.5 0.8 copy-start.4
  40.6 8.2 %copy-start.3 = (bf16[33,64,128]{2,1,0:T(8,128)(2,1)}, bf16[33,64,128]{2,1,0:T(8,128)(2,1)S(1)}, u32[]{:S(2)}) copy-start(bf16[33,64,128]{2,1,0:T(8,128)(2,1)S(1)} %get-tuple-element.89.refs_4_.refs_2_) | copy-start | bytes 1622020
  41.4 7.4 %copy-start.9 = (bf16[33,64,128]{2,1,0:T(8,128)(2,1)S(1)}, bf16[33,64,128]{2,1,0:T(8,128)(2,1)}, u32[]{:S(2)}) copy-start(bf16[33,64,128]{2,1,0:T(8,128)(2,1)} %copy-done.8) | copy-start | bytes 1622020
  42.0 7.9 %copy-start.10 = (f32[4,256]{1,0:T(4,128)S(1)}, f32[4,256]{1,0:T(4,128)}, u32[]{:S(2)}) copy-start(f32[4,256]{1,0:T(4,128)} %fusion.10.small_ref) | copy-start | bytes 12292
  42.0 20.9 %collective-permute-start.8 = (bf16[33,64,128]{2,1,0:T(8,128)(2,1)}, bf16[33,64,128]{2,1,0:T(8,128)(2,1)S(1)}, u32[]{:S(2)}, u32[]{:S(2)}) collective-permute-start(bf16[33,64,128]{2,1,0:T(8,128)(2,1)} %collective-permute-done.4), channel_id=1, source_target_pairs={{1,0},{33,32},{65,64},{97,96},{2,1},{34,33},{66,65},{98,97},{3,2},... | collective-permute-start | bytes 1622024 | tf_op jit(solution)/shard_map/ppermute | solution.py:316
  48.8 25.2 %collective-permute-start.5 = (bf16[33,64,128]{2,1,0:T(8,128)(2,1)S(1)}, bf16[33,64,128]{2,1,0:T(8,128)(2,1)S(1)}, u32[]{:S(2)}, u32[]{:S(2)}) collective-permute-start(bf16[33,64,128]{2,1,0:T(8,128)(2,1)S(1)} %copy-done.9), channel_id=1, source_target_pairs={{1,0},{33,32},{65,64},{97,96},{2,1},{34,33},{66,65},{98,97},{3,2},... | collective-permute-start | bytes 1622024 | tf_op jit(solution)/shard_map/ppermute | solution.py:316
  48.9 35.7 %collective-permute-start.6 = (bf16[33,64,128]{2,1,0:T(8,128)(2,1)}, bf16[33,64,128]{2,1,0:T(8,128)(2,1)S(1)}, u32[]{:S(2)}, u32[]{:S(2)}) collective-permute-start(bf16[33,64,128]{2,1,0:T(8,128)(2,1)} %collective-permute-done.3), channel_id=1, source_target_pairs={{1,0},{33,32},{65,64},{97,96},{2,1},{34,33},{66,65},{98,97},{3,2},... | collective-permute-start | bytes 1622024 | tf_op jit(solution)/shard_map/ppermute | solution.py:316
  63.0 0.8 copy-start.5
  74.0 10.5 %copy-start.6 = (bf16[33,64,128]{2,1,0:T(8,128)(2,1)}, bf16[33,64,128]{2,1,0:T(8,128)(2,1)S(1)}, u32[]{:S(2)}) copy-start(bf16[33,64,128]{2,1,0:T(8,128)(2,1)S(1)} %collective-permute-done.5.refs_3_.refs_5_) | copy-start | bytes 1622020
  84.6 0.8 copy-start.7
  96.6 21.7 %collective-permute-start.10 = (f32[14,80,128]{2,1,0:T(8,128)}, f32[14,80,128]{2,1,0:T(8,128)S(1)}, u32[]{:S(2)}, u32[]{:S(2)}) collective-permute-start(f32[14,80,128]{2,1,0:T(8,128)} %get-tuple-element.59), channel_id=1, source_target_pairs={{1,0},{33,32},{65,64},{97,96},{2,1},{34,33},{66,65},{98,97},{3,2},... | collective-permute-start | bytes 1720328 | tf_op jit(solution)/shard_map/ppermute | solution.py:316
  98.5 20.7 %collective-permute-start.9 = (f32[14,80,128]{2,1,0:T(8,128)}, f32[14,80,128]{2,1,0:T(8,128)S(1)}, u32[]{:S(2)}, u32[]{:S(2)}) collective-permute-start(f32[14,80,128]{2,1,0:T(8,128)} %get-tuple-element.58), channel_id=1, source_target_pairs={{0,1},{32,33},{64,65},{96,97},{1,2},{33,34},{65,66},{97,98},{2,3},... | collective-permute-start | bytes 1720328 | tf_op jit(solution)/shard_map/ppermute | solution.py:316
  119.2 7.4 %copy-start.11 = (pred[46]{0:T(512)(128)(4,1)S(1)}, pred[46]{0:T(512)(128)(4,1)}, u32[]{:S(2)}) copy-start(pred[46]{0:T(512)(128)(4,1)} %constant.164) | copy-start | bytes 142
  119.2 7.4 %copy-start.12 = (pred[46]{0:T(512)(128)(4,1)S(1)}, pred[46]{0:T(512)(128)(4,1)}, u32[]{:S(2)}) copy-start(pred[46]{0:T(512)(128)(4,1)} %constant.165) | copy-start | bytes 142
  121.0 7.6 %collective-permute-start.11 = (f32[46,16,128]{2,1,0:T(8,128)S(1)}, f32[46,16,128]{2,1,0:T(8,128)S(1)}, u32[]{:S(2)}, u32[]{:S(2)}) collective-permute-start(f32[46,16,128]{2,1,0:T(8,128)S(1)} %get-tuple-element.84), channel_id=1, source_target_pairs={{0,32},{32,64},{64,96},{1,33},{33,65},{65,97},{2,34},{34,66},{66,9... | collective-permute-start | bytes 1130504 | tf_op jit(solution)/shard_map/ppermute | solution.py:316
  123.0 8.9 %collective-permute-start.12 = (f32[46,16,128]{2,1,0:T(8,128)S(1)}, f32[46,16,128]{2,1,0:T(8,128)S(1)}, u32[]{:S(2)}, u32[]{:S(2)}) collective-permute-start(f32[46,16,128]{2,1,0:T(8,128)S(1)} %get-tuple-element.83), channel_id=1, source_target_pairs={{32,0},{64,32},{96,64},{33,1},{65,33},{97,65},{34,2},{66,34},{98,6... | collective-permute-start | bytes 1130504 | tf_op jit(solution)/shard_map/ppermute | solution.py:316
  156.7 13.3 %collective-permute-start.13 = (f32[7,80,128]{2,1,0:T(8,128)}, f32[7,80,128]{2,1,0:T(8,128)S(1)}, u32[]{:S(2)}, u32[]{:S(2)}) collective-permute-start(f32[7,80,128]{2,1,0:T(8,128)} %get-tuple-element.65), channel_id=1, source_target_pairs={{0,1},{32,33},{64,65},{96,97},{1,2},{33,34},{65,66},{97,98},{2,3},... | collective-permute-start | bytes 860168 | tf_op jit(solution)/shard_map/ppermute | solution.py:316
  166.2 13.0 %collective-permute-start.14 = (f32[7,80,128]{2,1,0:T(8,128)}, f32[7,80,128]{2,1,0:T(8,128)S(1)}, u32[]{:S(2)}, u32[]{:S(2)}) collective-permute-start(f32[7,80,128]{2,1,0:T(8,128)} %get-tuple-element.66), channel_id=1, source_target_pairs={{1,0},{33,32},{65,64},{97,96},{2,1},{34,33},{66,65},{98,97},{3,2},... | collective-permute-start | bytes 860168 | tf_op jit(solution)/shard_map/ppermute | solution.py:316
  180.7 4.3 %collective-permute-start.15 = (f32[32,8,128]{2,1,0:T(8,128)S(1)}, f32[32,8,128]{2,1,0:T(8,128)S(1)}, u32[]{:S(2)}, u32[]{:S(2)}) collective-permute-start(f32[32,8,128]{2,1,0:T(8,128)S(1)} %get-tuple-element.86), channel_id=1, source_target_pairs={{0,32},{32,64},{64,96},{1,33},{33,65},{65,97},{2,34},{34,66},{66,9... | collective-permute-start | bytes 393224 | tf_op jit(solution)/shard_map/ppermute | solution.py:316
  182.6 6.3 %collective-permute-start.16 = (f32[32,8,128]{2,1,0:T(8,128)S(1)}, f32[32,8,128]{2,1,0:T(8,128)S(1)}, u32[]{:S(2)}, u32[]{:S(2)}) collective-permute-start(f32[32,8,128]{2,1,0:T(8,128)S(1)} %get-tuple-element.85), channel_id=1, source_target_pairs={{32,0},{64,32},{96,64},{33,1},{65,33},{97,65},{34,2},{66,34},{98,6... | collective-permute-start | bytes 393224 | tf_op jit(solution)/shard_map/ppermute | solution.py:316
  190.3 23.7 %collective-permute-start.18 = (f32[32,64,128]{2,1,0:T(8,128)S(1)}, f32[32,64,128]{2,1,0:T(8,128)S(1)}, u32[]{:S(2)}, u32[]{:S(2)}) collective-permute-start(f32[32,64,128]{2,1,0:T(8,128)S(1)} %get-tuple-element.72), channel_id=1, source_target_pairs={{0,64},{32,96},{64,0},{96,32},{1,65},{33,97},{65,1},{97,33},{2,66}... | collective-permute-start | bytes 3145736 | tf_op jit(solution)/shard_map/ppermute | solution.py:320
  190.4 23.6 %collective-permute-start.17 = (f32[32,64,128]{2,1,0:T(8,128)S(1)}, f32[32,64,128]{2,1,0:T(8,128)S(1)}, u32[]{:S(2)}, u32[]{:S(2)}) collective-permute-start(f32[32,64,128]{2,1,0:T(8,128)S(1)} %get-tuple-element.72), channel_id=1, source_target_pairs={{0,32},{32,0},{64,96},{96,64},{1,33},{33,1},{65,97},{97,65},{2,34}... | collective-permute-start | bytes 3145736 | tf_op jit(solution)/shard_map/ppermute | solution.py:320
  214.0 2.7 %collective-permute-start.19 = (f32[32,64,128]{2,1,0:T(8,128)S(1)}, f32[32,64,128]{2,1,0:T(8,128)S(1)}, u32[]{:S(2)}, u32[]{:S(2)}) collective-permute-start(f32[32,64,128]{2,1,0:T(8,128)S(1)} %collective-permute-done.18), channel_id=1, source_target_pairs={{0,32},{32,0},{64,96},{96,64},{1,33},{33,1},{65,97},{97,65},{2,34}... | collective-permute-start | bytes 3145736 | tf_op jit(solution)/shard_map/ppermute | solution.py:320
  214.2 2.5 %copy-start = (f32[32,256,128]{2,1,0:T(8,128)}, f32[32,256,128]{2,1,0:T(8,128)S(1)}, u32[]{:S(2)}) copy-start(f32[32,256,128]{2,1,0:T(8,128)S(1)} %constant_dynamic-update-slice_fusion.1) | copy-start | bytes 12582916

commit v4 on v3

--- a/solution.py
+++ b/solution.py
@@ -292,7 +292,7 @@
 
 
 def call(kernel, outs, in_specs, scratch, flops, args):
-    bytes_all = sum(a.size * a.dtype.itemsize for a in args)
+    bytes_all = 1 if flops == 1 else sum(a.size * a.dtype.itemsize for a in args)
     return pl.pallas_call(
         kernel,
         out_shape=[jax.ShapeDtypeStruct(*out) for out in outs],
@@ -344,12 +344,42 @@
     return value + jnp.pad(from_previous, pads[0]) + jnp.pad(from_next, pads[1])
 
 
-def in_bf16(values):
-    rows = []
-    for _ in range(3):
-        rows.append(lax.reduce_precision(values, 8, 7))
-        values = values - rows[-1]
-    return jnp.stack(rows).astype(BF16)
+def gathered(own):
+    across = to_xor(own, 2)
+    return [own, to_xor(own, 1), across, to_xor(across, 1)]
+
+
+def assemble_kernel(groups, quarter_ref, *refs):
+    parts, out_ref, sems = refs[:VIEWS], refs[-2], refs[-1]
+    copies = []
+    for by, part in enumerate(parts):
+        at = pl.multiple_of(QY * (quarter_ref[0] ^ by), QY)
+        for start, row, rows in groups:
+            copies.append(
+                pltpu.make_async_copy(
+                    part.at[pl.ds(start, rows)],
+                    out_ref.at[pl.ds(row, rows), pl.ds(at, QY)],
+                    sems.at[len(copies)],
+                )
+            )
+    for copy in copies:
+        copy.start()
+    for copy in copies:
+        copy.wait()
+
+
+def assemble(quarter, parts, groups, result):
+    begun = [] if result is None else [result]
+    return pl.pallas_call(
+        functools.partial(assemble_kernel, groups),
+        out_shape=jax.ShapeDtypeStruct((BX, NY, NZ), F32),
+        in_specs=[SMEM] + [ANY] * (VIEWS + len(begun)),
+        out_specs=ANY,
+        scratch_shapes=[pltpu.SemaphoreType.DMA((VIEWS * len(groups),))],
+        input_output_aliases={1 + VIEWS: 0} if begun else {},
+        compiler_params=pltpu.CompilerParams(vmem_limit_bytes=1024 * 1024),
+        cost_estimate=pl.CostEstimate(flops=1, bytes_accessed=1, transcendentals=0),
+    )(quarter[None], *parts, *begun)
 
 
 def shards(start_estimate, observed, psf_taps, offsets, coverage):
@@ -357,21 +387,19 @@
     bricks = lax.axis_size("brick")
     quarter = me ^ (2 * (lax.axis_index("brick") // (bricks // 2)))
 
-    small = jnp.concatenate([psf_taps.reshape(-1), offsets.astype(F32)])
-    wide = -(-small.shape[0] // NZ)
-    row = in_bf16(jnp.pad(small, (0, wide * NZ - small.shape[0]))).reshape(1, 3 * wide, NZ)
-    row = jnp.pad(row, ((0, 0), (0, QY - 3 * wide), (0, 0)))
     pieces = [lax.dynamic_slice_in_dim(observed[0], QY * (quarter ^ by), QY, 1) for by in range(VIEWS)]
-    pieces = [jnp.concatenate([piece, row], axis=0) for piece in pieces]
-    start_estimate, pieces = lax.optimization_barrier((start_estimate, pieces))
     here = [to_xor(piece, by) if by else piece for by, piece in enumerate(pieces)]
-    beyond = [from_next_brick(tile) for tile in here]
+    here[1], start_estimate, psf_taps, offsets, coverage = lax.optimization_barrier(
+        (here[1], start_estimate, psf_taps, offsets, coverage)
+    )
     across = lax.rem(lax.axis_index("brick") + 1, bricks // 2) == 0
-    here = [jnp.where(across, here[by ^ 2], here[by]) for by in range(VIEWS)]
     first = jnp.where(across, me ^ 2, me)
-    tiles = list(zip(here, beyond))
-    smalls = jnp.concatenate([tile[BX:] for tile in here], axis=0)[:, : 3 * wide].astype(F32).reshape(VIEWS, 3, wide * NZ)
-    smalls = (smalls[:, 2] + smalls[:, 1]) + smalls[:, 0]
+    beyond = [from_next_brick(tile) for tile in here[:HALF]]
+
+    smalls = jnp.concatenate([psf_taps.reshape(-1), offsets.astype(F32)])[None]
+    for by in (1, 2):
+        smalls = jnp.concatenate([smalls, to_xor(smalls, by)], axis=0)
+    smalls = jnp.where(across, jnp.roll(smalls, HALF, axis=0), smalls)
     shifts = smalls[:, OFFSET].astype(jnp.int32)
 
     padded = jnp.pad(start_estimate, ((0, 0), (HY, HY), (0, 0)))
@@ -390,7 +418,7 @@
     row_counts = jnp.repeat(counts, jnp.array([HX, BX, HX]), total_repeat_length=EX)[:, None, None]
     estimate = jnp.concatenate([before[:HX].astype(F32), estimate, after[:HX].astype(F32)], axis=0)
     fplane, aplane, fline, aline = call(
-        prepare_kernel, [FPLANE, APLANE, FLINE, ALINE], [SMEM] * 3, [], 10**9, (first[None], smalls, covers)
+        prepare_kernel, [FPLANE, APLANE, FLINE, ALINE], [SMEM] * 3, [], 1, (first[None], smalls, covers)
     )
 
     half = ((HALF, BX, QY, NZ), F32)
@@ -399,9 +427,13 @@
         [half, half],
         [VMEM, VMEM, ANY],
         [MID, FLINE, 1],
-        FLOPS,
+        1,
         (estimate.astype(BF16), fplane, fline),
     )
+    here[HALF:], beyond, blurred = lax.optimization_barrier((here[HALF:], beyond, blurred))
+    beyond = beyond + [from_next_brick(tile) for tile in here[HALF:]]
+    here = [jnp.where(across, here[by ^ 2], here[by]) for by in range(VIEWS)]
+    tiles = list(zip(here, beyond))
     tile_scratch = lambda views: ((views, 2 * BX, QY, NZ), BF16)
     back_scratch = lambda views: ((views * RANK, BX, QY, NZ), BF16)
     terms = ()
@@ -430,18 +462,19 @@
         2 * FLOPS,
         (shifts, estimate.astype(BF16), fplane, fline, aline, aplane, *[tile for pair in tiles for tile in pair]),
     )
-    summed = fold(summed[HX : HX + BX], *exchange("brick", to_previous, to_next), 0, 0)
-    summed = fold(
-        summed[:, HY : HY + QY], *exchange("view", summed[:, :HY], summed[:, EY - HY :]), 1, 0
-    )
-    estimate = estimate[HX : HX + BX, HY : HY + QY] * summed / counts[1]
-
-    across = to_xor(estimate, 2)
-    quarters = [estimate, to_xor(estimate, 1), across, to_xor(across, 1)]
-    result = jnp.zeros(start_estimate.shape, F32)
-    for by in range(VIEWS):
-        result = lax.dynamic_update_slice_in_dim(result, quarters[by], QY * (quarter ^ by), 1)
-    return result
+    own = summed[HX : HX + BX]
+    inner = own[HX : BX - HX]
+    from_quarters = exchange("view", inner[:, :HY], inner[:, EY - HY :])
+    from_bricks = exchange("brick", to_previous, to_next)
+    estimate = estimate[HX : HX + BX, HY : HY + QY] / counts[1]
+    inner = estimate[HX : BX - HX] * fold(inner[:, HY : HY + QY], *from_quarters, 1, 0)
+    outer = jnp.concatenate([own[:HX] + from_bricks[0], own[BX - HX :] + from_bricks[1]], axis=0)
+    from_quarters = exchange("view", outer[:, :HY], outer[:, EY - HY :])
+    outer = fold(outer[:, HY : HY + QY], *from_quarters, 1, 0)
+    outer = jnp.concatenate([estimate[:HX], estimate[BX - HX :]], axis=0) * outer
+
+    result = assemble(quarter, gathered(inner), ((0, HX, BX - 2 * HX),), None)
+    return assemble(quarter, gathered(outer), ((0, 0, HX), (HX, BX - HX, HX)), result)
 
 
 def solution(mesh):

time: 218 us -> 207 us (0.950)
  waiting for transfers between devices: 84.8 us -> 73.7 us
  other arithmetic: 17.7 us -> 11.8 us
  starting transfers between devices: 42.6 us -> 47.5 us
  Pallas kernels: 64 us -> 66.5 us
    ppermute x6 -> x11, waiting for transfers between devices: 36.5 us -> 24.4 us  [to_xor(): return lax.ppermute(value, 'view', [(i, i ^ by) for i in range(VIEWS)])]
    ppermute x6 -> x11, starting transfers between devices: 2.96 us -> 9.55 us  [to_xor(): return lax.ppermute(value, 'view', [(i, i ^ by) for i in range(VIEWS)])]
    pallas_call x0 -> x2, Pallas kernels: none -> 2.72 us  [assemble(): pl.pallas_call(functools.partial(assemble_kernel, groups), out_shape=jax....]
    ppermute x14 -> x16, starting transfers between devices: 39.6 us -> 38 us  [send(): return lax.ppermute(value, ('view', 'brick'), perm)]
    ppermute x14 -> x16, waiting for transfers between devices: 48.2 us -> 49.3 us  [send(): return lax.ppermute(value, ('view', 'brick'), perm)]
  transfers between devices with their start and end apart: 20 -> 27, of which waited for: 11 -> 11; matrix products, arithmetic and copies ran while one was open for 5% -> 5% of each run, Pallas kernels for 13% -> 15%
where the time goes in v4:
time: 207 us
  waiting for transfers between devices  73.7 us (36%)
  Pallas kernels  66.5 us (32%)
  starting transfers between devices  47.5 us (23%)
  other arithmetic  11.8 us (6%)
  local copies, waits for them, and re-layouts  5.77 us (3%)
    pallas_call x5, Pallas kernels, call(): pl.pallas_call(kernel, out_shape=[jax.ShapeDtypeStruct(*out) for out in o...  63.8 us
    ppermute x16, waiting for transfers between devices, send(): return lax.ppermute(value, ('view', 'brick'), perm)  49.3 us
    ppermute x16, starting transfers between devices, send(): return lax.ppermute(value, ('view', 'brick'), perm)  38 us
    ppermute x11, waiting for transfers between devices, to_xor(): return lax.ppermute(value, 'view', [(i, i ^ by) for i in range(VIEWS)])  24.4 us
    ppermute x11, starting transfers between devices, to_xor(): return lax.ppermute(value, 'view', [(i, i ^ by) for i in range(VIEWS)])  9.55 us
  transfers between devices with their start and end apart: 27, of which 11 were waited for; matrix products, arithmetic and copies ran while one was open for 5% of the time, Pallas kernels for 15%

profile of v4, /device:TPU:31, one launch (start us, length us, event | category | flops | bytes accessed | tf_op | source)
XLA Modules:
  0.0 206.6 jit_solution(16990074183508429534)
XLA Ops:
  0.0 2.7 %dynamic-slice_bitcast_fusion = (bf16[32,64,128]{2,1,0:T(8,128)(2,1)S(1)}, bf16[32,64,128]{2,1,0:T(8,128)(2,1)}, bf16[32,64,128]{2,1,0:T(8,128)(2,1)}, bf16[32,64,128]{2,1,0:T(8,128)(2,1)S(1)}) fusion(bf16[1,32,256,128]{3,2,1,0:T(8,128)(2,1)} %param.9, s32[]{:T(128)S(6)} %select_n.96, s32[]{:T(128)S(6)} %select_n.94, s32[]{:T(128)S(6)} %select_n.90, ...), kind=kLoop, calls=%fused_computation.11 | loop fusion | bytes 4194320 | tf_op jit(solution)/shard_map/dynamic_slice | solution.py:390
  2.7 0.7 collective-permute-start
  3.4 1.7 collective-permute-start.5
  6.4 0.7 collective-permute-start.3
  7.1 1.5 fusion.9
  8.7 1.5 collective-permute-start.4
  10.3 2.1 %collective-permute-start.2 = (bf16[8,80,128]{2,1,0:T(8,128)(2,1)S(1)}, bf16[8,80,128]{2,1,0:T(8,128)(2,1)S(1)}, u32[]{:S(2)}, u32[]{:S(2)}) collective-permute-start(bf16[8,80,128]{2,1,0:T(8,128)(2,1)S(1)} %get-tuple-element.111), channel_id=1, source_target_pairs={{1,0},{33,32},{65,64},{97,96},{2,1},{34,33},{66,65},{98,97},{3,2},... | collective-permute-start | bytes 491528 | tf_op jit(solution)/shard_map/ppermute | solution.py:316
  12.4 16.3 %collective-permute-done.4 = f32[2,136]{1,0:T(2,128)S(1)} collective-permute-done((f32[2,136]{1,0:T(2,128)S(1)}, f32[2,136]{1,0:T(2,128)S(1)}, u32[]{:S(2)}, u32[]{:S(2)}) %collective-permute-start.4) | collective-permute-done | bytes 1120 | tf_op jit(solution)/shard_map/ppermute | solution.py:320
  28.7 5.0 %collective-permute-start.1 = (bf16[8,80,128]{2,1,0:T(8,128)(2,1)S(1)}, bf16[8,80,128]{2,1,0:T(8,128)(2,1)S(1)}, u32[]{:S(2)}, u32[]{:S(2)}) collective-permute-start(bf16[8,80,128]{2,1,0:T(8,128)(2,1)S(1)} %get-tuple-element.112), channel_id=1, source_target_pairs={{0,1},{32,33},{64,65},{96,97},{1,2},{33,34},{65,66},{97,98},{2,3},... | collective-permute-start | bytes 491528 | tf_op jit(solution)/shard_map/ppermute | solution.py:316
  33.7 0.8 fusion.6.refs_0_.offsets_ref
  34.4 1.9 collective-permute-done.1
  37.2 6.6 %shard_map.64 = (bf16[384,512]{1,0:T(8,128)(2,1)}, bf16[5,576,768]{2,1,0:T(8,128)(2,1)}, bf16[4,384,256]{2,1,0:T(8,128)(2,1)}, bf16[4,256,384]{2,1,0:T(8,128)(2,1)}) custom-call(s32[1]{0:T(128)} %bitcast.7.first_ref, f32[4,136]{1,0:T(4,128)} %copy-done.5, f32[3,4]{1,0:T(4,128)} %maximum_convert_fusion.covers_ref), custom_call_target="tpu_custom_call" | custom-call | flops 1 | bytes 1 | tf_op jit(solution)/shard_map/pallas_call | solution.py:296
  43.8 1.1 fusion.ext_ref
  44.9 12.3 %shard_map.65 = (f32[2,32,64,128]{3,2,1,0:T(8,128)}, f32[2,32,64,128]{3,2,1,0:T(8,128)}) custom-call(bf16[46,80,128]{2,1,0:T(8,128)(2,1)} %fusion.ext_ref, bf16[384,512]{1,0:T(8,128)(2,1)} %get-tuple-element.59.plane_ref.fplane_ref, bf16[4,384,256]{2,1,0:T(8,128)(2,1)} %get-tuple-element.60.line_hbm.fline_hbm), custom_call_target="tpu_custom_call" | custom-call | flops 1 | bytes 1 | tf_op jit(solution)/shard_map/pallas_call | solution.py:296
  57.5 1.6 broadcast_select_fusion
  59.1 10.2 %shard_map.66.refs_8_ = f32[46,80,128]{2,1,0:T(8,128)} custom-call(s32[4]{0:T(128)} %fusion.6.refs_0_.offsets_ref, f32[2,32,64,128]{3,2,1,0:T(8,128)} %get-tuple-element.68.refs_1_, bf16[32,64,128]{2,1,0:T(8,128)(2,1)} %get-tuple-element.119.refs_2_.refs_0_, bf16[32,64,128]{2,1,0:T(8,128)(2,1)} %copy-done.1, ...), custom_call_target="tpu_custom_call" | custom-call | flops 2264924160 | bytes 9404432 | tf_op jit(solution)/shard_map/pallas_call | solution.py:296
  69.3 6.2 %collective-permute-done.9.refs_3_.refs_5_ = bf16[32,64,128]{2,1,0:T(8,128)(2,1)S(1)} collective-permute-done((bf16[32,64,128]{2,1,0:T(8,128)(2,1)S(1)}, bf16[32,64,128]{2,1,0:T(8,128)(2,1)S(1)}, u32[]{:S(2)}, u32[]{:S(2)}) %collective-permute-start.9) | collective-permute-done | bytes 524320 | tf_op jit(solution)/shard_map/ppermute | solution.py:316
  75.5 11.2 %collective-permute-done.10.refs_5_.refs_7_ = bf16[32,64,128]{2,1,0:T(8,128)(2,1)S(1)} collective-permute-done((bf16[32,64,128]{2,1,0:T(8,128)(2,1)S(1)}, bf16[32,64,128]{2,1,0:T(8,128)(2,1)S(1)}, u32[]{:S(2)}, u32[]{:S(2)}) %collective-permute-start.10) | collective-permute-done | bytes 524320 | tf_op jit(solution)/shard_map/ppermute | solution.py:316
  86.8 0.8 copy-done.4
  87.6 11.1 %shard_map.67 = (f32[46,80,128]{2,1,0:T(8,128)}, f32[14,80,128]{2,1,0:T(8,128)}, f32[14,80,128]{2,1,0:T(8,128)}) custom-call(s32[4]{0:T(128)} %fusion.6.refs_0_.offsets_ref, f32[2,32,64,128]{3,2,1,0:T(8,128)} %get-tuple-element.63.refs_1_, bf16[32,64,128]{2,1,0:T(8,128)(2,1)} %get-tuple-element.118.refs_2_.refs_4_, bf16[32,64,128]{2,1,0:T(8,128)(2,1)} %copy-done.3, ...), custom_call_target="tpu_custom_call" | custom-call | flops 2264924160 | bytes 11288592 | tf_op jit(solution)/shard_map/pallas_call | solution.py:296
  98.7 3.1 %collective-permute-start.11 = (f32[14,80,128]{2,1,0:T(8,128)}, f32[14,80,128]{2,1,0:T(8,128)S(1)}, u32[]{:S(2)}, u32[]{:S(2)}) collective-permute-start(f32[14,80,128]{2,1,0:T(8,128)} %get-tuple-element.72), channel_id=1, source_target_pairs={{0,1},{32,33},{64,65},{96,97},{1,2},{33,34},{65,66},{97,98},{2,3},... | collective-permute-start | bytes 1720328 | tf_op jit(solution)/shard_map/ppermute | solution.py:316
  101.8 2.2 %collective-permute-start.12 = (f32[14,80,128]{2,1,0:T(8,128)}, f32[14,80,128]{2,1,0:T(8,128)S(1)}, u32[]{:S(2)}, u32[]{:S(2)}) collective-permute-start(f32[14,80,128]{2,1,0:T(8,128)} %get-tuple-element.73), channel_id=1, source_target_pairs={{1,0},{33,32},{65,64},{97,96},{2,1},{34,33},{66,65},{98,97},{3,2},... | collective-permute-start | bytes 1720328 | tf_op jit(solution)/shard_map/ppermute | solution.py:316
  104.1 8.8 %collective-permute-done.11 = f32[14,80,128]{2,1,0:T(8,128)S(1)} collective-permute-done((f32[14,80,128]{2,1,0:T(8,128)}, f32[14,80,128]{2,1,0:T(8,128)S(1)}, u32[]{:S(2)}, u32[]{:S(2)}) %collective-permute-start.11) | collective-permute-done | bytes 573472 | tf_op jit(solution)/shard_map/ppermute | solution.py:316
  112.9 8.0 %collective-permute-done.12 = f32[14,80,128]{2,1,0:T(8,128)S(1)} collective-permute-done((f32[14,80,128]{2,1,0:T(8,128)}, f32[14,80,128]{2,1,0:T(8,128)S(1)}, u32[]{:S(2)}, u32[]{:S(2)}) %collective-permute-start.12) | collective-permute-done | bytes 573472 | tf_op jit(solution)/shard_map/ppermute | solution.py:316
  120.9 1.7 pad_add_fusion
  122.7 5.8 %collective-permute-start.14 = (f32[46,16,128]{2,1,0:T(8,128)S(1)}, f32[46,16,128]{2,1,0:T(8,128)S(1)}, u32[]{:S(2)}, u32[]{:S(2)}) collective-permute-start(f32[46,16,128]{2,1,0:T(8,128)S(1)} %get-tuple-element.99), channel_id=1, source_target_pairs={{32,0},{64,32},{96,64},{33,1},{65,33},{97,65},{34,2},{66,34},{98,6... | collective-permute-start | bytes 1130504 | tf_op jit(solution)/shard_map/ppermute | solution.py:316
  128.4 2.1 %collective-permute-start.13 = (f32[46,16,128]{2,1,0:T(8,128)S(1)}, f32[46,16,128]{2,1,0:T(8,128)S(1)}, u32[]{:S(2)}, u32[]{:S(2)}) collective-permute-start(f32[46,16,128]{2,1,0:T(8,128)S(1)} %get-tuple-element.100), channel_id=1, source_target_pairs={{0,32},{32,64},{64,96},{1,33},{33,65},{65,97},{2,34},{34,66},{66,9... | collective-permute-start | bytes 1130504 | tf_op jit(solution)/shard_map/ppermute | solution.py:316
  130.6 0.6 fusion.14
  131.2 1.9 select_select_fusion
  133.1 1.8 collective-permute-done.13
  134.9 1.4 fusion.8
  136.2 23.5 %shard_map.68 = (f32[46,80,128]{2,1,0:T(8,128)}, f32[7,80,128]{2,1,0:T(8,128)}, f32[7,80,128]{2,1,0:T(8,128)}) custom-call(s32[4]{0:T(128)} %fusion.6.refs_0_.offsets_ref, bf16[46,80,128]{2,1,0:T(8,128)(2,1)} %get-tuple-element.87.ext_ref, bf16[384,512]{1,0:T(8,128)(2,1)} %get-tuple-element.59.plane_ref.fplane_ref, ...), custom_call_target="tpu_custom_call" | custom-call | flops 9059696640 | bytes 11526160 | tf_op jit(solution)/shard_map/pallas_call | solution.py:296
  159.7 1.1 fusion.10
  160.8 1.9 collective-permute-start.23
  162.7 4.4 %collective-permute-start.22 = (f32[18,8,128]{2,1,0:T(8,128)S(1)}, f32[18,8,128]{2,1,0:T(8,128)S(1)}, u32[]{:S(2)}, u32[]{:S(2)}) collective-permute-start(f32[18,8,128]{2,1,0:T(8,128)S(1)} %get-tuple-element.96), channel_id=1, source_target_pairs={{0,32},{32,64},{64,96},{1,33},{33,65},{65,97},{2,34},{34,66},{66,9... | collective-permute-start | bytes 221192 | tf_op jit(solution)/shard_map/ppermute | solution.py:316
  167.1 1.9 collective-permute-start.15
  169.1 3.4 %collective-permute-start.16 = (f32[7,80,128]{2,1,0:T(8,128)}, f32[7,80,128]{2,1,0:T(8,128)S(1)}, u32[]{:S(2)}, u32[]{:S(2)}) collective-permute-start(f32[7,80,128]{2,1,0:T(8,128)} %get-tuple-element.80), channel_id=1, source_target_pairs={{1,0},{33,32},{65,64},{97,96},{2,1},{34,33},{66,65},{98,97},{3,2},... | collective-permute-start | bytes 860168 | tf_op jit(solution)/shard_map/ppermute | solution.py:316
  172.4 0.8 slice_divide_fusion
  173.4 3.2 %collective-permute-done.15 = f32[7,80,128]{2,1,0:T(8,128)S(1)} collective-permute-done((f32[7,80,128]{2,1,0:T(8,128)}, f32[7,80,128]{2,1,0:T(8,128)S(1)}, u32[]{:S(2)}, u32[]{:S(2)}) %collective-permute-start.15) | collective-permute-done | bytes 286752 | tf_op jit(solution)/shard_map/ppermute | solution.py:316
  176.6 7.1 %collective-permute-done.16 = f32[7,80,128]{2,1,0:T(8,128)S(1)} collective-permute-done((f32[7,80,128]{2,1,0:T(8,128)}, f32[7,80,128]{2,1,0:T(8,128)S(1)}, u32[]{:S(2)}, u32[]{:S(2)}) %collective-permute-start.16) | collective-permute-done | bytes 286752 | tf_op jit(solution)/shard_map/ppermute | solution.py:316
  183.7 1.9 collective-permute-start.18
  185.7 3.6 %collective-permute-start.17 = (f32[14,8,128]{2,1,0:T(8,128)S(1)}, f32[14,8,128]{2,1,0:T(8,128)S(1)}, u32[]{:S(2)}, u32[]{:S(2)}) collective-permute-start(f32[14,8,128]{2,1,0:T(8,128)S(1)} %get-tuple-element.110), channel_id=1, source_target_pairs={{0,32},{32,64},{64,96},{1,33},{33,65},{65,97},{2,34},{34,66},{66,9... | collective-permute-start | bytes 172040 | tf_op jit(solution)/shard_map/ppermute | solution.py:316
  189.4 1.2 collective-permute-done.17
  190.7 2.7 %collective-permute-start.24 = (f32[18,64,128]{2,1,0:T(8,128)S(1)}, f32[18,64,128]{2,1,0:T(8,128)S(1)}, u32[]{:S(2)}, u32[]{:S(2)}) collective-permute-start(f32[18,64,128]{2,1,0:T(8,128)S(1)} %slice_multiply_fusion.refs_0_), channel_id=1, source_target_pairs={{0,32},{32,0},{64,96},{96,64},{1,33},{33,1},{65,97},{97,65},{2,34}... | collective-permute-start | bytes 1769480 | tf_op jit(solution)/shard_map/ppermute | solution.py:320
  194.0 8.1 %collective-permute-done.20.refs_2_ = f32[14,64,128]{2,1,0:T(8,128)S(1)} collective-permute-done((f32[14,64,128]{2,1,0:T(8,128)S(1)}, f32[14,64,128]{2,1,0:T(8,128)S(1)}, u32[]{:S(2)}, u32[]{:S(2)}) %collective-permute-start.20) | collective-permute-done | bytes 458784 | tf_op jit(solution)/shard_map/ppermute | solution.py:320
  202.0 1.6 collective-permute-start.21
  203.6 1.4 shard_map.69.refs_4_
  205.1 1.3 shard_map.70
  (67 shorter events, 3.1 us)
Async XLA Ops:
  0.0 6.2 %copy-start.6 = (f32[1,3,3,15]{3,0,2,1:T(1,128)S(1)}, f32[1,3,3,15]{3,0,2,1:T(1,128)}, u32[]{:S(2)}) copy-start(f32[1,3,3,15]{3,0,2,1:T(1,128)} %param.10) | copy-start | bytes 1624
  2.7 3.5 %collective-permute-start = (bf16[32,64,128]{2,1,0:T(8,128)(2,1)}, bf16[32,64,128]{2,1,0:T(8,128)(2,1)S(1)}, u32[]{:S(2)}, u32[]{:S(2)}) collective-permute-start(bf16[32,64,128]{2,1,0:T(8,128)(2,1)} %get-tuple-element.93), channel_id=1, source_target_pairs={{0,32},{32,0},{64,96},{96,64},{1,33},{33,1},{65,97},{97,65},{2,34}... | collective-permute-start | bytes 1572872 | tf_op jit(solution)/shard_map/ppermute | solution.py:320
  3.4 53.8 %collective-permute-start.5 = (bf16[32,64,128]{2,1,0:T(8,128)(2,1)}, bf16[32,64,128]{2,1,0:T(8,128)(2,1)S(1)}, u32[]{:S(2)}, u32[]{:S(2)}) collective-permute-start(bf16[32,64,128]{2,1,0:T(8,128)(2,1)} %get-tuple-element.92), channel_id=1, source_target_pairs={{0,64},{32,96},{64,0},{96,32},{1,65},{33,97},{65,1},{97,33},{2,66}... | collective-permute-start | bytes 1572872 | tf_op jit(solution)/shard_map/ppermute | solution.py:320
  5.1 52.2 %collective-permute-start.6 = (bf16[32,64,128]{2,1,0:T(8,128)(2,1)S(1)}, bf16[32,64,128]{2,1,0:T(8,128)(2,1)S(1)}, u32[]{:S(2)}, u32[]{:S(2)}) collective-permute-start(bf16[32,64,128]{2,1,0:T(8,128)(2,1)S(1)} %get-tuple-element.94), channel_id=1, source_target_pairs={{0,96},{32,64},{64,32},{96,0},{1,97},{33,65},{65,33},{97,1},{2,98}... | collective-permute-start | bytes 1572872 | tf_op jit(solution)/shard_map/ppermute | solution.py:320
  5.1 52.2 %collective-permute-start.7 = (bf16[32,64,128]{2,1,0:T(8,128)(2,1)S(1)}, bf16[32,64,128]{2,1,0:T(8,128)(2,1)S(1)}, u32[]{:S(2)}, u32[]{:S(2)}) collective-permute-start(bf16[32,64,128]{2,1,0:T(8,128)(2,1)S(1)} %get-tuple-element.91), channel_id=1, source_target_pairs={{1,0},{33,32},{65,64},{97,96},{2,1},{34,33},{66,65},{98,97},{3,2},... | collective-permute-start | bytes 1572872 | tf_op jit(solution)/shard_map/ppermute | solution.py:316
  6.4 2.2 %copy-start.9 = (s32[4,1]{0,1:T(1,128)S(1)}, s32[4,1]{0,1:T(1,128)}, u32[]{:S(2)}) copy-start(s32[4,1]{0,1:T(1,128)} %param.12) | copy-start | bytes 52
  6.4 2.3 %collective-permute-start.3 = (f32[1,136]{1,0:T(1,128)S(1)}, f32[1,136]{1,0:T(1,128)S(1)}, u32[]{:S(2)}, u32[]{:S(2)}) collective-permute-start(f32[1,136]{1,0:T(1,128)S(1)} %bitcast.20), channel_id=1, source_target_pairs={{0,32},{32,0},{64,96},{96,64},{1,33},{33,1},{65,97},{97,65},{2,34}... | collective-permute-start | bytes 1640 | tf_op jit(solution)/shard_map/ppermute | solution.py:320
  8.7 20.0 %collective-permute-start.4 = (f32[2,136]{1,0:T(2,128)S(1)}, f32[2,136]{1,0:T(2,128)S(1)}, u32[]{:S(2)}, u32[]{:S(2)}) collective-permute-start(f32[2,136]{1,0:T(2,128)S(1)} %pad_maximum_fusion.4), channel_id=1, source_target_pairs={{0,64},{32,96},{64,0},{96,32},{1,65},{33,97},{65,1},{97,33},{2,66}... | collective-permute-start | bytes 3272 | tf_op jit(solution)/shard_map/ppermute | solution.py:320
  10.3 24.1 %collective-permute-start.2 = (bf16[8,80,128]{2,1,0:T(8,128)(2,1)S(1)}, bf16[8,80,128]{2,1,0:T(8,128)(2,1)S(1)}, u32[]{:S(2)}, u32[]{:S(2)}) collective-permute-start(bf16[8,80,128]{2,1,0:T(8,128)(2,1)S(1)} %get-tuple-element.111), channel_id=1, source_target_pairs={{1,0},{33,32},{65,64},{97,96},{2,1},{34,33},{66,65},{98,97},{3,2},... | collective-permute-start | bytes 491528 | tf_op jit(solution)/shard_map/ppermute | solution.py:316
  28.7 7.6 %collective-permute-start.1 = (bf16[8,80,128]{2,1,0:T(8,128)(2,1)S(1)}, bf16[8,80,128]{2,1,0:T(8,128)(2,1)S(1)}, u32[]{:S(2)}, u32[]{:S(2)}) collective-permute-start(bf16[8,80,128]{2,1,0:T(8,128)(2,1)S(1)} %get-tuple-element.112), channel_id=1, source_target_pairs={{0,1},{32,33},{64,65},{96,97},{1,2},{33,34},{65,66},{97,98},{2,3},... | collective-permute-start | bytes 491528 | tf_op jit(solution)/shard_map/ppermute | solution.py:316
  33.7 3.5 %copy-start.5 = (f32[4,136]{1,0:T(4,128)}, f32[4,136]{1,0:T(4,128)S(1)}, u32[]{:S(2)}) copy-start(f32[4,136]{1,0:T(4,128)S(1)} %maximum_select_fusion.small_ref) | copy-start | bytes 6532
  34.4 22.9 %collective-permute-start.8 = (bf16[32,64,128]{2,1,0:T(8,128)(2,1)S(1)}, bf16[32,64,128]{2,1,0:T(8,128)(2,1)S(1)}, u32[]{:S(2)}, u32[]{:S(2)}) collective-permute-start(bf16[32,64,128]{2,1,0:T(8,128)(2,1)S(1)} %collective-permute-done), channel_id=1, source_target_pairs={{1,0},{33,32},{65,64},{97,96},{2,1},{34,33},{66,65},{98,97},{3,2},... | collective-permute-start | bytes 1572872 | tf_op jit(solution)/shard_map/ppermute | solution.py:316
  57.3 1.8 copy-start.1
  57.3 1.8 copy-start.2
  57.3 18.2 %collective-permute-start.9 = (bf16[32,64,128]{2,1,0:T(8,128)(2,1)S(1)}, bf16[32,64,128]{2,1,0:T(8,128)(2,1)S(1)}, u32[]{:S(2)}, u32[]{:S(2)}) collective-permute-start(bf16[32,64,128]{2,1,0:T(8,128)(2,1)S(1)} %collective-permute-done.5), channel_id=1, source_target_pairs={{1,0},{33,32},{65,64},{97,96},{2,1},{34,33},{66,65},{98,97},{3,2},... | collective-permute-start | bytes 1572872 | tf_op jit(solution)/shard_map/ppermute | solution.py:316
  57.4 29.4 %collective-permute-start.10 = (bf16[32,64,128]{2,1,0:T(8,128)(2,1)S(1)}, bf16[32,64,128]{2,1,0:T(8,128)(2,1)S(1)}, u32[]{:S(2)}, u32[]{:S(2)}) collective-permute-start(bf16[32,64,128]{2,1,0:T(8,128)(2,1)S(1)} %collective-permute-done.6), channel_id=1, source_target_pairs={{1,0},{33,32},{65,64},{97,96},{2,1},{34,33},{66,65},{98,97},{3,2},... | collective-permute-start | bytes 1572872 | tf_op jit(solution)/shard_map/ppermute | solution.py:316
  75.5 11.2 %copy-start.3 = (bf16[32,64,128]{2,1,0:T(8,128)(2,1)}, bf16[32,64,128]{2,1,0:T(8,128)(2,1)S(1)}, u32[]{:S(2)}) copy-start(bf16[32,64,128]{2,1,0:T(8,128)(2,1)S(1)} %collective-permute-done.9.refs_3_.refs_5_) | copy-start | bytes 1572868
  86.8 0.8 copy-start.4
  98.7 14.2 %collective-permute-start.11 = (f32[14,80,128]{2,1,0:T(8,128)}, f32[14,80,128]{2,1,0:T(8,128)S(1)}, u32[]{:S(2)}, u32[]{:S(2)}) collective-permute-start(f32[14,80,128]{2,1,0:T(8,128)} %get-tuple-element.72), channel_id=1, source_target_pairs={{0,1},{32,33},{64,65},{96,97},{1,2},{33,34},{65,66},{97,98},{2,3},... | collective-permute-start | bytes 1720328 | tf_op jit(solution)/shard_map/ppermute | solution.py:316
  101.8 19.1 %collective-permute-start.12 = (f32[14,80,128]{2,1,0:T(8,128)}, f32[14,80,128]{2,1,0:T(8,128)S(1)}, u32[]{:S(2)}, u32[]{:S(2)}) collective-permute-start(f32[14,80,128]{2,1,0:T(8,128)} %get-tuple-element.73), channel_id=1, source_target_pairs={{1,0},{33,32},{65,64},{97,96},{2,1},{34,33},{66,65},{98,97},{3,2},... | collective-permute-start | bytes 1720328 | tf_op jit(solution)/shard_map/ppermute | solution.py:316
  120.9 10.3 %copy-start.7 = (pred[46]{0:T(512)(128)(4,1)S(1)}, pred[46]{0:T(512)(128)(4,1)}, u32[]{:S(2)}) copy-start(pred[46]{0:T(512)(128)(4,1)} %constant.160) | copy-start | bytes 142
  120.9 10.3 %copy-start.8 = (pred[46]{0:T(512)(128)(4,1)S(1)}, pred[46]{0:T(512)(128)(4,1)}, u32[]{:S(2)}) copy-start(pred[46]{0:T(512)(128)(4,1)} %constant.159) | copy-start | bytes 142
  122.7 10.4 %collective-permute-start.14 = (f32[46,16,128]{2,1,0:T(8,128)S(1)}, f32[46,16,128]{2,1,0:T(8,128)S(1)}, u32[]{:S(2)}, u32[]{:S(2)}) collective-permute-start(f32[46,16,128]{2,1,0:T(8,128)S(1)} %get-tuple-element.99), channel_id=1, source_target_pairs={{32,0},{64,32},{96,64},{33,1},{65,33},{97,65},{34,2},{66,34},{98,6... | collective-permute-start | bytes 1130504 | tf_op jit(solution)/shard_map/ppermute | solution.py:316
  128.4 6.5 %collective-permute-start.13 = (f32[46,16,128]{2,1,0:T(8,128)S(1)}, f32[46,16,128]{2,1,0:T(8,128)S(1)}, u32[]{:S(2)}, u32[]{:S(2)}) collective-permute-start(f32[46,16,128]{2,1,0:T(8,128)S(1)} %get-tuple-element.100), channel_id=1, source_target_pairs={{0,32},{32,64},{64,96},{1,33},{33,65},{65,97},{2,34},{34,66},{66,9... | collective-permute-start | bytes 1130504 | tf_op jit(solution)/shard_map/ppermute | solution.py:316
  159.7 13.5 %copy-start = (f32[46,80,128]{2,1,0:T(8,128)S(1)}, f32[46,80,128]{2,1,0:T(8,128)}, u32[]{:S(2)}) copy-start(f32[46,80,128]{2,1,0:T(8,128)} %get-tuple-element.78) | copy-start | bytes 5652484
  160.8 12.4 %collective-permute-start.23 = (f32[18,8,128]{2,1,0:T(8,128)S(1)}, f32[18,8,128]{2,1,0:T(8,128)S(1)}, u32[]{:S(2)}, u32[]{:S(2)}) collective-permute-start(f32[18,8,128]{2,1,0:T(8,128)S(1)} %get-tuple-element.95), channel_id=1, source_target_pairs={{32,0},{64,32},{96,64},{33,1},{65,33},{97,65},{34,2},{66,34},{98,6... | collective-permute-start | bytes 221192 | tf_op jit(solution)/shard_map/ppermute | solution.py:316
  162.7 10.5 %collective-permute-start.22 = (f32[18,8,128]{2,1,0:T(8,128)S(1)}, f32[18,8,128]{2,1,0:T(8,128)S(1)}, u32[]{:S(2)}, u32[]{:S(2)}) collective-permute-start(f32[18,8,128]{2,1,0:T(8,128)S(1)} %get-tuple-element.96), channel_id=1, source_target_pairs={{0,32},{32,64},{64,96},{1,33},{33,65},{65,97},{2,34},{34,66},{66,9... | collective-permute-start | bytes 221192 | tf_op jit(solution)/shard_map/ppermute | solution.py:316
  167.1 9.4 %collective-permute-start.15 = (f32[7,80,128]{2,1,0:T(8,128)}, f32[7,80,128]{2,1,0:T(8,128)S(1)}, u32[]{:S(2)}, u32[]{:S(2)}) collective-permute-start(f32[7,80,128]{2,1,0:T(8,128)} %get-tuple-element.79), channel_id=1, source_target_pairs={{0,1},{32,33},{64,65},{96,97},{1,2},{33,34},{65,66},{97,98},{2,3},... | collective-permute-start | bytes 860168 | tf_op jit(solution)/shard_map/ppermute | solution.py:316
  169.1 14.6 %collective-permute-start.16 = (f32[7,80,128]{2,1,0:T(8,128)}, f32[7,80,128]{2,1,0:T(8,128)S(1)}, u32[]{:S(2)}, u32[]{:S(2)}) collective-permute-start(f32[7,80,128]{2,1,0:T(8,128)} %get-tuple-element.80), channel_id=1, source_target_pairs={{1,0},{33,32},{65,64},{97,96},{2,1},{34,33},{66,65},{98,97},{3,2},... | collective-permute-start | bytes 860168 | tf_op jit(solution)/shard_map/ppermute | solution.py:316
  173.3 20.1 %collective-permute-start.25 = (f32[18,64,128]{2,1,0:T(8,128)S(1)}, f32[18,64,128]{2,1,0:T(8,128)S(1)}, u32[]{:S(2)}, u32[]{:S(2)}) collective-permute-start(f32[18,64,128]{2,1,0:T(8,128)S(1)} %slice_multiply_fusion.refs_0_), channel_id=1, source_target_pairs={{0,64},{32,96},{64,0},{96,32},{1,65},{33,97},{65,1},{97,33},{2,66}... | collective-permute-start | bytes 1769480 | tf_op jit(solution)/shard_map/ppermute | solution.py:320
  183.7 5.6 %collective-permute-start.18 = (f32[14,8,128]{2,1,0:T(8,128)S(1)}, f32[14,8,128]{2,1,0:T(8,128)S(1)}, u32[]{:S(2)}, u32[]{:S(2)}) collective-permute-start(f32[14,8,128]{2,1,0:T(8,128)S(1)} %get-tuple-element.109), channel_id=1, source_target_pairs={{32,0},{64,32},{96,64},{33,1},{65,33},{97,65},{34,2},{66,34},{98,6... | collective-permute-start | bytes 172040 | tf_op jit(solution)/shard_map/ppermute | solution.py:316
  185.7 4.9 %collective-permute-start.17 = (f32[14,8,128]{2,1,0:T(8,128)S(1)}, f32[14,8,128]{2,1,0:T(8,128)S(1)}, u32[]{:S(2)}, u32[]{:S(2)}) collective-permute-start(f32[14,8,128]{2,1,0:T(8,128)S(1)} %get-tuple-element.110), channel_id=1, source_target_pairs={{0,32},{32,64},{64,96},{1,33},{33,65},{65,97},{2,34},{34,66},{66,9... | collective-permute-start | bytes 172040 | tf_op jit(solution)/shard_map/ppermute | solution.py:316
  190.6 11.4 %collective-permute-start.20 = (f32[14,64,128]{2,1,0:T(8,128)S(1)}, f32[14,64,128]{2,1,0:T(8,128)S(1)}, u32[]{:S(2)}, u32[]{:S(2)}) collective-permute-start(f32[14,64,128]{2,1,0:T(8,128)S(1)} %fusion.4.refs_0_), channel_id=1, source_target_pairs={{0,64},{32,96},{64,0},{96,32},{1,65},{33,97},{65,1},{97,33},{2,66}... | collective-permute-start | bytes 1376264 | tf_op jit(solution)/shard_map/ppermute | solution.py:320
  190.7 12.9 %collective-permute-start.24 = (f32[18,64,128]{2,1,0:T(8,128)S(1)}, f32[18,64,128]{2,1,0:T(8,128)S(1)}, u32[]{:S(2)}, u32[]{:S(2)}) collective-permute-start(f32[18,64,128]{2,1,0:T(8,128)S(1)} %slice_multiply_fusion.refs_0_), channel_id=1, source_target_pairs={{0,32},{32,0},{64,96},{96,64},{1,33},{33,1},{65,97},{97,65},{2,34}... | collective-permute-start | bytes 1769480 | tf_op jit(solution)/shard_map/ppermute | solution.py:320
  193.4 10.2 %collective-permute-start.26 = (f32[18,64,128]{2,1,0:T(8,128)S(1)}, f32[18,64,128]{2,1,0:T(8,128)S(1)}, u32[]{:S(2)}, u32[]{:S(2)}) collective-permute-start(f32[18,64,128]{2,1,0:T(8,128)S(1)} %collective-permute-done.25.refs_2_), channel_id=1, source_target_pairs={{0,32},{32,0},{64,96},{96,64},{1,33},{33,1},{65,97},{97,65},{2,34}... | collective-permute-start | bytes 1769480 | tf_op jit(solution)/shard_map/ppermute | solution.py:320
  193.4 11.6 %collective-permute-start.19 = (f32[14,64,128]{2,1,0:T(8,128)S(1)}, f32[14,64,128]{2,1,0:T(8,128)S(1)}, u32[]{:S(2)}, u32[]{:S(2)}) collective-permute-start(f32[14,64,128]{2,1,0:T(8,128)S(1)} %fusion.4.refs_0_), channel_id=1, source_target_pairs={{0,32},{32,0},{64,96},{96,64},{1,33},{33,1},{65,97},{97,65},{2,34}... | collective-permute-start | bytes 1376264 | tf_op jit(solution)/shard_map/ppermute | solution.py:320
  202.0 3.1 %collective-permute-start.21 = (f32[14,64,128]{2,1,0:T(8,128)S(1)}, f32[14,64,128]{2,1,0:T(8,128)S(1)}, u32[]{:S(2)}, u32[]{:S(2)}) collective-permute-start(f32[14,64,128]{2,1,0:T(8,128)S(1)} %collective-permute-done.20.refs_2_), channel_id=1, source_target_pairs={{0,32},{32,0},{64,96},{96,64},{1,33},{33,1},{65,97},{97,65},{2,34}... | collective-permute-start | bytes 1376264 | tf_op jit(solution)/shard_map/ppermute | solution.py:320

commit v5 on v4

--- a/solution.py
+++ b/solution.py
@@ -109,7 +109,7 @@
 
 
 def forward_plane(ext_ref, plane_ref, mid_ref):
-    @pl.loop(0, BX // (2 * FX))
+    @pl.loop(0, BX // (2 * FX), unroll=2)
     def _(step):
         x0 = step * (2 * FX)
         for y0 in range(0, QY, YB):
@@ -155,14 +155,13 @@
 def adjoint_plane(back_ref, plane_ref, out_ref, first_pair, pairs):
     columns = slice(first_pair * AX * YB, (first_pair + pairs) * AX * YB)
 
-    @pl.loop(0, BX // AX)
-    def _(step):
+    for step in range(BX // AX):
         x0 = step * AX
-        kind = jnp.minimum(step, 2) + jnp.maximum(step - 5, 0)
+        kind = min(step, 2) + max(step - 5, 0)
         for y0 in range(0, QY // 2, YB):
             starts = (y0, y0 + QY // 2)
             parts = [
-                back_ref[:pairs, pl.ds(x0, AX), at : at + YB, :].reshape(pairs * AX * YB, NZ)
+                back_ref[:pairs, x0 : x0 + AX, at : at + YB, :].reshape(pairs * AX * YB, NZ)
                 for at in starts
             ]
             made = jnp.dot(
@@ -171,7 +170,7 @@
                 preferred_element_type=jnp.float32,
             )
             for part, at in enumerate(starts):
-                out_ref[pl.ds(x0, AW), at : at + YW, :] += made[
+                out_ref[x0 : x0 + AW, at : at + YW, :] += made[
                     :, part * NZ : (part + 1) * NZ
                 ].reshape(AW, YW, NZ)
 
@@ -387,18 +386,16 @@
     bricks = lax.axis_size("brick")
     quarter = me ^ (2 * (lax.axis_index("brick") // (bricks // 2)))
 
+    small = jnp.concatenate([psf_taps.reshape(-1), offsets.astype(F32)])[None]
+    smalls = jnp.concatenate([small] + [to_xor(small, by) for by in range(1, VIEWS)], axis=0)
+
     pieces = [lax.dynamic_slice_in_dim(observed[0], QY * (quarter ^ by), QY, 1) for by in range(VIEWS)]
+    pieces, smalls = lax.optimization_barrier((pieces, smalls))
     here = [to_xor(piece, by) if by else piece for by, piece in enumerate(pieces)]
-    here[1], start_estimate, psf_taps, offsets, coverage = lax.optimization_barrier(
-        (here[1], start_estimate, psf_taps, offsets, coverage)
-    )
     across = lax.rem(lax.axis_index("brick") + 1, bricks // 2) == 0
     first = jnp.where(across, me ^ 2, me)
     beyond = [from_next_brick(tile) for tile in here[:HALF]]
 
-    smalls = jnp.concatenate([psf_taps.reshape(-1), offsets.astype(F32)])[None]
-    for by in (1, 2):
-        smalls = jnp.concatenate([smalls, to_xor(smalls, by)], axis=0)
     smalls = jnp.where(across, jnp.roll(smalls, HALF, axis=0), smalls)
     shifts = smalls[:, OFFSET].astype(jnp.int32)
 

time: 207 us -> 197 us (0.952)
  waiting for transfers between devices: 73.7 us -> 62 us
  Pallas kernels: 66.5 us -> 61.7 us
  other arithmetic: 11.8 us -> 15.8 us
  starting transfers between devices: 47.5 us -> 50.1 us
    ppermute x11 -> x12, waiting for transfers between devices: 24.4 us -> 8.1 us  [to_xor(): return lax.ppermute(value, 'view', [(i, i ^ by) for i in range(VIEWS)])]
    pallas_call x5, Pallas kernels: 63.8 us -> 59 us  [call(): pl.pallas_call(kernel, out_shape=[jax.ShapeDtypeStruct(*out) for out in o...]
    ppermute x16, waiting for transfers between devices: 49.3 us -> 53.9 us  [send(): return lax.ppermute(value, ('view', 'brick'), perm)]
    ppermute x16, starting transfers between devices: 38 us -> 40.2 us  [send(): return lax.ppermute(value, ('view', 'brick'), perm)]
    ppermute x11 -> x12, starting transfers between devices: 9.55 us -> 9.96 us  [to_xor(): return lax.ppermute(value, 'view', [(i, i ^ by) for i in range(VIEWS)])]
  transfers between devices with their start and end apart: 27 -> 28, of which waited for: 11 -> 10; matrix products, arithmetic and copies ran while one was open for 5% -> 8% of each run, Pallas kernels for 15% -> 15%
where the time goes in v5:
time: 197 us
  waiting for transfers between devices  62 us (31%)
  Pallas kernels  61.7 us (31%)
  starting transfers between devices  50.1 us (25%)
  other arithmetic  15.8 us (8%)
  local copies, waits for them, and re-layouts  5.79 us (3%)
    pallas_call x5, Pallas kernels, call(): pl.pallas_call(kernel, out_shape=[jax.ShapeDtypeStruct(*out) for out in o...  59 us
    ppermute x16, waiting for transfers between devices, send(): return lax.ppermute(value, ('view', 'brick'), perm)  53.9 us
    ppermute x16, starting transfers between devices, send(): return lax.ppermute(value, ('view', 'brick'), perm)  40.2 us
    ppermute x12, starting transfers between devices, to_xor(): return lax.ppermute(value, 'view', [(i, i ^ by) for i in range(VIEWS)])  9.96 us
    ppermute x12, waiting for transfers between devices, to_xor(): return lax.ppermute(value, 'view', [(i, i ^ by) for i in range(VIEWS)])  8.1 us
  transfers between devices with their start and end apart: 28, of which 10 were waited for; matrix products, arithmetic and copies ran while one was open for 8% of the time, Pallas kernels for 15%

profile of v5, /device:TPU:31, one launch (start us, length us, event | category | flops | bytes accessed | tf_op | source)
XLA Modules:
  0.0 196.7 jit_solution(8552882092659915788)
XLA Ops:
  1.5 2.2 %collective-permute-start.4 = (f32[1,136]{1,0:T(1,128)S(1)}, f32[1,136]{1,0:T(1,128)S(1)}, u32[]{:S(2)}, u32[]{:S(2)}) collective-permute-start(f32[1,136]{1,0:T(1,128)S(1)} %bitcast.20), channel_id=1, source_target_pairs={{0,96},{32,64},{64,32},{96,0},{1,97},{33,65},{65,33},{97,1},{2,98}... | collective-permute-start | bytes 1640 | tf_op jit(solution)/shard_map/ppermute | solution.py:319
  4.9 1.6 fusion.9
  6.7 0.8 pad_maximum_fusion.1
  7.4 2.4 %collective-permute-start.1 = (bf16[8,80,128]{2,1,0:T(8,128)(2,1)}, bf16[8,80,128]{2,1,0:T(8,128)(2,1)}, u32[]{:S(2)}, u32[]{:S(2)}) collective-permute-start(bf16[8,80,128]{2,1,0:T(8,128)(2,1)} %get-tuple-element.111), channel_id=1, source_target_pairs={{1,0},{33,32},{65,64},{97,96},{2,1},{34,33},{66,65},{98,97},{3,2},... | collective-permute-start | bytes 491528 | tf_op jit(solution)/shard_map/ppermute | solution.py:315
  9.8 8.3 %collective-permute-start = (bf16[8,80,128]{2,1,0:T(8,128)(2,1)}, bf16[8,80,128]{2,1,0:T(8,128)(2,1)}, u32[]{:S(2)}, u32[]{:S(2)}) collective-permute-start(bf16[8,80,128]{2,1,0:T(8,128)(2,1)} %get-tuple-element.112), channel_id=1, source_target_pairs={{0,1},{32,33},{64,65},{96,97},{1,2},{33,34},{65,66},{97,98},{2,3},... | collective-permute-start | bytes 491528 | tf_op jit(solution)/shard_map/ppermute | solution.py:315
  18.2 1.4 dynamic-slice_bitcast_fusion
  19.7 2.2 %collective-permute-start.6 = (bf16[32,64,128]{2,1,0:T(8,128)(2,1)}, bf16[32,64,128]{2,1,0:T(8,128)(2,1)S(1)}, u32[]{:S(2)}, u32[]{:S(2)}) collective-permute-start(bf16[32,64,128]{2,1,0:T(8,128)(2,1)} %get-tuple-element.56), channel_id=1, source_target_pairs={{0,96},{32,64},{64,32},{96,0},{1,97},{33,65},{65,33},{97,1},{2,98}... | collective-permute-start | bytes 1572872 | tf_op jit(solution)/shard_map/ppermute | solution.py:319
  22.6 0.8 slice_reduce_fusion.1
  23.4 0.8 slice_reduce_fusion
  24.7 6.6 %shard_map.64 = (bf16[384,512]{1,0:T(8,128)(2,1)}, bf16[5,576,768]{2,1,0:T(8,128)(2,1)}, bf16[4,384,256]{2,1,0:T(8,128)(2,1)}, bf16[4,256,384]{2,1,0:T(8,128)(2,1)}) custom-call(s32[1]{0:T(128)} %bitcast.7.first_ref, f32[4,136]{1,0:T(4,128)} %copy-done.7, f32[3,4]{1,0:T(4,128)} %maximum_convert_fusion.covers_ref), custom_call_target="tpu_custom_call" | custom-call | flops 1 | bytes 1 | tf_op jit(solution)/shard_map/pallas_call | solution.py:295
  31.4 0.9 slice_convert_fusion
  32.3 0.9 slice_convert_fusion.1
  33.2 1.1 fusion.ext_ref
  34.3 11.7 %shard_map.65 = (f32[2,32,64,128]{3,2,1,0:T(8,128)}, f32[2,32,64,128]{3,2,1,0:T(8,128)}) custom-call(bf16[46,80,128]{2,1,0:T(8,128)(2,1)} %fusion.ext_ref, bf16[384,512]{1,0:T(8,128)(2,1)} %get-tuple-element.59.plane_ref.fplane_ref, bf16[4,384,256]{2,1,0:T(8,128)(2,1)} %get-tuple-element.60.line_hbm.fline_hbm), custom_call_target="tpu_custom_call" | custom-call | flops 1 | bytes 1 | tf_op jit(solution)/shard_map/pallas_call | solution.py:295
  46.1 6.4 %collective-permute-done.9.refs_5_.refs_3_ = bf16[32,64,128]{2,1,0:T(8,128)(2,1)S(1)} collective-permute-done((bf16[32,64,128]{2,1,0:T(8,128)(2,1)S(1)}, bf16[32,64,128]{2,1,0:T(8,128)(2,1)S(1)}, u32[]{:S(2)}, u32[]{:S(2)}) %collective-permute-start.9) | collective-permute-done | bytes 524320 | tf_op jit(solution)/shard_map/ppermute | solution.py:315
  52.5 1.5 broadcast_select_fusion
  54.0 9.2 %shard_map.66.refs_8_ = f32[46,80,128]{2,1,0:T(8,128)} custom-call(s32[4]{0:T(128)} %fusion.6.refs_0_.offsets_ref, f32[2,32,64,128]{3,2,1,0:T(8,128)} %get-tuple-element.68.refs_1_, bf16[32,64,128]{2,1,0:T(8,128)(2,1)} %get-tuple-element.121.refs_2_.refs_0_, bf16[32,64,128]{2,1,0:T(8,128)(2,1)} %copy-done.3, ...), custom_call_target="tpu_custom_call" | custom-call | flops 2264924160 | bytes 9404432 | tf_op jit(solution)/shard_map/pallas_call | solution.py:295
  63.2 6.8 %collective-permute-done.10.refs_3_.refs_5_ = bf16[32,64,128]{2,1,0:T(8,128)(2,1)S(1)} collective-permute-done((bf16[32,64,128]{2,1,0:T(8,128)(2,1)S(1)}, bf16[32,64,128]{2,1,0:T(8,128)(2,1)S(1)}, u32[]{:S(2)}, u32[]{:S(2)}) %collective-permute-start.10) | collective-permute-done | bytes 524320 | tf_op jit(solution)/shard_map/ppermute | solution.py:315
  69.9 11.2 %collective-permute-done.11.refs_5_.refs_7_ = bf16[32,64,128]{2,1,0:T(8,128)(2,1)S(1)} collective-permute-done((bf16[32,64,128]{2,1,0:T(8,128)(2,1)S(1)}, bf16[32,64,128]{2,1,0:T(8,128)(2,1)S(1)}, u32[]{:S(2)}, u32[]{:S(2)}) %collective-permute-start.11) | collective-permute-done | bytes 524320 | tf_op jit(solution)/shard_map/ppermute | solution.py:315
  81.2 0.8 copy-done.6
  82.0 9.9 %shard_map.67 = (f32[46,80,128]{2,1,0:T(8,128)}, f32[14,80,128]{2,1,0:T(8,128)}, f32[14,80,128]{2,1,0:T(8,128)}) custom-call(s32[4]{0:T(128)} %fusion.6.refs_0_.offsets_ref, f32[2,32,64,128]{3,2,1,0:T(8,128)} %get-tuple-element.63.refs_1_, bf16[32,64,128]{2,1,0:T(8,128)(2,1)} %get-tuple-element.120.refs_2_.refs_4_, bf16[32,64,128]{2,1,0:T(8,128)(2,1)} %copy-done.5, ...), custom_call_target="tpu_custom_call" | custom-call | flops 2264924160 | bytes 11288592 | tf_op jit(solution)/shard_map/pallas_call | solution.py:295
  91.9 1.9 collective-permute-start.12
  93.8 3.4 %collective-permute-start.13 = (f32[14,80,128]{2,1,0:T(8,128)}, f32[14,80,128]{2,1,0:T(8,128)S(1)}, u32[]{:S(2)}, u32[]{:S(2)}) collective-permute-start(f32[14,80,128]{2,1,0:T(8,128)} %get-tuple-element.73), channel_id=1, source_target_pairs={{1,0},{33,32},{65,64},{97,96},{2,1},{34,33},{66,65},{98,97},{3,2},... | collective-permute-start | bytes 1720328 | tf_op jit(solution)/shard_map/ppermute | solution.py:315
  97.3 8.9 %collective-permute-done.12 = f32[14,80,128]{2,1,0:T(8,128)S(1)} collective-permute-done((f32[14,80,128]{2,1,0:T(8,128)}, f32[14,80,128]{2,1,0:T(8,128)S(1)}, u32[]{:S(2)}, u32[]{:S(2)}) %collective-permute-start.12) | collective-permute-done | bytes 573472 | tf_op jit(solution)/shard_map/ppermute | solution.py:315
  106.2 7.4 %collective-permute-done.13 = f32[14,80,128]{2,1,0:T(8,128)S(1)} collective-permute-done((f32[14,80,128]{2,1,0:T(8,128)}, f32[14,80,128]{2,1,0:T(8,128)S(1)}, u32[]{:S(2)}, u32[]{:S(2)}) %collective-permute-start.13) | collective-permute-done | bytes 573472 | tf_op jit(solution)/shard_map/ppermute | solution.py:315
  113.5 1.8 pad_add_fusion
  115.4 5.1 %collective-permute-start.15 = (f32[46,16,128]{2,1,0:T(8,128)S(1)}, f32[46,16,128]{2,1,0:T(8,128)S(1)}, u32[]{:S(2)}, u32[]{:S(2)}) collective-permute-start(f32[46,16,128]{2,1,0:T(8,128)S(1)} %get-tuple-element.99), channel_id=1, source_target_pairs={{32,0},{64,32},{96,64},{33,1},{65,33},{97,65},{34,2},{66,34},{98,6... | collective-permute-start | bytes 1130504 | tf_op jit(solution)/shard_map/ppermute | solution.py:315
  120.5 1.9 collective-permute-start.14
  123.1 1.9 select_select_fusion
  125.0 1.9 collective-permute-done.14
  127.0 1.4 fusion.8
  128.3 21.5 %shard_map.68 = (f32[46,80,128]{2,1,0:T(8,128)}, f32[7,80,128]{2,1,0:T(8,128)}, f32[7,80,128]{2,1,0:T(8,128)}) custom-call(s32[4]{0:T(128)} %fusion.6.refs_0_.offsets_ref, bf16[46,80,128]{2,1,0:T(8,128)(2,1)} %get-tuple-element.87.ext_ref, bf16[384,512]{1,0:T(8,128)(2,1)} %get-tuple-element.59.plane_ref.fplane_ref, ...), custom_call_target="tpu_custom_call" | custom-call | flops 9059696640 | bytes 11526160 | tf_op jit(solution)/shard_map/pallas_call | solution.py:295
  149.9 1.1 fusion.10
  151.0 1.9 collective-permute-start.24
  152.9 4.4 %collective-permute-start.23 = (f32[18,8,128]{2,1,0:T(8,128)S(1)}, f32[18,8,128]{2,1,0:T(8,128)S(1)}, u32[]{:S(2)}, u32[]{:S(2)}) collective-permute-start(f32[18,8,128]{2,1,0:T(8,128)S(1)} %get-tuple-element.96), channel_id=1, source_target_pairs={{0,32},{32,64},{64,96},{1,33},{33,65},{65,97},{2,34},{34,66},{66,9... | collective-permute-start | bytes 221192 | tf_op jit(solution)/shard_map/ppermute | solution.py:315
  157.3 1.9 collective-permute-start.16
  159.2 3.4 %collective-permute-start.17 = (f32[7,80,128]{2,1,0:T(8,128)}, f32[7,80,128]{2,1,0:T(8,128)S(1)}, u32[]{:S(2)}, u32[]{:S(2)}) collective-permute-start(f32[7,80,128]{2,1,0:T(8,128)} %get-tuple-element.80), channel_id=1, source_target_pairs={{1,0},{33,32},{65,64},{97,96},{2,1},{34,33},{66,65},{98,97},{3,2},... | collective-permute-start | bytes 860168 | tf_op jit(solution)/shard_map/ppermute | solution.py:315
  162.6 0.8 slice_divide_fusion
  163.6 3.1 %collective-permute-done.16 = f32[7,80,128]{2,1,0:T(8,128)S(1)} collective-permute-done((f32[7,80,128]{2,1,0:T(8,128)}, f32[7,80,128]{2,1,0:T(8,128)S(1)}, u32[]{:S(2)}, u32[]{:S(2)}) %collective-permute-start.16) | collective-permute-done | bytes 286752 | tf_op jit(solution)/shard_map/ppermute | solution.py:315
  166.7 7.1 %collective-permute-done.17 = f32[7,80,128]{2,1,0:T(8,128)S(1)} collective-permute-done((f32[7,80,128]{2,1,0:T(8,128)}, f32[7,80,128]{2,1,0:T(8,128)S(1)}, u32[]{:S(2)}, u32[]{:S(2)}) %collective-permute-start.17) | collective-permute-done | bytes 286752 | tf_op jit(solution)/shard_map/ppermute | solution.py:315
  173.9 1.9 collective-permute-start.19
  175.8 3.6 %collective-permute-start.18 = (f32[14,8,128]{2,1,0:T(8,128)S(1)}, f32[14,8,128]{2,1,0:T(8,128)S(1)}, u32[]{:S(2)}, u32[]{:S(2)}) collective-permute-start(f32[14,8,128]{2,1,0:T(8,128)S(1)} %get-tuple-element.110), channel_id=1, source_target_pairs={{0,32},{32,64},{64,96},{1,33},{33,65},{65,97},{2,34},{34,66},{66,9... | collective-permute-start | bytes 172040 | tf_op jit(solution)/shard_map/ppermute | solution.py:315
  179.5 1.2 collective-permute-done.18
  180.9 2.7 %collective-permute-start.25 = (f32[18,64,128]{2,1,0:T(8,128)S(1)}, f32[18,64,128]{2,1,0:T(8,128)S(1)}, u32[]{:S(2)}, u32[]{:S(2)}) collective-permute-start(f32[18,64,128]{2,1,0:T(8,128)S(1)} %slice_multiply_fusion.refs_0_), channel_id=1, source_target_pairs={{0,32},{32,0},{64,96},{96,64},{1,33},{33,1},{65,97},{97,65},{2,34}... | collective-permute-start | bytes 1769480 | tf_op jit(solution)/shard_map/ppermute | solution.py:319
  184.1 8.1 %collective-permute-done.21.refs_2_ = f32[14,64,128]{2,1,0:T(8,128)S(1)} collective-permute-done((f32[14,64,128]{2,1,0:T(8,128)S(1)}, f32[14,64,128]{2,1,0:T(8,128)S(1)}, u32[]{:S(2)}, u32[]{:S(2)}) %collective-permute-start.21) | collective-permute-done | bytes 458784 | tf_op jit(solution)/shard_map/ppermute | solution.py:319
  192.2 1.6 collective-permute-start.22
  193.8 1.4 shard_map.69.refs_4_
  195.3 1.3 shard_map.70
  (70 shorter events, 5.4 us)
Async XLA Ops:
  1.5 18.0 %collective-permute-start.4 = (f32[1,136]{1,0:T(1,128)S(1)}, f32[1,136]{1,0:T(1,128)S(1)}, u32[]{:S(2)}, u32[]{:S(2)}) collective-permute-start(f32[1,136]{1,0:T(1,128)S(1)} %bitcast.20), channel_id=1, source_target_pairs={{0,96},{32,64},{64,32},{96,0},{1,97},{33,65},{65,33},{97,1},{2,98}... | collective-permute-start | bytes 1640 | tf_op jit(solution)/shard_map/ppermute | solution.py:319
  3.7 15.8 %collective-permute-start.3 = (f32[1,136]{1,0:T(1,128)S(1)}, f32[1,136]{1,0:T(1,128)S(1)}, u32[]{:S(2)}, u32[]{:S(2)}) collective-permute-start(f32[1,136]{1,0:T(1,128)S(1)} %bitcast.21), channel_id=1, source_target_pairs={{0,64},{32,96},{64,0},{96,32},{1,65},{33,97},{65,1},{97,33},{2,66}... | collective-permute-start | bytes 1640 | tf_op jit(solution)/shard_map/ppermute | solution.py:319
  3.7 15.8 %collective-permute-start.2 = (f32[1,136]{1,0:T(1,128)S(1)}, f32[1,136]{1,0:T(1,128)S(1)}, u32[]{:S(2)}, u32[]{:S(2)}) collective-permute-start(f32[1,136]{1,0:T(1,128)S(1)} %bitcast.22), channel_id=1, source_target_pairs={{0,32},{32,0},{64,96},{96,64},{1,33},{33,1},{65,97},{97,65},{2,34}... | collective-permute-start | bytes 1640 | tf_op jit(solution)/shard_map/ppermute | solution.py:319
  4.9 13.3 %copy-start = (bf16[1,32,256,128]{3,2,1,0:T(8,128)(2,1)S(1)}, bf16[1,32,256,128]{3,2,1,0:T(8,128)(2,1)}, u32[]{:S(2)}) copy-start(bf16[1,32,256,128]{3,2,1,0:T(8,128)(2,1)} %param.9) | copy-start | bytes 6291460
  7.4 15.1 %collective-permute-start.1 = (bf16[8,80,128]{2,1,0:T(8,128)(2,1)}, bf16[8,80,128]{2,1,0:T(8,128)(2,1)}, u32[]{:S(2)}, u32[]{:S(2)}) collective-permute-start(bf16[8,80,128]{2,1,0:T(8,128)(2,1)} %get-tuple-element.111), channel_id=1, source_target_pairs={{1,0},{33,32},{65,64},{97,96},{2,1},{34,33},{66,65},{98,97},{3,2},... | collective-permute-start | bytes 491528 | tf_op jit(solution)/shard_map/ppermute | solution.py:315
  9.8 12.8 %collective-permute-start = (bf16[8,80,128]{2,1,0:T(8,128)(2,1)}, bf16[8,80,128]{2,1,0:T(8,128)(2,1)}, u32[]{:S(2)}, u32[]{:S(2)}) collective-permute-start(bf16[8,80,128]{2,1,0:T(8,128)(2,1)} %get-tuple-element.112), channel_id=1, source_target_pairs={{0,1},{32,33},{64,65},{96,97},{1,2},{33,34},{65,66},{97,98},{2,3},... | collective-permute-start | bytes 491528 | tf_op jit(solution)/shard_map/ppermute | solution.py:315
  19.6 26.4 %collective-permute-start.5 = (bf16[32,64,128]{2,1,0:T(8,128)(2,1)}, bf16[32,64,128]{2,1,0:T(8,128)(2,1)S(1)}, u32[]{:S(2)}, u32[]{:S(2)}) collective-permute-start(bf16[32,64,128]{2,1,0:T(8,128)(2,1)} %get-tuple-element.55), channel_id=1, source_target_pairs={{0,64},{32,96},{64,0},{96,32},{1,65},{33,97},{65,1},{97,33},{2,66}... | collective-permute-start | bytes 1572872 | tf_op jit(solution)/shard_map/ppermute | solution.py:319
  19.7 26.3 %collective-permute-start.6 = (bf16[32,64,128]{2,1,0:T(8,128)(2,1)}, bf16[32,64,128]{2,1,0:T(8,128)(2,1)S(1)}, u32[]{:S(2)}, u32[]{:S(2)}) collective-permute-start(bf16[32,64,128]{2,1,0:T(8,128)(2,1)} %get-tuple-element.56), channel_id=1, source_target_pairs={{0,96},{32,64},{64,32},{96,0},{1,97},{33,65},{65,33},{97,1},{2,98}... | collective-permute-start | bytes 1572872 | tf_op jit(solution)/shard_map/ppermute | solution.py:319
  21.9 9.5 %collective-permute-start.8 = (bf16[32,64,128]{2,1,0:T(8,128)(2,1)}, bf16[32,64,128]{2,1,0:T(8,128)(2,1)S(1)}, u32[]{:S(2)}, u32[]{:S(2)}) collective-permute-start(bf16[32,64,128]{2,1,0:T(8,128)(2,1)} %get-tuple-element.58), channel_id=1, source_target_pairs={{0,32},{32,0},{64,96},{96,64},{1,33},{33,1},{65,97},{97,65},{2,34}... | collective-permute-start | bytes 1572872 | tf_op jit(solution)/shard_map/ppermute | solution.py:319
  21.9 2.8 %copy-start.7 = (f32[4,136]{1,0:T(4,128)}, f32[4,136]{1,0:T(4,128)S(1)}, u32[]{:S(2)}) copy-start(f32[4,136]{1,0:T(4,128)S(1)} %maximum_select_fusion.small_ref) | copy-start | bytes 6532
  22.6 23.5 %collective-permute-start.7 = (bf16[32,64,128]{2,1,0:T(8,128)(2,1)}, bf16[32,64,128]{2,1,0:T(8,128)(2,1)S(1)}, u32[]{:S(2)}, u32[]{:S(2)}) collective-permute-start(bf16[32,64,128]{2,1,0:T(8,128)(2,1)} %get-tuple-element.57), channel_id=1, source_target_pairs={{1,0},{33,32},{65,64},{97,96},{2,1},{34,33},{66,65},{98,97},{3,2},... | collective-permute-start | bytes 1572872 | tf_op jit(solution)/shard_map/ppermute | solution.py:315
  31.4 21.1 %collective-permute-start.9 = (bf16[32,64,128]{2,1,0:T(8,128)(2,1)S(1)}, bf16[32,64,128]{2,1,0:T(8,128)(2,1)S(1)}, u32[]{:S(2)}, u32[]{:S(2)}) collective-permute-start(bf16[32,64,128]{2,1,0:T(8,128)(2,1)S(1)} %collective-permute-done.8), channel_id=1, source_target_pairs={{1,0},{33,32},{65,64},{97,96},{2,1},{34,33},{66,65},{98,97},{3,2},... | collective-permute-start | bytes 1572872 | tf_op jit(solution)/shard_map/ppermute | solution.py:315
  33.2 19.2 %copy-start.1 = (bf16[32,64,128]{2,1,0:T(8,128)(2,1)S(1)}, bf16[32,64,128]{2,1,0:T(8,128)(2,1)}, u32[]{:S(2)}) copy-start(bf16[32,64,128]{2,1,0:T(8,128)(2,1)} %get-tuple-element.57) | copy-start | bytes 1572868
  46.1 7.9 %copy-start.3 = (bf16[32,64,128]{2,1,0:T(8,128)(2,1)}, bf16[32,64,128]{2,1,0:T(8,128)(2,1)S(1)}, u32[]{:S(2)}) copy-start(bf16[32,64,128]{2,1,0:T(8,128)(2,1)S(1)} %collective-permute-done.7.refs_3_.refs_1_) | copy-start | bytes 1572868
  52.4 1.5 copy-start.4
  52.4 17.5 %collective-permute-start.10 = (bf16[32,64,128]{2,1,0:T(8,128)(2,1)S(1)}, bf16[32,64,128]{2,1,0:T(8,128)(2,1)S(1)}, u32[]{:S(2)}, u32[]{:S(2)}) collective-permute-start(bf16[32,64,128]{2,1,0:T(8,128)(2,1)S(1)} %collective-permute-done.5), channel_id=1, source_target_pairs={{1,0},{33,32},{65,64},{97,96},{2,1},{34,33},{66,65},{98,97},{3,2},... | collective-permute-start | bytes 1572872 | tf_op jit(solution)/shard_map/ppermute | solution.py:315
  52.4 28.7 %collective-permute-start.11 = (bf16[32,64,128]{2,1,0:T(8,128)(2,1)S(1)}, bf16[32,64,128]{2,1,0:T(8,128)(2,1)S(1)}, u32[]{:S(2)}, u32[]{:S(2)}) collective-permute-start(bf16[32,64,128]{2,1,0:T(8,128)(2,1)S(1)} %collective-permute-done.6), channel_id=1, source_target_pairs={{1,0},{33,32},{65,64},{97,96},{2,1},{34,33},{66,65},{98,97},{3,2},... | collective-permute-start | bytes 1572872 | tf_op jit(solution)/shard_map/ppermute | solution.py:315
  69.9 11.2 %copy-start.5 = (bf16[32,64,128]{2,1,0:T(8,128)(2,1)}, bf16[32,64,128]{2,1,0:T(8,128)(2,1)S(1)}, u32[]{:S(2)}) copy-start(bf16[32,64,128]{2,1,0:T(8,128)(2,1)S(1)} %collective-permute-done.10.refs_3_.refs_5_) | copy-start | bytes 1572868
  81.2 0.8 copy-start.6
  91.9 14.3 %collective-permute-start.12 = (f32[14,80,128]{2,1,0:T(8,128)}, f32[14,80,128]{2,1,0:T(8,128)S(1)}, u32[]{:S(2)}, u32[]{:S(2)}) collective-permute-start(f32[14,80,128]{2,1,0:T(8,128)} %get-tuple-element.72), channel_id=1, source_target_pairs={{0,1},{32,33},{64,65},{96,97},{1,2},{33,34},{65,66},{97,98},{2,3},... | collective-permute-start | bytes 1720328 | tf_op jit(solution)/shard_map/ppermute | solution.py:315
  93.8 19.7 %collective-permute-start.13 = (f32[14,80,128]{2,1,0:T(8,128)}, f32[14,80,128]{2,1,0:T(8,128)S(1)}, u32[]{:S(2)}, u32[]{:S(2)}) collective-permute-start(f32[14,80,128]{2,1,0:T(8,128)} %get-tuple-element.73), channel_id=1, source_target_pairs={{1,0},{33,32},{65,64},{97,96},{2,1},{34,33},{66,65},{98,97},{3,2},... | collective-permute-start | bytes 1720328 | tf_op jit(solution)/shard_map/ppermute | solution.py:315
  113.5 9.6 %copy-start.8 = (pred[46]{0:T(512)(128)(4,1)S(1)}, pred[46]{0:T(512)(128)(4,1)}, u32[]{:S(2)}) copy-start(pred[46]{0:T(512)(128)(4,1)} %constant.160) | copy-start | bytes 142
  113.5 9.6 %copy-start.9 = (pred[46]{0:T(512)(128)(4,1)S(1)}, pred[46]{0:T(512)(128)(4,1)}, u32[]{:S(2)}) copy-start(pred[46]{0:T(512)(128)(4,1)} %constant.159) | copy-start | bytes 142
  115.4 9.7 %collective-permute-start.15 = (f32[46,16,128]{2,1,0:T(8,128)S(1)}, f32[46,16,128]{2,1,0:T(8,128)S(1)}, u32[]{:S(2)}, u32[]{:S(2)}) collective-permute-start(f32[46,16,128]{2,1,0:T(8,128)S(1)} %get-tuple-element.99), channel_id=1, source_target_pairs={{32,0},{64,32},{96,64},{33,1},{65,33},{97,65},{34,2},{66,34},{98,6... | collective-permute-start | bytes 1130504 | tf_op jit(solution)/shard_map/ppermute | solution.py:315
  120.5 6.5 %collective-permute-start.14 = (f32[46,16,128]{2,1,0:T(8,128)S(1)}, f32[46,16,128]{2,1,0:T(8,128)S(1)}, u32[]{:S(2)}, u32[]{:S(2)}) collective-permute-start(f32[46,16,128]{2,1,0:T(8,128)S(1)} %get-tuple-element.100), channel_id=1, source_target_pairs={{0,32},{32,64},{64,96},{1,33},{33,65},{65,97},{2,34},{34,66},{66,9... | collective-permute-start | bytes 1130504 | tf_op jit(solution)/shard_map/ppermute | solution.py:315
  149.9 13.5 %copy-start.2 = (f32[46,80,128]{2,1,0:T(8,128)S(1)}, f32[46,80,128]{2,1,0:T(8,128)}, u32[]{:S(2)}) copy-start(f32[46,80,128]{2,1,0:T(8,128)} %get-tuple-element.78) | copy-start | bytes 5652484
  151.0 12.4 %collective-permute-start.24 = (f32[18,8,128]{2,1,0:T(8,128)S(1)}, f32[18,8,128]{2,1,0:T(8,128)S(1)}, u32[]{:S(2)}, u32[]{:S(2)}) collective-permute-start(f32[18,8,128]{2,1,0:T(8,128)S(1)} %get-tuple-element.95), channel_id=1, source_target_pairs={{32,0},{64,32},{96,64},{33,1},{65,33},{97,65},{34,2},{66,34},{98,6... | collective-permute-start | bytes 221192 | tf_op jit(solution)/shard_map/ppermute | solution.py:315
  152.9 10.5 %collective-permute-start.23 = (f32[18,8,128]{2,1,0:T(8,128)S(1)}, f32[18,8,128]{2,1,0:T(8,128)S(1)}, u32[]{:S(2)}, u32[]{:S(2)}) collective-permute-start(f32[18,8,128]{2,1,0:T(8,128)S(1)} %get-tuple-element.96), channel_id=1, source_target_pairs={{0,32},{32,64},{64,96},{1,33},{33,65},{65,97},{2,34},{34,66},{66,9... | collective-permute-start | bytes 221192 | tf_op jit(solution)/shard_map/ppermute | solution.py:315
  157.3 9.4 %collective-permute-start.16 = (f32[7,80,128]{2,1,0:T(8,128)}, f32[7,80,128]{2,1,0:T(8,128)S(1)}, u32[]{:S(2)}, u32[]{:S(2)}) collective-permute-start(f32[7,80,128]{2,1,0:T(8,128)} %get-tuple-element.79), channel_id=1, source_target_pairs={{0,1},{32,33},{64,65},{96,97},{1,2},{33,34},{65,66},{97,98},{2,3},... | collective-permute-start | bytes 860168 | tf_op jit(solution)/shard_map/ppermute | solution.py:315
  159.2 14.6 %collective-permute-start.17 = (f32[7,80,128]{2,1,0:T(8,128)}, f32[7,80,128]{2,1,0:T(8,128)S(1)}, u32[]{:S(2)}, u32[]{:S(2)}) collective-permute-start(f32[7,80,128]{2,1,0:T(8,128)} %get-tuple-element.80), channel_id=1, source_target_pairs={{1,0},{33,32},{65,64},{97,96},{2,1},{34,33},{66,65},{98,97},{3,2},... | collective-permute-start | bytes 860168 | tf_op jit(solution)/shard_map/ppermute | solution.py:315
  163.5 20.1 %collective-permute-start.26 = (f32[18,64,128]{2,1,0:T(8,128)S(1)}, f32[18,64,128]{2,1,0:T(8,128)S(1)}, u32[]{:S(2)}, u32[]{:S(2)}) collective-permute-start(f32[18,64,128]{2,1,0:T(8,128)S(1)} %slice_multiply_fusion.refs_0_), channel_id=1, source_target_pairs={{0,64},{32,96},{64,0},{96,32},{1,65},{33,97},{65,1},{97,33},{2,66}... | collective-permute-start | bytes 1769480 | tf_op jit(solution)/shard_map/ppermute | solution.py:319
  173.9 5.6 %collective-permute-start.19 = (f32[14,8,128]{2,1,0:T(8,128)S(1)}, f32[14,8,128]{2,1,0:T(8,128)S(1)}, u32[]{:S(2)}, u32[]{:S(2)}) collective-permute-start(f32[14,8,128]{2,1,0:T(8,128)S(1)} %get-tuple-element.109), channel_id=1, source_target_pairs={{32,0},{64,32},{96,64},{33,1},{65,33},{97,65},{34,2},{66,34},{98,6... | collective-permute-start | bytes 172040 | tf_op jit(solution)/shard_map/ppermute | solution.py:315
  175.8 4.9 %collective-permute-start.18 = (f32[14,8,128]{2,1,0:T(8,128)S(1)}, f32[14,8,128]{2,1,0:T(8,128)S(1)}, u32[]{:S(2)}, u32[]{:S(2)}) collective-permute-start(f32[14,8,128]{2,1,0:T(8,128)S(1)} %get-tuple-element.110), channel_id=1, source_target_pairs={{0,32},{32,64},{64,96},{1,33},{33,65},{65,97},{2,34},{34,66},{66,9... | collective-permute-start | bytes 172040 | tf_op jit(solution)/shard_map/ppermute | solution.py:315
  180.8 11.4 %collective-permute-start.21 = (f32[14,64,128]{2,1,0:T(8,128)S(1)}, f32[14,64,128]{2,1,0:T(8,128)S(1)}, u32[]{:S(2)}, u32[]{:S(2)}) collective-permute-start(f32[14,64,128]{2,1,0:T(8,128)S(1)} %fusion.4.refs_0_), channel_id=1, source_target_pairs={{0,64},{32,96},{64,0},{96,32},{1,65},{33,97},{65,1},{97,33},{2,66}... | collective-permute-start | bytes 1376264 | tf_op jit(solution)/shard_map/ppermute | solution.py:319
  180.9 12.9 %collective-permute-start.25 = (f32[18,64,128]{2,1,0:T(8,128)S(1)}, f32[18,64,128]{2,1,0:T(8,128)S(1)}, u32[]{:S(2)}, u32[]{:S(2)}) collective-permute-start(f32[18,64,128]{2,1,0:T(8,128)S(1)} %slice_multiply_fusion.refs_0_), channel_id=1, source_target_pairs={{0,32},{32,0},{64,96},{96,64},{1,33},{33,1},{65,97},{97,65},{2,34}... | collective-permute-start | bytes 1769480 | tf_op jit(solution)/shard_map/ppermute | solution.py:319
  183.6 10.2 %collective-permute-start.27 = (f32[18,64,128]{2,1,0:T(8,128)S(1)}, f32[18,64,128]{2,1,0:T(8,128)S(1)}, u32[]{:S(2)}, u32[]{:S(2)}) collective-permute-start(f32[18,64,128]{2,1,0:T(8,128)S(1)} %collective-permute-done.26.refs_2_), channel_id=1, source_target_pairs={{0,32},{32,0},{64,96},{96,64},{1,33},{33,1},{65,97},{97,65},{2,34}... | collective-permute-start | bytes 1769480 | tf_op jit(solution)/shard_map/ppermute | solution.py:319
  183.6 11.6 %collective-permute-start.20 = (f32[14,64,128]{2,1,0:T(8,128)S(1)}, f32[14,64,128]{2,1,0:T(8,128)S(1)}, u32[]{:S(2)}, u32[]{:S(2)}) collective-permute-start(f32[14,64,128]{2,1,0:T(8,128)S(1)} %fusion.4.refs_0_), channel_id=1, source_target_pairs={{0,32},{32,0},{64,96},{96,64},{1,33},{33,1},{65,97},{97,65},{2,34}... | collective-permute-start | bytes 1376264 | tf_op jit(solution)/shard_map/ppermute | solution.py:319
  192.2 3.1 %collective-permute-start.22 = (f32[14,64,128]{2,1,0:T(8,128)S(1)}, f32[14,64,128]{2,1,0:T(8,128)S(1)}, u32[]{:S(2)}, u32[]{:S(2)}) collective-permute-start(f32[14,64,128]{2,1,0:T(8,128)S(1)} %collective-permute-done.21.refs_2_), channel_id=1, source_target_pairs={{0,32},{32,0},{64,96},{96,64},{1,33},{33,1},{65,97},{97,65},{2,34}... | collective-permute-start | bytes 1376264 | tf_op jit(solution)/shard_map/ppermute | solution.py:319

commit v6 on v5

--- a/solution.py
+++ b/solution.py
@@ -109,7 +109,7 @@
 
 
 def forward_plane(ext_ref, plane_ref, mid_ref):
-    @pl.loop(0, BX // (2 * FX), unroll=2)
+    @pl.loop(0, BX // (2 * FX), unroll=4)
     def _(step):
         x0 = step * (2 * FX)
         for y0 in range(0, QY, YB):
@@ -192,10 +192,7 @@
     copy.wait()
     for view in range(VIEWS):
         out_ref = (first_ref, last_ref)[view // HALF]
-
-        @pl.loop(0, BX // ROWS)
-        def _(step):
-            x0 = step * ROWS
+        for x0 in range(0, BX, ROWS):
             blurred = forward_line(mid_ref, line_ref, view, x0)
             out_ref[view % HALF, pl.ds(x0, ROWS)] = blurred.reshape(ROWS, QY, NZ)
 
@@ -227,10 +224,7 @@
         offset = offsets_ref[view]
         for copy in copies[slot]:
             copy.wait()
-
-        @pl.loop(0, BX // ROWS)
-        def _(step):
-            x0 = step * ROWS
+        for x0 in range(0, BX, ROWS):
             blurred = blurred_ref[slot, pl.ds(x0, ROWS)].reshape(ROWS * QY, NZ)
             quotient = quotient_rows(tiles_ref, slot, offset + x0, blurred)
             adjoint_line(quotient, line_ref, back_ref, view, slot, x0)
@@ -264,10 +258,7 @@
         copy.wait()
     for view in range(VIEWS):
         offset = offsets_ref[view]
-
-        @pl.loop(0, BX // ROWS)
-        def _(step):
-            x0 = step * ROWS
+        for x0 in range(0, BX, ROWS):
             blurred = forward_line(mid_ref, fline_ref, view, x0)
             quotient = quotient_rows(tiles_ref, view, offset + x0, blurred)
             adjoint_line(quotient, aline_ref, back_ref, view, view, x0)
@@ -418,6 +409,8 @@
         prepare_kernel, [FPLANE, APLANE, FLINE, ALINE], [SMEM] * 3, [], 1, (first[None], smalls, covers)
     )
 
+    here[HALF:], beyond, estimate = lax.optimization_barrier((here[HALF:], beyond, estimate))
+    beyond = beyond + [from_next_brick(tile) for tile in here[HALF:]]
     half = ((HALF, BX, QY, NZ), F32)
     blurred = call(
         blur_kernel,
@@ -427,8 +420,6 @@
         1,
         (estimate.astype(BF16), fplane, fline),
     )
-    here[HALF:], beyond, blurred = lax.optimization_barrier((here[HALF:], beyond, blurred))
-    beyond = beyond + [from_next_brick(tile) for tile in here[HALF:]]
     here = [jnp.where(across, here[by ^ 2], here[by]) for by in range(VIEWS)]
     tiles = list(zip(here, beyond))
     tile_scratch = lambda views: ((views, 2 * BX, QY, NZ), BF16)

time: 197 us -> 191 us (0.970)
  Pallas kernels: 61.7 us -> 51.2 us
  waiting for transfers between devices: 62 us -> 66.1 us
    ppermute x12, waiting for transfers between devices: 8.1 us -> 20.5 us  [to_xor(): return lax.ppermute(value, 'view', [(i, i ^ by) for i in range(VIEWS)])]
    pallas_call x5, Pallas kernels: 59 us -> 48.5 us  [call(): pl.pallas_call(kernel, out_shape=[jax.ShapeDtypeStruct(*out) for out in o...]
    ppermute x16, waiting for transfers between devices: 53.9 us -> 45.6 us  [send(): return lax.ppermute(value, ('view', 'brick'), perm)]
  transfers between devices with their start and end apart: 28 -> 28, of which waited for: 10 -> 11; matrix products, arithmetic and copies ran while one was open for 8% -> 8% of each run, Pallas kernels for 15% -> 13%
where the time goes in v6:
time: 191 us; the launch traced here: 190 us
  waiting for transfers between devices  66.1 us (35%)
  Pallas kernels  51.2 us (27%)
  starting transfers between devices  50.4 us (26%)
  other arithmetic  15.9 us (8%)
  local copies, waits for them, and re-layouts  5.05 us (3%)
    pallas_call x5, Pallas kernels, call(): pl.pallas_call(kernel, out_shape=[jax.ShapeDtypeStruct(*out) for out in o...  48.5 us
    ppermute x16, waiting for transfers between devices, send(): return lax.ppermute(value, ('view', 'brick'), perm)  45.6 us
    ppermute x16, starting transfers between devices, send(): return lax.ppermute(value, ('view', 'brick'), perm)  40.4 us
    ppermute x12, waiting for transfers between devices, to_xor(): return lax.ppermute(value, 'view', [(i, i ^ by) for i in range(VIEWS)])  20.5 us
    ppermute x12, starting transfers between devices, to_xor(): return lax.ppermute(value, 'view', [(i, i ^ by) for i in range(VIEWS)])  9.96 us
  transfers between devices with their start and end apart: 28, of which 11 were waited for; matrix products, arithmetic and copies ran while one was open for 8% of the time, Pallas kernels for 13%

profile of v6, /device:TPU:31, one launch (start us, length us, event | category | flops | bytes accessed | tf_op | source)
XLA Modules:
  0.0 189.9 jit_solution(669439674585699848)
XLA Ops:
  1.5 2.2 %collective-permute-start.2 = (f32[1,136]{1,0:T(1,128)S(1)}, f32[1,136]{1,0:T(1,128)S(1)}, u32[]{:S(2)}, u32[]{:S(2)}) collective-permute-start(f32[1,136]{1,0:T(1,128)S(1)} %bitcast.24), channel_id=1, source_target_pairs={{0,96},{32,64},{64,32},{96,0},{1,97},{33,65},{65,33},{97,1},{2,98}... | collective-permute-start | bytes 1640 | tf_op jit(solution)/shard_map/ppermute | solution.py:310
  4.9 1.6 fusion.8
  6.7 0.8 pad_maximum_fusion.1
  7.4 2.4 %collective-permute-start.9 = (bf16[8,80,128]{2,1,0:T(8,128)(2,1)}, bf16[8,80,128]{2,1,0:T(8,128)(2,1)}, u32[]{:S(2)}, u32[]{:S(2)}) collective-permute-start(bf16[8,80,128]{2,1,0:T(8,128)(2,1)} %get-tuple-element.109), channel_id=1, source_target_pairs={{1,0},{33,32},{65,64},{97,96},{2,1},{34,33},{66,65},{98,97},{3,2},... | collective-permute-start | bytes 491528 | tf_op jit(solution)/shard_map/ppermute | solution.py:306
  9.8 8.3 %collective-permute-start.8 = (bf16[8,80,128]{2,1,0:T(8,128)(2,1)}, bf16[8,80,128]{2,1,0:T(8,128)(2,1)}, u32[]{:S(2)}, u32[]{:S(2)}) collective-permute-start(bf16[8,80,128]{2,1,0:T(8,128)(2,1)} %get-tuple-element.110), channel_id=1, source_target_pairs={{0,1},{32,33},{64,65},{96,97},{1,2},{33,34},{65,66},{97,98},{2,3},... | collective-permute-start | bytes 491528 | tf_op jit(solution)/shard_map/ppermute | solution.py:306
  18.2 1.4 dynamic-slice_bitcast_fusion
  19.7 2.2 %collective-permute-start.4 = (bf16[32,64,128]{2,1,0:T(8,128)(2,1)}, bf16[32,64,128]{2,1,0:T(8,128)(2,1)S(1)}, u32[]{:S(2)}, u32[]{:S(2)}) collective-permute-start(bf16[32,64,128]{2,1,0:T(8,128)(2,1)} %get-tuple-element.52), channel_id=1, source_target_pairs={{0,96},{32,64},{64,32},{96,0},{1,97},{33,65},{65,33},{97,1},{2,98}... | collective-permute-start | bytes 1572872 | tf_op jit(solution)/shard_map/ppermute | solution.py:310
  21.9 0.7 fusion.5.refs_0_.offsets_ref
  22.6 0.8 slice_reduce_fusion
  24.0 6.6 %shard_map.64 = (bf16[384,512]{1,0:T(8,128)(2,1)}, bf16[5,576,768]{2,1,0:T(8,128)(2,1)}, bf16[4,384,256]{2,1,0:T(8,128)(2,1)}, bf16[4,256,384]{2,1,0:T(8,128)(2,1)}) custom-call(s32[1]{0:T(128)} %bitcast.7.first_ref, f32[4,136]{1,0:T(4,128)} %copy-done.7, f32[3,4]{1,0:T(4,128)} %maximum_convert_fusion.covers_ref), custom_call_target="tpu_custom_call" | custom-call | flops 1 | bytes 1 | tf_op jit(solution)/shard_map/pallas_call | solution.py:286
  30.7 0.9 slice_convert_fusion.1
  31.6 0.9 slice_convert_fusion
  32.8 12.2 %collective-permute-done.4 = bf16[32,64,128]{2,1,0:T(8,128)(2,1)S(1)} collective-permute-done((bf16[32,64,128]{2,1,0:T(8,128)(2,1)}, bf16[32,64,128]{2,1,0:T(8,128)(2,1)S(1)}, u32[]{:S(2)}, u32[]{:S(2)}) %collective-permute-start.4) | collective-permute-done | bytes 524320 | tf_op jit(solution)/shard_map/ppermute | solution.py:310
  45.1 7.4 %collective-permute-done.7.refs_5_.refs_3_ = bf16[32,64,128]{2,1,0:T(8,128)(2,1)S(1)} collective-permute-done((bf16[32,64,128]{2,1,0:T(8,128)(2,1)S(1)}, bf16[32,64,128]{2,1,0:T(8,128)(2,1)S(1)}, u32[]{:S(2)}, u32[]{:S(2)}) %collective-permute-start.7) | collective-permute-done | bytes 524320 | tf_op jit(solution)/shard_map/ppermute | solution.py:306
  52.5 1.1 convert_element_type.75.ext_ref
  53.6 8.6 %shard_map.65 = (f32[2,32,64,128]{3,2,1,0:T(8,128)}, f32[2,32,64,128]{3,2,1,0:T(8,128)}) custom-call(bf16[46,80,128]{2,1,0:T(8,128)(2,1)} %convert_element_type.75.ext_ref, bf16[384,512]{1,0:T(8,128)(2,1)} %get-tuple-element.59.plane_ref.fplane_ref, bf16[4,384,256]{2,1,0:T(8,128)(2,1)} %get-tuple-element.60.line_hbm.fline_hbm), custom_call_target="tpu_custom_call" | custom-call | flops 1 | bytes 1 | tf_op jit(solution)/shard_map/pallas_call | solution.py:286
  62.2 1.4 broadcast_select_fusion
  63.6 8.7 %shard_map.66.refs_8_ = f32[46,80,128]{2,1,0:T(8,128)} custom-call(s32[4]{0:T(128)} %fusion.5.refs_0_.offsets_ref, f32[2,32,64,128]{3,2,1,0:T(8,128)} %get-tuple-element.66.refs_1_, bf16[32,64,128]{2,1,0:T(8,128)(2,1)} %get-tuple-element.119.refs_2_.refs_0_, bf16[32,64,128]{2,1,0:T(8,128)(2,1)} %copy-done.3, ...), custom_call_target="tpu_custom_call" | custom-call | flops 2264924160 | bytes 9404432 | tf_op jit(solution)/shard_map/pallas_call | solution.py:286
  72.4 8.8 %collective-permute-done.11.refs_5_.refs_7_ = bf16[32,64,128]{2,1,0:T(8,128)(2,1)S(1)} collective-permute-done((bf16[32,64,128]{2,1,0:T(8,128)(2,1)S(1)}, bf16[32,64,128]{2,1,0:T(8,128)(2,1)S(1)}, u32[]{:S(2)}, u32[]{:S(2)}) %collective-permute-start.11) | collective-permute-done | bytes 524320 | tf_op jit(solution)/shard_map/ppermute | solution.py:306
  81.2 0.8 copy-done.6
  82.0 9.5 %shard_map.67 = (f32[46,80,128]{2,1,0:T(8,128)}, f32[14,80,128]{2,1,0:T(8,128)}, f32[14,80,128]{2,1,0:T(8,128)}) custom-call(s32[4]{0:T(128)} %fusion.5.refs_0_.offsets_ref, f32[2,32,64,128]{3,2,1,0:T(8,128)} %get-tuple-element.61.refs_1_, bf16[32,64,128]{2,1,0:T(8,128)(2,1)} %get-tuple-element.118.refs_2_.refs_4_, bf16[32,64,128]{2,1,0:T(8,128)(2,1)} %copy-done.5, ...), custom_call_target="tpu_custom_call" | custom-call | flops 2264924160 | bytes 11288592 | tf_op jit(solution)/shard_map/pallas_call | solution.py:286
  91.5 1.9 %collective-permute-start.12 = (f32[14,80,128]{2,1,0:T(8,128)}, f32[14,80,128]{2,1,0:T(8,128)S(1)}, u32[]{:S(2)}, u32[]{:S(2)}) collective-permute-start(f32[14,80,128]{2,1,0:T(8,128)} %get-tuple-element.70), channel_id=1, source_target_pairs={{0,1},{32,33},{64,65},{96,97},{1,2},{33,34},{65,66},{97,98},{2,3},... | collective-permute-start | bytes 1720328 | tf_op jit(solution)/shard_map/ppermute | solution.py:306
  93.4 3.4 %collective-permute-start.13 = (f32[14,80,128]{2,1,0:T(8,128)}, f32[14,80,128]{2,1,0:T(8,128)S(1)}, u32[]{:S(2)}, u32[]{:S(2)}) collective-permute-start(f32[14,80,128]{2,1,0:T(8,128)} %get-tuple-element.71), channel_id=1, source_target_pairs={{1,0},{33,32},{65,64},{97,96},{2,1},{34,33},{66,65},{98,97},{3,2},... | collective-permute-start | bytes 1720328 | tf_op jit(solution)/shard_map/ppermute | solution.py:306
  96.9 8.9 %collective-permute-done.12 = f32[14,80,128]{2,1,0:T(8,128)S(1)} collective-permute-done((f32[14,80,128]{2,1,0:T(8,128)}, f32[14,80,128]{2,1,0:T(8,128)S(1)}, u32[]{:S(2)}, u32[]{:S(2)}) %collective-permute-start.12) | collective-permute-done | bytes 573472 | tf_op jit(solution)/shard_map/ppermute | solution.py:306
  105.8 7.4 %collective-permute-done.13 = f32[14,80,128]{2,1,0:T(8,128)S(1)} collective-permute-done((f32[14,80,128]{2,1,0:T(8,128)}, f32[14,80,128]{2,1,0:T(8,128)S(1)}, u32[]{:S(2)}, u32[]{:S(2)}) %collective-permute-start.13) | collective-permute-done | bytes 573472 | tf_op jit(solution)/shard_map/ppermute | solution.py:306
  113.1 1.8 pad_add_fusion
  115.0 5.1 %collective-permute-start.15 = (f32[46,16,128]{2,1,0:T(8,128)S(1)}, f32[46,16,128]{2,1,0:T(8,128)S(1)}, u32[]{:S(2)}, u32[]{:S(2)}) collective-permute-start(f32[46,16,128]{2,1,0:T(8,128)S(1)} %get-tuple-element.97), channel_id=1, source_target_pairs={{32,0},{64,32},{96,64},{33,1},{65,33},{97,65},{34,2},{66,34},{98,6... | collective-permute-start | bytes 1130504 | tf_op jit(solution)/shard_map/ppermute | solution.py:306
  120.1 2.1 %collective-permute-start.14 = (f32[46,16,128]{2,1,0:T(8,128)S(1)}, f32[46,16,128]{2,1,0:T(8,128)S(1)}, u32[]{:S(2)}, u32[]{:S(2)}) collective-permute-start(f32[46,16,128]{2,1,0:T(8,128)S(1)} %get-tuple-element.98), channel_id=1, source_target_pairs={{0,32},{32,64},{64,96},{1,33},{33,65},{65,97},{2,34},{34,66},{66,9... | collective-permute-start | bytes 1130504 | tf_op jit(solution)/shard_map/ppermute | solution.py:306
  122.9 1.9 %select_select_fusion = f32[46]{0:T(128)S(1)} fusion(pred[46]{0:T(512)(128)(4,1)S(1)} %copy-done.9, pred[46]{0:T(512)(128)(4,1)S(1)} %copy-done.8, f32[]{:T(128)} %bitcast.11, f32[]{:T(128)} %bitcast.9, f32[]{:T(128)} %bitcast.10), kind=kLoop, calls=%fused_computation.38 | loop fusion | flops 92 | bytes 288 | tf_op jit(solution)/shard_map/jit(_take)/gather | solution.py:406
  124.9 1.7 collective-permute-done.14
  126.6 1.3 fusion.7
  127.9 15.1 %shard_map.68 = (f32[46,80,128]{2,1,0:T(8,128)}, f32[7,80,128]{2,1,0:T(8,128)}, f32[7,80,128]{2,1,0:T(8,128)}) custom-call(s32[4]{0:T(128)} %fusion.5.refs_0_.offsets_ref, bf16[46,80,128]{2,1,0:T(8,128)(2,1)} %get-tuple-element.85.ext_ref, bf16[384,512]{1,0:T(8,128)(2,1)} %get-tuple-element.59.plane_ref.fplane_ref, ...), custom_call_target="tpu_custom_call" | custom-call | flops 9059696640 | bytes 11526160 | tf_op jit(solution)/shard_map/pallas_call | solution.py:286
  143.0 1.1 fusion.9
  144.1 1.9 %collective-permute-start.24 = (f32[18,8,128]{2,1,0:T(8,128)S(1)}, f32[18,8,128]{2,1,0:T(8,128)S(1)}, u32[]{:S(2)}, u32[]{:S(2)}) collective-permute-start(f32[18,8,128]{2,1,0:T(8,128)S(1)} %get-tuple-element.93), channel_id=1, source_target_pairs={{32,0},{64,32},{96,64},{33,1},{65,33},{97,65},{34,2},{66,34},{98,6... | collective-permute-start | bytes 221192 | tf_op jit(solution)/shard_map/ppermute | solution.py:306
  146.0 4.4 %collective-permute-start.23 = (f32[18,8,128]{2,1,0:T(8,128)S(1)}, f32[18,8,128]{2,1,0:T(8,128)S(1)}, u32[]{:S(2)}, u32[]{:S(2)}) collective-permute-start(f32[18,8,128]{2,1,0:T(8,128)S(1)} %get-tuple-element.94), channel_id=1, source_target_pairs={{0,32},{32,64},{64,96},{1,33},{33,65},{65,97},{2,34},{34,66},{66,9... | collective-permute-start | bytes 221192 | tf_op jit(solution)/shard_map/ppermute | solution.py:306
  150.4 1.9 %collective-permute-start.16 = (f32[7,80,128]{2,1,0:T(8,128)}, f32[7,80,128]{2,1,0:T(8,128)S(1)}, u32[]{:S(2)}, u32[]{:S(2)}) collective-permute-start(f32[7,80,128]{2,1,0:T(8,128)} %get-tuple-element.77), channel_id=1, source_target_pairs={{0,1},{32,33},{64,65},{96,97},{1,2},{33,34},{65,66},{97,98},{2,3},... | collective-permute-start | bytes 860168 | tf_op jit(solution)/shard_map/ppermute | solution.py:306
  152.4 3.4 %collective-permute-start.17 = (f32[7,80,128]{2,1,0:T(8,128)}, f32[7,80,128]{2,1,0:T(8,128)S(1)}, u32[]{:S(2)}, u32[]{:S(2)}) collective-permute-start(f32[7,80,128]{2,1,0:T(8,128)} %get-tuple-element.78), channel_id=1, source_target_pairs={{1,0},{33,32},{65,64},{97,96},{2,1},{34,33},{66,65},{98,97},{3,2},... | collective-permute-start | bytes 860168 | tf_op jit(solution)/shard_map/ppermute | solution.py:306
  155.7 0.7 slice_divide_fusion
  156.7 3.2 %collective-permute-done.16 = f32[7,80,128]{2,1,0:T(8,128)S(1)} collective-permute-done((f32[7,80,128]{2,1,0:T(8,128)}, f32[7,80,128]{2,1,0:T(8,128)S(1)}, u32[]{:S(2)}, u32[]{:S(2)}) %collective-permute-start.16) | collective-permute-done | bytes 286752 | tf_op jit(solution)/shard_map/ppermute | solution.py:306
  159.9 7.1 %collective-permute-done.17 = f32[7,80,128]{2,1,0:T(8,128)S(1)} collective-permute-done((f32[7,80,128]{2,1,0:T(8,128)}, f32[7,80,128]{2,1,0:T(8,128)S(1)}, u32[]{:S(2)}, u32[]{:S(2)}) %collective-permute-start.17) | collective-permute-done | bytes 286752 | tf_op jit(solution)/shard_map/ppermute | solution.py:306
  167.0 1.9 %collective-permute-start.19 = (f32[14,8,128]{2,1,0:T(8,128)S(1)}, f32[14,8,128]{2,1,0:T(8,128)S(1)}, u32[]{:S(2)}, u32[]{:S(2)}) collective-permute-start(f32[14,8,128]{2,1,0:T(8,128)S(1)} %get-tuple-element.107), channel_id=1, source_target_pairs={{32,0},{64,32},{96,64},{33,1},{65,33},{97,65},{34,2},{66,34},{98,6... | collective-permute-start | bytes 172040 | tf_op jit(solution)/shard_map/ppermute | solution.py:306
  169.0 3.6 %collective-permute-start.18 = (f32[14,8,128]{2,1,0:T(8,128)S(1)}, f32[14,8,128]{2,1,0:T(8,128)S(1)}, u32[]{:S(2)}, u32[]{:S(2)}) collective-permute-start(f32[14,8,128]{2,1,0:T(8,128)S(1)} %get-tuple-element.108), channel_id=1, source_target_pairs={{0,32},{32,64},{64,96},{1,33},{33,65},{65,97},{2,34},{34,66},{66,9... | collective-permute-start | bytes 172040 | tf_op jit(solution)/shard_map/ppermute | solution.py:306
  172.7 1.2 collective-permute-done.18
  174.0 2.7 %collective-permute-start.25 = (f32[18,64,128]{2,1,0:T(8,128)S(1)}, f32[18,64,128]{2,1,0:T(8,128)S(1)}, u32[]{:S(2)}, u32[]{:S(2)}) collective-permute-start(f32[18,64,128]{2,1,0:T(8,128)S(1)} %slice_multiply_fusion.refs_0_), channel_id=1, source_target_pairs={{0,32},{32,0},{64,96},{96,64},{1,33},{33,1},{65,97},{97,65},{2,34}... | collective-permute-start | bytes 1769480 | tf_op jit(solution)/shard_map/ppermute | solution.py:310
  177.3 8.1 %collective-permute-done.21.refs_2_ = f32[14,64,128]{2,1,0:T(8,128)S(1)} collective-permute-done((f32[14,64,128]{2,1,0:T(8,128)S(1)}, f32[14,64,128]{2,1,0:T(8,128)S(1)}, u32[]{:S(2)}, u32[]{:S(2)}) %collective-permute-start.21) | collective-permute-done | bytes 458784 | tf_op jit(solution)/shard_map/ppermute | solution.py:310
  185.3 1.6 collective-permute-start.22
  186.9 1.4 shard_map.69.refs_4_
  188.4 1.3 shard_map.70
  (70 shorter events, 5.0 us)
Async XLA Ops:
  1.5 18.0 %collective-permute-start.2 = (f32[1,136]{1,0:T(1,128)S(1)}, f32[1,136]{1,0:T(1,128)S(1)}, u32[]{:S(2)}, u32[]{:S(2)}) collective-permute-start(f32[1,136]{1,0:T(1,128)S(1)} %bitcast.24), channel_id=1, source_target_pairs={{0,96},{32,64},{64,32},{96,0},{1,97},{33,65},{65,33},{97,1},{2,98}... | collective-permute-start | bytes 1640 | tf_op jit(solution)/shard_map/ppermute | solution.py:310
  3.7 15.8 %collective-permute-start.1 = (f32[1,136]{1,0:T(1,128)S(1)}, f32[1,136]{1,0:T(1,128)S(1)}, u32[]{:S(2)}, u32[]{:S(2)}) collective-permute-start(f32[1,136]{1,0:T(1,128)S(1)} %bitcast.25), channel_id=1, source_target_pairs={{0,64},{32,96},{64,0},{96,32},{1,65},{33,97},{65,1},{97,33},{2,66}... | collective-permute-start | bytes 1640 | tf_op jit(solution)/shard_map/ppermute | solution.py:310
  3.7 15.8 %collective-permute-start = (f32[1,136]{1,0:T(1,128)S(1)}, f32[1,136]{1,0:T(1,128)S(1)}, u32[]{:S(2)}, u32[]{:S(2)}) collective-permute-start(f32[1,136]{1,0:T(1,128)S(1)} %bitcast.26), channel_id=1, source_target_pairs={{0,32},{32,0},{64,96},{96,64},{1,33},{33,1},{65,97},{97,65},{2,34}... | collective-permute-start | bytes 1640 | tf_op jit(solution)/shard_map/ppermute | solution.py:310
  4.9 13.3 %copy-start = (bf16[1,32,256,128]{3,2,1,0:T(8,128)(2,1)S(1)}, bf16[1,32,256,128]{3,2,1,0:T(8,128)(2,1)}, u32[]{:S(2)}) copy-start(bf16[1,32,256,128]{3,2,1,0:T(8,128)(2,1)} %param.9) | copy-start | bytes 6291460
  7.4 15.2 %collective-permute-start.9 = (bf16[8,80,128]{2,1,0:T(8,128)(2,1)}, bf16[8,80,128]{2,1,0:T(8,128)(2,1)}, u32[]{:S(2)}, u32[]{:S(2)}) collective-permute-start(bf16[8,80,128]{2,1,0:T(8,128)(2,1)} %get-tuple-element.109), channel_id=1, source_target_pairs={{1,0},{33,32},{65,64},{97,96},{2,1},{34,33},{66,65},{98,97},{3,2},... | collective-permute-start | bytes 491528 | tf_op jit(solution)/shard_map/ppermute | solution.py:306
  9.8 12.8 %collective-permute-start.8 = (bf16[8,80,128]{2,1,0:T(8,128)(2,1)}, bf16[8,80,128]{2,1,0:T(8,128)(2,1)}, u32[]{:S(2)}, u32[]{:S(2)}) collective-permute-start(bf16[8,80,128]{2,1,0:T(8,128)(2,1)} %get-tuple-element.110), channel_id=1, source_target_pairs={{0,1},{32,33},{64,65},{96,97},{1,2},{33,34},{65,66},{97,98},{2,3},... | collective-permute-start | bytes 491528 | tf_op jit(solution)/shard_map/ppermute | solution.py:306
  19.6 13.2 %collective-permute-start.3 = (bf16[32,64,128]{2,1,0:T(8,128)(2,1)}, bf16[32,64,128]{2,1,0:T(8,128)(2,1)S(1)}, u32[]{:S(2)}, u32[]{:S(2)}) collective-permute-start(bf16[32,64,128]{2,1,0:T(8,128)(2,1)} %get-tuple-element.51), channel_id=1, source_target_pairs={{0,64},{32,96},{64,0},{96,32},{1,65},{33,97},{65,1},{97,33},{2,66}... | collective-permute-start | bytes 1572872 | tf_op jit(solution)/shard_map/ppermute | solution.py:310
  19.7 25.4 %collective-permute-start.4 = (bf16[32,64,128]{2,1,0:T(8,128)(2,1)}, bf16[32,64,128]{2,1,0:T(8,128)(2,1)S(1)}, u32[]{:S(2)}, u32[]{:S(2)}) collective-permute-start(bf16[32,64,128]{2,1,0:T(8,128)(2,1)} %get-tuple-element.52), channel_id=1, source_target_pairs={{0,96},{32,64},{64,32},{96,0},{1,97},{33,65},{65,33},{97,1},{2,98}... | collective-permute-start | bytes 1572872 | tf_op jit(solution)/shard_map/ppermute | solution.py:310
  21.8 8.8 %collective-permute-start.6 = (bf16[32,64,128]{2,1,0:T(8,128)(2,1)}, bf16[32,64,128]{2,1,0:T(8,128)(2,1)S(1)}, u32[]{:S(2)}, u32[]{:S(2)}) collective-permute-start(bf16[32,64,128]{2,1,0:T(8,128)(2,1)} %get-tuple-element.54), channel_id=1, source_target_pairs={{0,32},{32,0},{64,96},{96,64},{1,33},{33,1},{65,97},{97,65},{2,34}... | collective-permute-start | bytes 1572872 | tf_op jit(solution)/shard_map/ppermute | solution.py:310
  21.9 2.2 %copy-start.7 = (f32[4,136]{1,0:T(4,128)}, f32[4,136]{1,0:T(4,128)S(1)}, u32[]{:S(2)}) copy-start(f32[4,136]{1,0:T(4,128)S(1)} %maximum_select_fusion.small_ref) | copy-start | bytes 6532
  22.6 22.5 %collective-permute-start.5 = (bf16[32,64,128]{2,1,0:T(8,128)(2,1)}, bf16[32,64,128]{2,1,0:T(8,128)(2,1)S(1)}, u32[]{:S(2)}, u32[]{:S(2)}) collective-permute-start(bf16[32,64,128]{2,1,0:T(8,128)(2,1)} %get-tuple-element.53), channel_id=1, source_target_pairs={{1,0},{33,32},{65,64},{97,96},{2,1},{34,33},{66,65},{98,97},{3,2},... | collective-permute-start | bytes 1572872 | tf_op jit(solution)/shard_map/ppermute | solution.py:306
  30.7 21.8 %collective-permute-start.7 = (bf16[32,64,128]{2,1,0:T(8,128)(2,1)S(1)}, bf16[32,64,128]{2,1,0:T(8,128)(2,1)S(1)}, u32[]{:S(2)}, u32[]{:S(2)}) collective-permute-start(bf16[32,64,128]{2,1,0:T(8,128)(2,1)S(1)} %collective-permute-done.6), channel_id=1, source_target_pairs={{1,0},{33,32},{65,64},{97,96},{2,1},{34,33},{66,65},{98,97},{3,2},... | collective-permute-start | bytes 1572872 | tf_op jit(solution)/shard_map/ppermute | solution.py:306
  32.7 29.5 %copy-start.1 = (bf16[32,64,128]{2,1,0:T(8,128)(2,1)S(1)}, bf16[32,64,128]{2,1,0:T(8,128)(2,1)}, u32[]{:S(2)}) copy-start(bf16[32,64,128]{2,1,0:T(8,128)(2,1)} %get-tuple-element.53) | copy-start | bytes 1572868
  45.1 17.1 %copy-start.3 = (bf16[32,64,128]{2,1,0:T(8,128)(2,1)}, bf16[32,64,128]{2,1,0:T(8,128)(2,1)S(1)}, u32[]{:S(2)}) copy-start(bf16[32,64,128]{2,1,0:T(8,128)(2,1)S(1)} %collective-permute-done.5.refs_3_.refs_1_) | copy-start | bytes 1572868
  52.4 9.7 %copy-start.4 = (bf16[32,64,128]{2,1,0:T(8,128)(2,1)}, bf16[32,64,128]{2,1,0:T(8,128)(2,1)S(1)}, u32[]{:S(2)}) copy-start(bf16[32,64,128]{2,1,0:T(8,128)(2,1)S(1)} %collective-permute-done.7.refs_5_.refs_3_) | copy-start | bytes 1572868
  52.4 19.9 %collective-permute-start.10 = (bf16[32,64,128]{2,1,0:T(8,128)(2,1)S(1)}, bf16[32,64,128]{2,1,0:T(8,128)(2,1)S(1)}, u32[]{:S(2)}, u32[]{:S(2)}) collective-permute-start(bf16[32,64,128]{2,1,0:T(8,128)(2,1)S(1)} %collective-permute-done.3), channel_id=1, source_target_pairs={{1,0},{33,32},{65,64},{97,96},{2,1},{34,33},{66,65},{98,97},{3,2},... | collective-permute-start | bytes 1572872 | tf_op jit(solution)/shard_map/ppermute | solution.py:306
  52.5 28.7 %collective-permute-start.11 = (bf16[32,64,128]{2,1,0:T(8,128)(2,1)S(1)}, bf16[32,64,128]{2,1,0:T(8,128)(2,1)S(1)}, u32[]{:S(2)}, u32[]{:S(2)}) collective-permute-start(bf16[32,64,128]{2,1,0:T(8,128)(2,1)S(1)} %collective-permute-done.4), channel_id=1, source_target_pairs={{1,0},{33,32},{65,64},{97,96},{2,1},{34,33},{66,65},{98,97},{3,2},... | collective-permute-start | bytes 1572872 | tf_op jit(solution)/shard_map/ppermute | solution.py:306
  72.3 8.8 %copy-start.5 = (bf16[32,64,128]{2,1,0:T(8,128)(2,1)}, bf16[32,64,128]{2,1,0:T(8,128)(2,1)S(1)}, u32[]{:S(2)}) copy-start(bf16[32,64,128]{2,1,0:T(8,128)(2,1)S(1)} %collective-permute-done.10.refs_3_.refs_5_) | copy-start | bytes 1572868
  81.2 0.8 copy-start.6
  91.5 14.3 %collective-permute-start.12 = (f32[14,80,128]{2,1,0:T(8,128)}, f32[14,80,128]{2,1,0:T(8,128)S(1)}, u32[]{:S(2)}, u32[]{:S(2)}) collective-permute-start(f32[14,80,128]{2,1,0:T(8,128)} %get-tuple-element.70), channel_id=1, source_target_pairs={{0,1},{32,33},{64,65},{96,97},{1,2},{33,34},{65,66},{97,98},{2,3},... | collective-permute-start | bytes 1720328 | tf_op jit(solution)/shard_map/ppermute | solution.py:306
  93.4 19.7 %collective-permute-start.13 = (f32[14,80,128]{2,1,0:T(8,128)}, f32[14,80,128]{2,1,0:T(8,128)S(1)}, u32[]{:S(2)}, u32[]{:S(2)}) collective-permute-start(f32[14,80,128]{2,1,0:T(8,128)} %get-tuple-element.71), channel_id=1, source_target_pairs={{1,0},{33,32},{65,64},{97,96},{2,1},{34,33},{66,65},{98,97},{3,2},... | collective-permute-start | bytes 1720328 | tf_op jit(solution)/shard_map/ppermute | solution.py:306
  113.1 9.8 %copy-start.8 = (pred[46]{0:T(512)(128)(4,1)S(1)}, pred[46]{0:T(512)(128)(4,1)}, u32[]{:S(2)}) copy-start(pred[46]{0:T(512)(128)(4,1)} %constant.160) | copy-start | bytes 142
  113.1 9.8 %copy-start.9 = (pred[46]{0:T(512)(128)(4,1)S(1)}, pred[46]{0:T(512)(128)(4,1)}, u32[]{:S(2)}) copy-start(pred[46]{0:T(512)(128)(4,1)} %constant.159) | copy-start | bytes 142
  115.0 9.9 %collective-permute-start.15 = (f32[46,16,128]{2,1,0:T(8,128)S(1)}, f32[46,16,128]{2,1,0:T(8,128)S(1)}, u32[]{:S(2)}, u32[]{:S(2)}) collective-permute-start(f32[46,16,128]{2,1,0:T(8,128)S(1)} %get-tuple-element.97), channel_id=1, source_target_pairs={{32,0},{64,32},{96,64},{33,1},{65,33},{97,65},{34,2},{66,34},{98,6... | collective-permute-start | bytes 1130504 | tf_op jit(solution)/shard_map/ppermute | solution.py:306
  120.1 6.5 %collective-permute-start.14 = (f32[46,16,128]{2,1,0:T(8,128)S(1)}, f32[46,16,128]{2,1,0:T(8,128)S(1)}, u32[]{:S(2)}, u32[]{:S(2)}) collective-permute-start(f32[46,16,128]{2,1,0:T(8,128)S(1)} %get-tuple-element.98), channel_id=1, source_target_pairs={{0,32},{32,64},{64,96},{1,33},{33,65},{65,97},{2,34},{34,66},{66,9... | collective-permute-start | bytes 1130504 | tf_op jit(solution)/shard_map/ppermute | solution.py:306
  143.0 13.5 %copy-start.2 = (f32[46,80,128]{2,1,0:T(8,128)S(1)}, f32[46,80,128]{2,1,0:T(8,128)}, u32[]{:S(2)}) copy-start(f32[46,80,128]{2,1,0:T(8,128)} %get-tuple-element.76) | copy-start | bytes 5652484
  144.1 12.4 %collective-permute-start.24 = (f32[18,8,128]{2,1,0:T(8,128)S(1)}, f32[18,8,128]{2,1,0:T(8,128)S(1)}, u32[]{:S(2)}, u32[]{:S(2)}) collective-permute-start(f32[18,8,128]{2,1,0:T(8,128)S(1)} %get-tuple-element.93), channel_id=1, source_target_pairs={{32,0},{64,32},{96,64},{33,1},{65,33},{97,65},{34,2},{66,34},{98,6... | collective-permute-start | bytes 221192 | tf_op jit(solution)/shard_map/ppermute | solution.py:306
  146.0 10.5 %collective-permute-start.23 = (f32[18,8,128]{2,1,0:T(8,128)S(1)}, f32[18,8,128]{2,1,0:T(8,128)S(1)}, u32[]{:S(2)}, u32[]{:S(2)}) collective-permute-start(f32[18,8,128]{2,1,0:T(8,128)S(1)} %get-tuple-element.94), channel_id=1, source_target_pairs={{0,32},{32,64},{64,96},{1,33},{33,65},{65,97},{2,34},{34,66},{66,9... | collective-permute-start | bytes 221192 | tf_op jit(solution)/shard_map/ppermute | solution.py:306
  150.4 9.4 %collective-permute-start.16 = (f32[7,80,128]{2,1,0:T(8,128)}, f32[7,80,128]{2,1,0:T(8,128)S(1)}, u32[]{:S(2)}, u32[]{:S(2)}) collective-permute-start(f32[7,80,128]{2,1,0:T(8,128)} %get-tuple-element.77), channel_id=1, source_target_pairs={{0,1},{32,33},{64,65},{96,97},{1,2},{33,34},{65,66},{97,98},{2,3},... | collective-permute-start | bytes 860168 | tf_op jit(solution)/shard_map/ppermute | solution.py:306
  152.4 14.6 %collective-permute-start.17 = (f32[7,80,128]{2,1,0:T(8,128)}, f32[7,80,128]{2,1,0:T(8,128)S(1)}, u32[]{:S(2)}, u32[]{:S(2)}) collective-permute-start(f32[7,80,128]{2,1,0:T(8,128)} %get-tuple-element.78), channel_id=1, source_target_pairs={{1,0},{33,32},{65,64},{97,96},{2,1},{34,33},{66,65},{98,97},{3,2},... | collective-permute-start | bytes 860168 | tf_op jit(solution)/shard_map/ppermute | solution.py:306
  156.6 20.2 %collective-permute-start.26 = (f32[18,64,128]{2,1,0:T(8,128)S(1)}, f32[18,64,128]{2,1,0:T(8,128)S(1)}, u32[]{:S(2)}, u32[]{:S(2)}) collective-permute-start(f32[18,64,128]{2,1,0:T(8,128)S(1)} %slice_multiply_fusion.refs_0_), channel_id=1, source_target_pairs={{0,64},{32,96},{64,0},{96,32},{1,65},{33,97},{65,1},{97,33},{2,66}... | collective-permute-start | bytes 1769480 | tf_op jit(solution)/shard_map/ppermute | solution.py:310
  167.0 5.6 %collective-permute-start.19 = (f32[14,8,128]{2,1,0:T(8,128)S(1)}, f32[14,8,128]{2,1,0:T(8,128)S(1)}, u32[]{:S(2)}, u32[]{:S(2)}) collective-permute-start(f32[14,8,128]{2,1,0:T(8,128)S(1)} %get-tuple-element.107), channel_id=1, source_target_pairs={{32,0},{64,32},{96,64},{33,1},{65,33},{97,65},{34,2},{66,34},{98,6... | collective-permute-start | bytes 172040 | tf_op jit(solution)/shard_map/ppermute | solution.py:306
  169.0 4.9 %collective-permute-start.18 = (f32[14,8,128]{2,1,0:T(8,128)S(1)}, f32[14,8,128]{2,1,0:T(8,128)S(1)}, u32[]{:S(2)}, u32[]{:S(2)}) collective-permute-start(f32[14,8,128]{2,1,0:T(8,128)S(1)} %get-tuple-element.108), channel_id=1, source_target_pairs={{0,32},{32,64},{64,96},{1,33},{33,65},{65,97},{2,34},{34,66},{66,9... | collective-permute-start | bytes 172040 | tf_op jit(solution)/shard_map/ppermute | solution.py:306
  173.9 11.4 %collective-permute-start.21 = (f32[14,64,128]{2,1,0:T(8,128)S(1)}, f32[14,64,128]{2,1,0:T(8,128)S(1)}, u32[]{:S(2)}, u32[]{:S(2)}) collective-permute-start(f32[14,64,128]{2,1,0:T(8,128)S(1)} %fusion.3.refs_0_), channel_id=1, source_target_pairs={{0,64},{32,96},{64,0},{96,32},{1,65},{33,97},{65,1},{97,33},{2,66}... | collective-permute-start | bytes 1376264 | tf_op jit(solution)/shard_map/ppermute | solution.py:310
  174.0 12.9 %collective-permute-start.25 = (f32[18,64,128]{2,1,0:T(8,128)S(1)}, f32[18,64,128]{2,1,0:T(8,128)S(1)}, u32[]{:S(2)}, u32[]{:S(2)}) collective-permute-start(f32[18,64,128]{2,1,0:T(8,128)S(1)} %slice_multiply_fusion.refs_0_), channel_id=1, source_target_pairs={{0,32},{32,0},{64,96},{96,64},{1,33},{33,1},{65,97},{97,65},{2,34}... | collective-permute-start | bytes 1769480 | tf_op jit(solution)/shard_map/ppermute | solution.py:310
  176.8 10.2 %collective-permute-start.27 = (f32[18,64,128]{2,1,0:T(8,128)S(1)}, f32[18,64,128]{2,1,0:T(8,128)S(1)}, u32[]{:S(2)}, u32[]{:S(2)}) collective-permute-start(f32[18,64,128]{2,1,0:T(8,128)S(1)} %collective-permute-done.26.refs_2_), channel_id=1, source_target_pairs={{0,32},{32,0},{64,96},{96,64},{1,33},{33,1},{65,97},{97,65},{2,34}... | collective-permute-start | bytes 1769480 | tf_op jit(solution)/shard_map/ppermute | solution.py:310
  176.8 11.6 %collective-permute-start.20 = (f32[14,64,128]{2,1,0:T(8,128)S(1)}, f32[14,64,128]{2,1,0:T(8,128)S(1)}, u32[]{:S(2)}, u32[]{:S(2)}) collective-permute-start(f32[14,64,128]{2,1,0:T(8,128)S(1)} %fusion.3.refs_0_), channel_id=1, source_target_pairs={{0,32},{32,0},{64,96},{96,64},{1,33},{33,1},{65,97},{97,65},{2,34}... | collective-permute-start | bytes 1376264 | tf_op jit(solution)/shard_map/ppermute | solution.py:310
  185.3 3.1 %collective-permute-start.22 = (f32[14,64,128]{2,1,0:T(8,128)S(1)}, f32[14,64,128]{2,1,0:T(8,128)S(1)}, u32[]{:S(2)}, u32[]{:S(2)}) collective-permute-start(f32[14,64,128]{2,1,0:T(8,128)S(1)} %collective-permute-done.21.refs_2_), channel_id=1, source_target_pairs={{0,32},{32,0},{64,96},{96,64},{1,33},{33,1},{65,97},{97,65},{2,34}... | collective-permute-start | bytes 1376264 | tf_op jit(solution)/shard_map/ppermute | solution.py:310
